TPU v7x, 256 devices: a whole 4x4x8 slice. The times are simulated.
256 devices in a mesh: tm: 16 (over x_hi, y, core), space: 16 (over x_lo, z).
Axes of the slice: x: 4 (x_hi: 2, x_lo: 2; x = x_hi * 2 + x_lo), y: 4, z: 8, core: 2. Of those that a mesh axis runs over, the one named last changes fastest.
Arguments:
- frames_in: bfloat16 [32, 32, 128, 256], P('tm', 'space'), may hold values from -6 to 6
- weight: bfloat16 [3, 3, 3, 256, 256], replicated, may hold values from -0.078125 to 0.078125
- cotangent: bfloat16 [32, 32, 128, 256], P('tm', 'space'), may hold values from -6 to 6
Outputs:
- output: bfloat16 [32, 32, 128, 256], P('tm', 'space')
- grad_input: bfloat16 [32, 32, 128, 256], P('tm', 'space')
- grad_weight: float32 [256, 3, 3, 3, 256], P('space')
All inputs are finite; a program needn't handle non-finite values.
Results may differ from a plain program's by a relative error of at most 0.0032.
Values may be sent and summed in bfloat16 or wider, within the bound.
No kernel may reach another device: no remote copies, remote signals or barrier semaphores. Data moves between devices by JAX's collectives and lax.ppermute only.
A program may use at most 128 MiB of HBM per device.

v0:
```python
import math

import jax
import jax.numpy as jnp
from jax import lax
from jax.sharding import PartitionSpec as P


def shifted(value, axis, steps):
    count = lax.axis_size(axis)
    leading, last = (max(0, -steps), min(count, count - steps))
    return lax.ppermute(value, axis, [(source, source + steps) for source in range(leading, last)])


def extended_2(x, sides, width):
    for axis, dim in sides:
        count, length = (lax.axis_size(axis), x.shape[dim])
        up = [(i, (i + 1) % count) for i in range(count - 1)]
        down = [(j, i) for i, j in up]
        last = lax.slice_in_dim(x, length - width, length, axis=dim)
        leading = lax.slice_in_dim(x, 0, width, axis=dim)
        before = lax.ppermute(last, axis, up)
        after = lax.ppermute(leading, axis, down)
        x = jnp.concatenate([before, x, after], axis=dim)
    return x


def unfold_cols(slab, offsets, count):
    return jnp.concatenate([slab[:, :, shift_c : shift_c + count] for shift_c in offsets], axis=-1)


def local(frames_in, weight, cotangent):
    fr_count, row_count, width, chans = frames_in.shape
    cells = fr_count * row_count * width
    space_count = lax.axis_size("space")
    space_place = lax.axis_index("space")
    carried = shifted(frames_in, "tm", 1)
    extended = jnp.concatenate([carried, frames_in], axis=0)
    extended = extended_2(extended, (("space", 1),), 1)
    extended = jnp.pad(extended, ((0, 0), (0, 0), (1, 1), (0, 0)))
    fwd_mats = weight.reshape(3, 3, 3 * chans, chans)
    back_mats = jnp.transpose(weight, (0, 1, 2, 4, 3)).reshape(3, 3, 3 * chans, chans)
    pieces = []
    preact = jnp.zeros((cells, chans), jnp.float32)
    for tap_t in range(3):
        for tap_h in range(3):
            slab = extended[tap_t : tap_t + fr_count, tap_h : tap_h + row_count]
            piece = unfold_cols(slab, (0, 1, 2), width).reshape(cells, 3 * chans)
            pieces.append(piece)
            preact = preact + jnp.dot(
                piece, fwd_mats[tap_t, tap_h], preferred_element_type=jnp.float32
            )
    own_flat = frames_in.reshape(cells, chans).astype(jnp.float32)
    output = (own_flat + jax.nn.silu(preact)).astype(jnp.bfloat16).reshape(frames_in.shape)
    sigma = jax.nn.sigmoid(preact)
    cot_flat = cotangent.reshape(cells, chans).astype(jnp.float32)
    flat_grad = (cot_flat * sigma * (1.0 + preact * (1.0 - sigma))).astype(jnp.bfloat16)
    grad_pre = flat_grad.reshape(frames_in.shape)
    follow = shifted(grad_pre, "tm", -1)
    grad_ext = jnp.concatenate([grad_pre, follow], axis=0)
    grad_ext = extended_2(grad_ext, (("space", 1),), 1)
    grad_ext = jnp.pad(grad_ext, ((0, 0), (0, 0), (1, 1), (0, 0)))
    back_sum = jnp.zeros((cells, chans), jnp.float32)
    for tap_t in range(3):
        for tap_h in range(3):
            slab = grad_ext[2 - tap_t : 2 - tap_t + fr_count, 2 - tap_h : 2 - tap_h + row_count]
            piece = unfold_cols(slab, (2, 1, 0), width).reshape(cells, 3 * chans)
            back_sum = back_sum + jnp.dot(
                piece, back_mats[tap_t, tap_h], preferred_element_type=jnp.float32
            )
    grad_input = (cot_flat + back_sum).astype(jnp.bfloat16).reshape(frames_in.shape)
    share_rows = chans // space_count
    terms = [
        lax.dot_general(
            flat_grad, piece, (((0,), (0,)), ((), ())), preferred_element_type=jnp.float32
        )
        for piece in pieces
    ]
    summed = lax.psum(jnp.concatenate(terms, axis=1), ("tm", "space"))
    shared = lax.dynamic_slice_in_dim(summed, space_place * share_rows, share_rows, 0)
    total_cells = fr_count * lax.axis_size("tm") * row_count * space_count * width
    scale = 1.0 / math.sqrt(float(total_cells))
    grad_weight = (shared * jnp.float32(scale)).reshape(share_rows, 3, 3, 3, chans)
    return (output, grad_input, grad_weight)


def solution(mesh):
    placed = (P("tm", "space", None, None), P(), P("tm", "space", None, None))
    return jax.shard_map(
        local,
        mesh=mesh,
        in_specs=placed,
        out_specs=(
            P("tm", "space", None, None),
            P("tm", "space", None, None),
            P("space", None, None, None, None),
        ),
        check_vma=False,
    )
```

profile of v0, /device:TPU:1, one launch (start us, length us, event | category | flops | bytes accessed | tf_op | source)
XLA Modules:
  0.0 352.3 jit_solution(12841473491730203490)
XLA Ops:
  7.2 4.6 %collective-permute-start = (bf16[2,2,128,256]{3,2,1,0:T(8,128)(2,1)}, bf16[2,2,128,256]{3,2,1,0:T(8,128)(2,1)S(1)}, u32[]{:S(2)}, u32[]{:S(2)}) collective-permute-start(bf16[2,2,128,256]{3,2,1,0:T(8,128)(2,1)} %param.3), channel_id=1, source_target_pairs={{0,16},{16,32},{32,48},{48,64},{64,80},{80,96},{96,112},{112,128},... | collective-permute-start | bytes 786440 | tf_op jit(solution)/shard_map/ppermute | solution.py:12
  11.8 3.6 %collective-permute-done = bf16[2,2,128,256]{3,2,1,0:T(8,128)(2,1)S(1)} collective-permute-done((bf16[2,2,128,256]{3,2,1,0:T(8,128)(2,1)}, bf16[2,2,128,256]{3,2,1,0:T(8,128)(2,1)S(1)}, u32[]{:S(2)}, u32[]{:S(2)}) %collective-permute-start) | collective-permute-done | bytes 262176 | tf_op jit(solution)/shard_map/ppermute | solution.py:12
  15.4 1.0 constant_dynamic-update-slice_fusion
  16.5 3.6 %collective-permute-start.1 = (bf16[4,1,128,256]{3,2,1,0:T(8,128)(2,1)S(1)}, bf16[4,1,128,256]{3,2,1,0:T(8,128)(2,1)S(1)}, u32[]{:S(2)}, u32[]{:S(2)}) collective-permute-start(bf16[4,1,128,256]{3,2,1,0:T(8,128)(2,1)S(1)} %get-tuple-element.66), channel_id=1, source_target_pairs={{0,1},{1,2},{2,3},{3,4},{4,5},{5,6},{6,7},{7,8},{8,9},{9,10},{10,1... | collective-permute-start | bytes 786440 | tf_op jit(solution)/shard_map/ppermute | solution.py:22
  20.0 1.3 collective-permute-start.2
  21.3 6.1 %copy.7 = bf16[3,3,3,256,256]{3,4,2,1,0:T(8,128)(2,1)} copy(bf16[3,3,3,256,256]{4,3,2,1,0:T(8,128)(2,1)} %param.4) | data formatting | bytes 7077888 | tf_op args[1]
  27.4 0.4 select_maximum_fusion.3
  27.9 0.9 fusion.28
  29.0 1.8 copy-done
  31.4 0.4 convolution_add_fusion.15
  31.7 0.4 convolution_add_fusion.14
  32.2 0.4 convolution_add_fusion.13
  32.6 0.4 convolution_add_fusion.12
  33.0 0.6 copy-done.2
  33.7 0.4 convolution_add_fusion.11
  34.1 0.4 convolution_add_fusion.10
  34.5 0.4 convolution_add_fusion.9
  34.8 0.6 copy-done.3
  35.4 1.3 fusion.16
  36.7 1.3 convolution_dynamic-update-slice_fusion.8
  37.9 1.3 convolution_dynamic-update-slice_fusion.7
  39.2 1.3 convolution_dynamic-update-slice_fusion.6
  40.6 1.3 convolution_dynamic-update-slice_fusion.5
  41.9 1.3 convolution_dynamic-update-slice_fusion.4
  43.2 1.3 convolution_dynamic-update-slice_fusion.3
  44.5 1.3 convolution_dynamic-update-slice_fusion.2
  45.8 1.9 collective-permute-start.3
  47.7 1.3 convolution_dynamic-update-slice_fusion.1
  49.0 7.3 %collective-permute-done.3 = bf16[2,2,128,256]{3,2,1,0:T(8,128)(2,1)S(1)} collective-permute-done((bf16[2,2,128,256]{3,2,1,0:T(8,128)(2,1)S(1)}, bf16[2,2,128,256]{3,2,1,0:T(8,128)(2,1)S(1)}, u32[]{:S(2)}, u32[]{:S(2)}) %collective-permute-start.3) | collective-permute-done | bytes 262176 | tf_op jit(solution)/shard_map/ppermute | solution.py:12
  56.3 3.8 %collective-permute-start.4 = (bf16[4,1,128,256]{3,2,1,0:T(8,128)(2,1)S(1)}, bf16[4,1,128,256]{3,2,1,0:T(8,128)(2,1)S(1)}, u32[]{:S(2)}, u32[]{:S(2)}) collective-permute-start(bf16[4,1,128,256]{3,2,1,0:T(8,128)(2,1)S(1)} %get-tuple-element.57), channel_id=1, source_target_pairs={{0,1},{1,2},{2,3},{3,4},{4,5},{5,6},{6,7},{7,8},{8,9},{9,10},{10,1... | collective-permute-start | bytes 786440 | tf_op jit(solution)/shard_map/ppermute | solution.py:22
  60.2 1.5 collective-permute-start.5
  61.7 1.3 convolution_dynamic-update-slice_fusion
  63.0 0.5 collective-permute-done.4
  63.5 5.2 %collective-permute-done.5 = bf16[4,1,128,256]{3,2,1,0:T(8,128)(2,1)S(1)} collective-permute-done((bf16[4,1,128,256]{3,2,1,0:T(8,128)(2,1)S(1)}, bf16[4,1,128,256]{3,2,1,0:T(8,128)(2,1)S(1)}, u32[]{:S(2)}, u32[]{:S(2)}) %collective-permute-start.5) | collective-permute-done | bytes 262176 | tf_op jit(solution)/shard_map/ppermute | solution.py:23
  68.9 0.4 select_maximum_fusion
  69.3 0.9 fusion.27
  70.8 1.8 copy-done.1
  73.0 0.4 convolution_add_fusion.7
  73.3 0.4 convolution_add_fusion.6
  73.7 0.4 convolution_add_fusion.5
  74.1 0.4 convolution_add_fusion.4
  74.5 0.4 convolution_add_fusion.3
  74.9 0.4 convolution_add_fusion.2
  75.2 0.4 convolution_add_fusion.1
  75.6 1.1 fusion.2
  76.7 266.6 %all-reduce.4.cloned.1.call-done = f32[256,6912]{1,0:T(8,128)} async-done(((f32[256,6912]{1,0:T(8,128)}), f32[256,6912]{1,0:T(8,128)}) %all-reduce.4.cloned.1.call-update) | async-done | bytes 7077904 | tf_op jit(solution)/shard_map/psum | solution.py:79
  343.3 1.1 dynamic-slice_multiply_fusion
  344.6 0.8 copy.8
  (29 shorter events, 2.4 us)
Async XLA Ops:
  7.2 336.2 %all-reduce.4.cloned.1.call-start = ((), (), s32[]{:S(2)}) async-start(), calls=%async_computation | async-start | bytes 14155776 | tf_op jit(solution)/shard_map/psum | solution.py:79
  7.2 8.2 %collective-permute-start = (bf16[2,2,128,256]{3,2,1,0:T(8,128)(2,1)}, bf16[2,2,128,256]{3,2,1,0:T(8,128)(2,1)S(1)}, u32[]{:S(2)}, u32[]{:S(2)}) collective-permute-start(bf16[2,2,128,256]{3,2,1,0:T(8,128)(2,1)} %param.3), channel_id=1, source_target_pairs={{0,16},{16,32},{32,48},{48,64},{64,80},{80,96},{96,112},{112,128},... | collective-permute-start | bytes 786440 | tf_op jit(solution)/shard_map/ppermute | solution.py:12
  16.5 11.0 %collective-permute-start.1 = (bf16[4,1,128,256]{3,2,1,0:T(8,128)(2,1)S(1)}, bf16[4,1,128,256]{3,2,1,0:T(8,128)(2,1)S(1)}, u32[]{:S(2)}, u32[]{:S(2)}) collective-permute-start(bf16[4,1,128,256]{3,2,1,0:T(8,128)(2,1)S(1)} %get-tuple-element.66), channel_id=1, source_target_pairs={{0,1},{1,2},{2,3},{3,4},{4,5},{5,6},{6,7},{7,8},{8,9},{9,10},{10,1... | collective-permute-start | bytes 786440 | tf_op jit(solution)/shard_map/ppermute | solution.py:22
  20.0 7.4 %collective-permute-start.2 = (bf16[4,1,128,256]{3,2,1,0:T(8,128)(2,1)S(1)}, bf16[4,1,128,256]{3,2,1,0:T(8,128)(2,1)S(1)}, u32[]{:S(2)}, u32[]{:S(2)}) collective-permute-start(bf16[4,1,128,256]{3,2,1,0:T(8,128)(2,1)S(1)} %get-tuple-element.67), channel_id=1, source_target_pairs={{1,0},{2,1},{3,2},{4,3},{5,4},{6,5},{7,6},{8,7},{9,8},{10,9},{11,1... | collective-permute-start | bytes 786440 | tf_op jit(solution)/shard_map/ppermute | solution.py:23
  28.9 2.0 copy-start
  32.6 1.0 copy-start.2
  34.5 1.0 copy-start.3
  45.8 10.5 %collective-permute-start.3 = (bf16[2,2,128,256]{3,2,1,0:T(8,128)(2,1)S(1)}, bf16[2,2,128,256]{3,2,1,0:T(8,128)(2,1)S(1)}, u32[]{:S(2)}, u32[]{:S(2)}) collective-permute-start(bf16[2,2,128,256]{3,2,1,0:T(8,128)(2,1)S(1)} %bitcast.123), channel_id=1, source_target_pairs={{16,0},{32,16},{48,32},{64,48},{80,64},{96,80},{112,96},{128,112},... | collective-permute-start | bytes 786440 | tf_op jit(solution)/shard_map/ppermute | solution.py:12
  56.3 7.1 %collective-permute-start.4 = (bf16[4,1,128,256]{3,2,1,0:T(8,128)(2,1)S(1)}, bf16[4,1,128,256]{3,2,1,0:T(8,128)(2,1)S(1)}, u32[]{:S(2)}, u32[]{:S(2)}) collective-permute-start(bf16[4,1,128,256]{3,2,1,0:T(8,128)(2,1)S(1)} %get-tuple-element.57), channel_id=1, source_target_pairs={{0,1},{1,2},{2,3},{3,4},{4,5},{5,6},{6,7},{7,8},{8,9},{9,10},{10,1... | collective-permute-start | bytes 786440 | tf_op jit(solution)/shard_map/ppermute | solution.py:22
  60.2 8.5 %collective-permute-start.5 = (bf16[4,1,128,256]{3,2,1,0:T(8,128)(2,1)S(1)}, bf16[4,1,128,256]{3,2,1,0:T(8,128)(2,1)S(1)}, u32[]{:S(2)}, u32[]{:S(2)}) collective-permute-start(bf16[4,1,128,256]{3,2,1,0:T(8,128)(2,1)S(1)} %get-tuple-element.58), channel_id=1, source_target_pairs={{1,0},{2,1},{3,2},{4,3},{5,4},{6,5},{7,6},{8,7},{9,8},{10,9},{11,1... | collective-permute-start | bytes 786440 | tf_op jit(solution)/shard_map/ppermute | solution.py:23
  70.6 2.0 copy-start.1
Sparse Core Ops, SparseCore 0:
  63.1 280.1 all-reduce.3
where the time goes:
time: 354 us; the launch traced here: 352 us
  waiting for transfers between devices  283 us (80%)
  matrix products  20.1 us (6%)
  starting transfers between devices  16.7 us (5%)
  local copies, waits for them, and re-layouts  14.9 us (4%)
  between operations  14.4 us (4%)
    psum x1, waiting for transfers between devices, local(): summed = lax.psum(jnp.concatenate(terms, axis=1), ('tm', 'space'))  267 us
    dot_general x9, matrix products, local(): lax.dot_general(flat_grad, piece, (((0,), (0,)), ((), ())), preferred_ele...  11.8 us
    unnamed x11, local copies, waits for them, and re-layouts  11.7 us
    ppermute x2, waiting for transfers between devices, shifted(): lax.ppermute(value, axis, [(source, source + steps) for source in range(l...  10.9 us
    ppermute x2, starting transfers between devices, extended_2(): before = lax.ppermute(last, axis, up)  7.41 us
  transfers between devices with their start and end apart: 7, of which 5 were waited for; matrix products, arithmetic and copies ran while one was open for 4% of the time, Pallas kernels for 0%

commit v1 on v0

v1 whole, which is shorter than its diff:
```python
import functools
import itertools
import math

import jax
import jax.numpy as jnp
import numpy as np
from jax import lax
from jax.experimental import pallas as pl
from jax.experimental.pallas import tpu as pltpu
from jax.sharding import PartitionSpec as P

BOTH = ("tm", "space")
VMEM = pltpu.CompilerParams(vmem_limit_bytes=48 * 1024 * 1024)
SIZES = {"x_hi": 2, "y": 4, "core": 2, "x_lo": 2, "z": 8}


def groups_of(names):
    rest = [n for n in SIZES if n not in names]
    groups = []
    for fixed in itertools.product(*(range(SIZES[n]) for n in rest)):
        group = []
        for varied in itertools.product(*(range(SIZES[n]) for n in names)):
            at = dict(zip(rest, fixed)) | dict(zip(names, varied))
            tm = (at["x_hi"] * 4 + at["y"]) * 2 + at["core"]
            group.append(tm * 16 + at["x_lo"] * 8 + at["z"])
        groups.append(group)
    return groups


def exchange(value, names):
    return lax.all_to_all(value, BOTH, 0, 0, tiled=True, axis_index_groups=groups_of(names))


def flip_core(value):
    return lax.ppermute(value, "tm", [(i, i ^ 1) for i in range(16)])


def shifted(value, axis, steps):
    count = lax.axis_size(axis)
    leading, last = (max(0, -steps), min(count, count - steps))
    return lax.ppermute(value, axis, [(source, source + steps) for source in range(leading, last)])


def with_rows(x):
    before = shifted(x[:, -1:], "space", 1)
    after = shifted(x[:, :1], "space", -1)
    return jnp.concatenate([before, x, after], axis=1)


def shift_cols(value, steps):
    zero = jnp.zeros_like(value[:, :1])
    if steps == 1:
        return jnp.concatenate([zero, value[:, :-1]], axis=1)
    return jnp.concatenate([value[:, 1:], zero], axis=1)


def block_of(ref, a, b):
    return ref[a : a + 2, b : b + 2].reshape(512, -1)


def forward_kernel(ext_ref, w_ref, cot_ref, out_ref, grad_ref):
    sums = []
    for c in range(3):
        acc = jnp.zeros((512, 256), jnp.float32)
        for a in range(3):
            for b in range(3):
                acc += jnp.dot(
                    block_of(ext_ref, a, b), w_ref[a, b, c], preferred_element_type=jnp.float32
                )
        sums.append(acc.reshape(4, 128, 256))
    preact = shift_cols(sums[0], 1) + sums[1] + shift_cols(sums[2], -1)
    own = ext_ref[2:4, 1:3].reshape(4, 128, 256).astype(jnp.float32)
    sigma = 1.0 / (1.0 + jnp.exp(-preact))
    out_ref[...] = (own + preact * sigma).astype(jnp.bfloat16).reshape(2, 2, 128, 256)
    cot = cot_ref[...].reshape(4, 128, 256).astype(jnp.float32)
    grad = cot * sigma * (1.0 + preact * (1.0 - sigma))
    grad_ref[...] = grad.astype(jnp.bfloat16).reshape(2, 2, 128, 256)


def backward_kernel(ext_ref, w_ref, cot_ref, out_ref):
    sums = []
    for c in range(3):
        acc = jnp.zeros((512, 256), jnp.float32)
        for a in range(3):
            for b in range(3):
                acc += lax.dot_general(
                    block_of(ext_ref, 2 - a, 2 - b),
                    w_ref[a, b, c],
                    (((1,), (1,)), ((), ())),
                    preferred_element_type=jnp.float32,
                )
        sums.append(acc.reshape(4, 128, 256))
    total = shift_cols(sums[0], -1) + sums[1] + shift_cols(sums[2], 1)
    cot = cot_ref[...].reshape(4, 128, 256).astype(jnp.float32)
    out_ref[...] = (cot + total).astype(jnp.bfloat16).reshape(2, 2, 128, 256)


def weight_kernel(mine_ref, theirs_ref, grad_ref, grad2_ref, order_ref, out_ref):
    order = order_ref[...]
    flipped = []
    for steps in (-1, 0, 1):
        parts = []
        for ref in (grad_ref, grad2_ref):
            value = ref[...].reshape(4, 128, 256)
            if steps:
                value = shift_cols(value.astype(jnp.float32), steps).astype(jnp.bfloat16)
            turned = lax.dot_general(
                order,
                value.reshape(512, 256),
                (((1,), (1,)), ((), ())),
                preferred_element_type=jnp.float32,
            )
            parts.append(turned.astype(jnp.bfloat16))
        flipped.append(jnp.concatenate(parts, axis=1))
    for a in range(3):
        for b in range(3):
            cells = jnp.concatenate(
                [block_of(mine_ref, a, b), block_of(theirs_ref, a, b)], axis=0
            )
            for c in range(3):
                tap = (a * 3 + b) * 3 + c
                out_ref[:, tap * 128 : (tap + 1) * 128] = jnp.dot(
                    flipped[c], cells, preferred_element_type=jnp.float32
                ).astype(jnp.bfloat16)


def call(kernel, shapes, flops):
    return pl.pallas_call(
        kernel,
        out_shape=shapes,
        compiler_params=VMEM,
        cost_estimate=pl.CostEstimate(flops=flops, bytes_accessed=5000000, transcendentals=0),
    )


def row_order():
    channels = np.arange(256).reshape(2, 8, 8, 2).transpose(0, 2, 1, 3).reshape(256)
    return (channels[:, None] == np.arange(256)[None, :]).astype(np.float32)


def local(frames_in, weight, cotangent):
    core = lax.axis_index("tm") % 2
    block = jax.ShapeDtypeStruct((2, 2, 128, 256), jnp.bfloat16)
    flops = 2 * 512 * 6912 * 256

    carried = shifted(frames_in, "tm", 1)
    ext = with_rows(jnp.concatenate([carried, frames_in], axis=0))
    low, high = ext[..., :128], ext[..., 128:]
    mine = jnp.where(core == 0, low, high)
    theirs = flip_core(jnp.where(core == 0, high, low))
    output, grad_pre = call(forward_kernel, (block, block), flops)(ext, weight, cotangent)

    grad_other = flip_core(grad_pre)
    order = jnp.asarray(row_order(), jnp.bfloat16)
    terms = call(weight_kernel, jax.ShapeDtypeStruct((256, 3456), jnp.bfloat16), flops)(
        mine, theirs, grad_pre, grad_other, order
    )
    got = exchange(terms, ("x_lo", "x_hi", "y")).reshape(16, 16, 3456)
    plane = jnp.sum(got.astype(jnp.float32), axis=0)
    got = exchange(plane, ("z",)).reshape(8, 2, 3456)
    scale = 1.0 / math.sqrt(32.0 * 32.0 * 128.0)
    total = jnp.sum(got, axis=0) * jnp.float32(scale)
    share = lax.all_gather(total, "tm", axis=0, tiled=False)
    share = share.reshape(8, 2, 2, 27, 128).transpose(0, 2, 3, 1, 4)
    grad_weight = share.reshape(16, 3, 3, 3, 256)

    follow = shifted(grad_pre, "tm", -1)
    grad_ext = with_rows(jnp.concatenate([grad_pre, follow], axis=0))
    grad_input = call(backward_kernel, block, flops)(grad_ext, weight, cotangent)
    return (output, grad_input, grad_weight)


def solution(mesh):
    placed = (P("tm", "space", None, None), P(), P("tm", "space", None, None))
    return jax.shard_map(
        local,
        mesh=mesh,
        in_specs=placed,
        out_specs=(
            P("tm", "space", None, None),
            P("tm", "space", None, None),
            P("space", None, None, None, None),
        ),
        check_vma=False,
    )
```

time: 354 us -> 124 us (0.35)
  waiting for transfers between devices: 283 us -> 37.5 us
  blocking collectives: 0 us -> 25.2 us
  starting transfers between devices: 16.7 us -> 37.1 us
  matrix products: 20.1 us -> 0 us
  between operations: 14.4 us -> 0.87 us
  Pallas kernels: 0 us -> 11.1 us
  local copies, waits for them, and re-layouts: 14.9 us -> 6.29 us
    psum x1 -> x0, waiting for transfers between devices: 267 us -> none  [local(): summed = lax.psum(jnp.concatenate(terms, axis=1), ('tm', 'space'))]
    all_gather x0 -> x1, blocking collectives: none -> 25.2 us  [local(): share = lax.all_gather(total, 'tm', axis=0, tiled=False)]
    ppermute x2 -> x6, waiting for transfers between devices: 10.9 us -> 31.4 us  [shifted(): lax.ppermute(value, axis, [(source, source + steps) for source in range(l...]
    all_to_all x0 -> x2, starting transfers between devices: none -> 20.3 us  [exchange(): lax.all_to_all(value, BOTH, 0, 0, tiled=True, axis_index_groups=groups_of...]
    dot_general x27 -> x0, matrix products: 20.1 us -> none  [the longest x9 11.8 us: local(): lax.dot_general(flat_grad, piece, (((0,), (0,)), ((), ())), preferred_ele...]
    pallas_call x0 -> x3, Pallas kernels: none -> 11.1 us  [the longest x1 5.52 us: local(): call(weight_kernel, jax.ShapeDtypeStruct((256, 3456), jnp.bfloat16), flops)]
    unnamed x11 -> x14, local copies, waits for them, and re-layouts: 11.7 us -> 0.85 us
    ppermute x2 -> x6, starting transfers between devices: 6.51 us -> 16.3 us  [shifted(): lax.ppermute(value, axis, [(source, source + steps) for source in range(l...]
  transfers between devices with their start and end apart: 7 -> 10, of which waited for: 5 -> 6; matrix products, arithmetic and copies ran while one was open for 4% -> 4% of each run, Pallas kernels for 0% -> 5%
where the time goes in v1:
time: 124 us; the launch traced here: 123 us
  waiting for transfers between devices  37.5 us (30%)
  starting transfers between devices  37.1 us (30%)
  blocking collectives  25.2 us (20%)
  Pallas kernels  11.1 us (9%)
  local copies, waits for them, and re-layouts  6.29 us (5%)
  other arithmetic  5.15 us (4%)
    ppermute x6, waiting for transfers between devices, shifted(): lax.ppermute(value, axis, [(source, source + steps) for source in range(l...  31.4 us
    all_gather x1, blocking collectives, local(): share = lax.all_gather(total, 'tm', axis=0, tiled=False)  25.2 us
    all_to_all x2, starting transfers between devices, exchange(): lax.all_to_all(value, BOTH, 0, 0, tiled=True, axis_index_groups=groups_of...  20.3 us
    ppermute x6, starting transfers between devices, shifted(): lax.ppermute(value, axis, [(source, source + steps) for source in range(l...  16.3 us
    pallas_call x1, Pallas kernels, local(): call(weight_kernel, jax.ShapeDtypeStruct((256, 3456), jnp.bfloat16), flops)  5.52 us
    all_to_all x2, waiting for transfers between devices, exchange(): lax.all_to_all(value, BOTH, 0, 0, tiled=True, axis_index_groups=groups_of...  4.87 us
    pallas_call x1, Pallas kernels, local(): call(forward_kernel, (block, block), flops)(ext, weight, cotangent)  2.9 us
    pallas_call x1, Pallas kernels, local(): call(backward_kernel, block, flops)(grad_ext, weight, cotangent)  2.73 us
  transfers between devices with their start and end apart: 10, of which 6 were waited for; matrix products, arithmetic and copies ran while one was open for 4% of the time, Pallas kernels for 5%

profile of v1, /device:TPU:1, one launch (start us, length us, event | category | flops | bytes accessed | tf_op | source)
XLA Modules:
  0.0 123.2 jit_solution(10503749029890928289)
XLA Ops:
  0.6 4.6 %collective-permute-start = (bf16[2,2,128,256]{3,2,1,0:T(8,128)(2,1)}, bf16[2,2,128,256]{3,2,1,0:T(8,128)(2,1)S(1)}, u32[]{:S(2)}, u32[]{:S(2)}) collective-permute-start(bf16[2,2,128,256]{3,2,1,0:T(8,128)(2,1)} %param.4), channel_id=1, source_target_pairs={{0,16},{16,32},{32,48},{48,64},{64,80},{80,96},{96,112},{112,128},... | collective-permute-start | bytes 786440 | tf_op jit(solution)/shard_map/ppermute | solution.py:42
  5.2 3.6 %collective-permute-done = bf16[2,2,128,256]{3,2,1,0:T(8,128)(2,1)S(1)} collective-permute-done((bf16[2,2,128,256]{3,2,1,0:T(8,128)(2,1)}, bf16[2,2,128,256]{3,2,1,0:T(8,128)(2,1)S(1)}, u32[]{:S(2)}, u32[]{:S(2)}) %collective-permute-start) | collective-permute-done | bytes 262176 | tf_op jit(solution)/shard_map/ppermute | solution.py:42
  8.9 1.0 constant_dynamic-update-slice_fusion
  9.9 3.6 %collective-permute-start.1 = (bf16[4,1,128,256]{3,2,1,0:T(8,128)(2,1)S(1)}, bf16[4,1,128,256]{3,2,1,0:T(8,128)(2,1)S(1)}, u32[]{:S(2)}, u32[]{:S(2)}) collective-permute-start(bf16[4,1,128,256]{3,2,1,0:T(8,128)(2,1)S(1)} %get-tuple-element.11), channel_id=1, source_target_pairs={{0,1},{1,2},{2,3},{3,4},{4,5},{5,6},{6,7},{7,8},{8,9},{9,10},{10,1... | collective-permute-start | bytes 786440 | tf_op jit(solution)/shard_map/ppermute | solution.py:42
  13.4 1.3 %collective-permute-start.2 = (bf16[4,1,128,256]{3,2,1,0:T(8,128)(2,1)S(1)}, bf16[4,1,128,256]{3,2,1,0:T(8,128)(2,1)S(1)}, u32[]{:S(2)}, u32[]{:S(2)}) collective-permute-start(bf16[4,1,128,256]{3,2,1,0:T(8,128)(2,1)S(1)} %get-tuple-element.12), channel_id=1, source_target_pairs={{1,0},{2,1},{3,2},{4,3},{5,4},{6,5},{7,6},{8,7},{9,8},{10,9},{11,1... | collective-permute-start | bytes 786440 | tf_op jit(solution)/shard_map/ppermute | solution.py:42
  14.8 0.0 copy-start
  14.8 0.0 copy-start.2
  14.8 1.9 %collective-permute-done.1 = bf16[4,1,128,256]{3,2,1,0:T(8,128)(2,1)S(1)} collective-permute-done((bf16[4,1,128,256]{3,2,1,0:T(8,128)(2,1)S(1)}, bf16[4,1,128,256]{3,2,1,0:T(8,128)(2,1)S(1)}, u32[]{:S(2)}, u32[]{:S(2)}) %collective-permute-start.1) | collective-permute-done | bytes 262176 | tf_op jit(solution)/shard_map/ppermute | solution.py:42
  16.7 4.0 %collective-permute-done.2 = bf16[4,1,128,256]{3,2,1,0:T(8,128)(2,1)S(1)} collective-permute-done((bf16[4,1,128,256]{3,2,1,0:T(8,128)(2,1)S(1)}, bf16[4,1,128,256]{3,2,1,0:T(8,128)(2,1)S(1)}, u32[]{:S(2)}, u32[]{:S(2)}) %collective-permute-start.2) | collective-permute-done | bytes 262176 | tf_op jit(solution)/shard_map/ppermute | solution.py:42
  20.7 0.1 pad_maximum_fusion.ext_ref
  20.9 0.1 broadcast_select_fusion
  20.9 0.0 copy-start.4
  21.0 0.1 collective-permute-start.6
  21.1 0.0 copy-done
  21.1 0.0 copy-done.2
  21.1 2.9 %shard_map.67 = (bf16[2,2,128,256]{3,2,1,0:T(8,128)(2,1)}, bf16[2,2,128,256]{3,2,1,0:T(8,128)(2,1)S(1)}) custom-call(bf16[4,4,128,256]{3,2,1,0:T(8,128)(2,1)S(1)} %pad_maximum_fusion.ext_ref, bf16[3,3,3,256,256]{4,3,2,1,0:T(8,128)(2,1)S(1)} %copy-done, bf16[2,2,128,256]{3,2,1,0:T(8,128)(2,1)S(1)} %copy-done.2), custom_call_target="tpu_custom_call" | custom-call | flops 1811939328 | bytes 5000000 | tf_op jit(solution)/shard_map/pallas_call | solution.py:152
  24.0 0.5 collective-permute-start.7
  24.5 1.2 collective-permute-done.7.grad2_ref
  25.6 0.0 collective-permute-done.6.theirs_ref
  25.6 0.0 copy-done.4
  25.6 5.5 %shard_map.69 = bf16[256,3456]{1,0:T(8,128)(2,1)} custom-call(bf16[4,4,128,128]{3,2,1,0:T(8,128)(2,1)S(1)} %get-tuple-element.8.mine_ref, bf16[4,4,128,128]{3,2,1,0:T(8,128)(2,1)S(1)} %collective-permute-done.6.theirs_ref, bf16[2,2,128,256]{3,2,1,0:T(8,128)(2,1)S(1)} %get-tuple-element.6.grad_ref, ...), custom_call_target="tpu_custom_call" | custom-call | flops 1811939328 | bytes 5000000 | tf_op jit(solution)/shard_map/pallas_call | solution.py:156
  31.1 11.6 %all-to-all-start = ((bf16[16,16,3456]{2,1,0:T(8,128)(2,1)}), bf16[16,16,3456]{2,1,0:T(8,128)(2,1)}, u32[]{:S(2)}, u32[]{:S(2)}) async-start(bf16[16,16,3456]{2,1,0:T(8,128)(2,1)} %bitcast), calls=%async_computation | async-start | bytes 3538944 | tf_op jit(solution)/shard_map/all_to_all | solution.py:32
  42.7 2.3 %collective-permute-start.3 = (bf16[2,2,128,256]{3,2,1,0:T(8,128)(2,1)S(1)}, bf16[2,2,128,256]{3,2,1,0:T(8,128)(2,1)S(1)}, u32[]{:S(2)}, u32[]{:S(2)}) collective-permute-start(bf16[2,2,128,256]{3,2,1,0:T(8,128)(2,1)S(1)} %get-tuple-element.6.grad_ref), channel_id=1, source_target_pairs={{16,0},{32,16},{48,32},{64,48},{80,64},{96,80},{112,96},{128,112},... | collective-permute-start | bytes 786440 | tf_op jit(solution)/shard_map/ppermute | solution.py:42
  45.1 21.9 %collective-permute-done.3 = bf16[2,2,128,256]{3,2,1,0:T(8,128)(2,1)S(1)} collective-permute-done((bf16[2,2,128,256]{3,2,1,0:T(8,128)(2,1)S(1)}, bf16[2,2,128,256]{3,2,1,0:T(8,128)(2,1)S(1)}, u32[]{:S(2)}, u32[]{:S(2)}) %collective-permute-start.3) | collective-permute-done | bytes 262176 | tf_op jit(solution)/shard_map/ppermute | solution.py:42
  67.0 0.0 copy-start.5
  67.0 0.8 copy-done.5
  67.8 0.8 fusion
  68.6 3.2 %collective-permute-start.4 = (bf16[4,1,128,256]{3,2,1,0:T(8,128)(2,1)}, bf16[4,1,128,256]{3,2,1,0:T(8,128)(2,1)}, u32[]{:S(2)}, u32[]{:S(2)}) collective-permute-start(bf16[4,1,128,256]{3,2,1,0:T(8,128)(2,1)} %get-tuple-element.9), channel_id=1, source_target_pairs={{0,1},{1,2},{2,3},{3,4},{4,5},{5,6},{6,7},{7,8},{8,9},{9,10},{10,1... | collective-permute-start | bytes 786440 | tf_op jit(solution)/shard_map/ppermute | solution.py:42
  71.8 1.3 %collective-permute-start.5 = (bf16[4,1,128,256]{3,2,1,0:T(8,128)(2,1)}, bf16[4,1,128,256]{3,2,1,0:T(8,128)(2,1)}, u32[]{:S(2)}, u32[]{:S(2)}) collective-permute-start(bf16[4,1,128,256]{3,2,1,0:T(8,128)(2,1)} %get-tuple-element.10), channel_id=1, source_target_pairs={{1,0},{2,1},{3,2},{4,3},{5,4},{6,5},{7,6},{8,7},{9,8},{10,9},{11,1... | collective-permute-start | bytes 786440 | tf_op jit(solution)/shard_map/ppermute | solution.py:42
  73.1 0.0 all-to-all-done
  73.1 0.0 copy-start.1
  73.1 2.6 %convert_reduce_fusion = f32[16,3456]{1,0:T(8,128)} fusion(bf16[16,16,3456]{2,1,0:T(8,128)(2,1)} %all-to-all-done), kind=kLoop, calls=%fused_computation | loop fusion | flops 1714176 | bytes 1990656 | tf_op jit(solution)/shard_map/reduce_sum | solution.py:160
  75.7 1.8 %all_to_all.14 = f32[8,2,3456]{2,1,0:T(2,128)} reshape(f32[16,3456]{1,0:T(8,128)} %convert_reduce_fusion) | data formatting | bytes 442368 | tf_op jit(solution)/shard_map/all_to_all | solution.py:32
  77.4 8.7 %all-to-all-start.1 = ((f32[8,2,3456]{2,1,0:T(2,128)}), f32[8,2,3456]{2,1,0:T(2,128)}, u32[]{:S(2)}, u32[]{:S(2)}) async-start(f32[8,2,3456]{2,1,0:T(2,128)} %all_to_all.14), calls=%async_computation.1 | async-start | bytes 442368 | tf_op jit(solution)/shard_map/all_to_all | solution.py:32
  86.1 0.0 copy-start.3
  86.2 0.0 collective-permute-done.4
  86.2 0.0 collective-permute-done.5
  86.2 1.3 %pad_maximum_fusion.1.ext_ref = bf16[4,4,128,256]{3,2,1,0:T(8,128)(2,1)S(1)} fusion(bf16[4,1,128,256]{3,2,1,0:T(8,128)(2,1)} %collective-permute-done.5, bf16[4,2,128,256]{3,2,1,0:T(8,128)(2,1)} %copy-done.5, bf16[4,1,128,256]{3,2,1,0:T(8,128)(2,1)} %collective-permute-done.4), kind=kLoop, calls=%fused_computation.2 | loop fusion | flops 1048576 | bytes 2097152 | tf_op jit(solution)/shard_map/concatenate | solution.py:48
  87.5 0.0 copy-done.1
  87.5 0.0 copy-done.3
  87.5 2.7 %shard_map.68 = bf16[2,2,128,256]{3,2,1,0:T(8,128)(2,1)} custom-call(bf16[4,4,128,256]{3,2,1,0:T(8,128)(2,1)S(1)} %pad_maximum_fusion.1.ext_ref, bf16[3,3,3,256,256]{4,3,2,1,0:T(8,128)(2,1)S(1)} %copy-done.1, bf16[2,2,128,256]{3,2,1,0:T(8,128)(2,1)S(1)} %copy-done.3), custom_call_target="tpu_custom_call" | custom-call | flops 1811939328 | bytes 5000000 | tf_op jit(solution)/shard_map/pallas_call | solution.py:170
  90.3 4.9 %all-to-all-done.1 = f32[8,2,3456]{2,1,0:T(2,128)} async-done(((f32[8,2,3456]{2,1,0:T(2,128)}), f32[8,2,3456]{2,1,0:T(2,128)}, u32[]{:S(2)}, u32[]{:S(2)}) %all-to-all-start.1) | async-done | bytes 221216 | tf_op jit(solution)/shard_map/all_to_all | solution.py:32
  95.1 1.0 reduce_sum.19
  96.2 25.2 %all-gather.1 = f32[16,2,3456]{2,1,0:T(2,128)S(1)} all-gather(f32[1,2,3456]{2,1,0:T(2,128)S(1)} %multiply_bitcast_fusion), channel_id=2, replica_groups=mesh['tm'=16,'space'=16] {'tm'}, dimensions={0}, use_global_device_ids=true | all-gather | bytes 470016 | tf_op jit(solution)/shard_map/all_gather | solution.py:164
  121.4 0.4 reshape.36
  121.7 0.3 copy.14
  122.1 1.1 reshape.30
  (5 shorter events, 0.1 us)
Async XLA Ops:
  0.6 8.2 %collective-permute-start = (bf16[2,2,128,256]{3,2,1,0:T(8,128)(2,1)}, bf16[2,2,128,256]{3,2,1,0:T(8,128)(2,1)S(1)}, u32[]{:S(2)}, u32[]{:S(2)}) collective-permute-start(bf16[2,2,128,256]{3,2,1,0:T(8,128)(2,1)} %param.4), channel_id=1, source_target_pairs={{0,16},{16,32},{32,48},{48,64},{64,80},{80,96},{96,112},{112,128},... | collective-permute-start | bytes 786440 | tf_op jit(solution)/shard_map/ppermute | solution.py:42
  9.9 6.8 %collective-permute-start.1 = (bf16[4,1,128,256]{3,2,1,0:T(8,128)(2,1)S(1)}, bf16[4,1,128,256]{3,2,1,0:T(8,128)(2,1)S(1)}, u32[]{:S(2)}, u32[]{:S(2)}) collective-permute-start(bf16[4,1,128,256]{3,2,1,0:T(8,128)(2,1)S(1)} %get-tuple-element.11), channel_id=1, source_target_pairs={{0,1},{1,2},{2,3},{3,4},{4,5},{5,6},{6,7},{7,8},{8,9},{9,10},{10,1... | collective-permute-start | bytes 786440 | tf_op jit(solution)/shard_map/ppermute | solution.py:42
  13.4 7.3 %collective-permute-start.2 = (bf16[4,1,128,256]{3,2,1,0:T(8,128)(2,1)S(1)}, bf16[4,1,128,256]{3,2,1,0:T(8,128)(2,1)S(1)}, u32[]{:S(2)}, u32[]{:S(2)}) collective-permute-start(bf16[4,1,128,256]{3,2,1,0:T(8,128)(2,1)S(1)} %get-tuple-element.12), channel_id=1, source_target_pairs={{1,0},{2,1},{3,2},{4,3},{5,4},{6,5},{7,6},{8,7},{9,8},{10,9},{11,1... | collective-permute-start | bytes 786440 | tf_op jit(solution)/shard_map/ppermute | solution.py:42
  14.8 6.3 %copy-start = (bf16[3,3,3,256,256]{4,3,2,1,0:T(8,128)(2,1)S(1)}, bf16[3,3,3,256,256]{4,3,2,1,0:T(8,128)(2,1)}, u32[]{:S(2)}) copy-start(bf16[3,3,3,256,256]{4,3,2,1,0:T(8,128)(2,1)} %w_ref.3) | copy-start | bytes 10616836
  14.8 6.3 %copy-start.2 = (bf16[2,2,128,256]{3,2,1,0:T(8,128)(2,1)S(1)}, bf16[2,2,128,256]{3,2,1,0:T(8,128)(2,1)}, u32[]{:S(2)}) copy-start(bf16[2,2,128,256]{3,2,1,0:T(8,128)(2,1)} %cot_ref.3) | copy-start | bytes 786436
  20.9 4.7 %copy-start.4 = (bf16[256,256]{1,0:T(8,128)(2,1)S(1)}, bf16[256,256]{1,0:T(8,128)(2,1)}, u32[]{:S(2)}) copy-start(bf16[256,256]{1,0:T(8,128)(2,1)} %constant.25.clone.order_ref) | copy-start | bytes 393220
  21.0 4.7 %collective-permute-start.6 = (bf16[4,4,128,128]{3,2,1,0:T(8,128)(2,1)S(1)}, bf16[4,4,128,128]{3,2,1,0:T(8,128)(2,1)S(1)}, u32[]{:S(2)}, u32[]{:S(2)}) collective-permute-start(bf16[4,4,128,128]{3,2,1,0:T(8,128)(2,1)S(1)} %get-tuple-element.7), channel_id=1, source_target_pairs={{0,16},{16,0},{32,48},{48,32},{64,80},{80,64},{96,112},{112,96},{1... | collective-permute-start | bytes 1572872 | tf_op jit(solution)/shard_map/ppermute | solution.py:36
  24.0 1.6 %collective-permute-start.7 = (bf16[2,2,128,256]{3,2,1,0:T(8,128)(2,1)S(1)}, bf16[2,2,128,256]{3,2,1,0:T(8,128)(2,1)S(1)}, u32[]{:S(2)}, u32[]{:S(2)}) collective-permute-start(bf16[2,2,128,256]{3,2,1,0:T(8,128)(2,1)S(1)} %get-tuple-element.6.grad_ref), channel_id=1, source_target_pairs={{0,16},{16,0},{32,48},{48,32},{64,80},{80,64},{96,112},{112,96},{1... | collective-permute-start | bytes 786440 | tf_op jit(solution)/shard_map/ppermute | solution.py:36
  31.1 41.9 %all-to-all-start = ((bf16[16,16,3456]{2,1,0:T(8,128)(2,1)}), bf16[16,16,3456]{2,1,0:T(8,128)(2,1)}, u32[]{:S(2)}, u32[]{:S(2)}) async-start(bf16[16,16,3456]{2,1,0:T(8,128)(2,1)} %bitcast), calls=%async_computation | async-start | bytes 3538944 | tf_op jit(solution)/shard_map/all_to_all | solution.py:32
  42.7 24.2 %collective-permute-start.3 = (bf16[2,2,128,256]{3,2,1,0:T(8,128)(2,1)S(1)}, bf16[2,2,128,256]{3,2,1,0:T(8,128)(2,1)S(1)}, u32[]{:S(2)}, u32[]{:S(2)}) collective-permute-start(bf16[2,2,128,256]{3,2,1,0:T(8,128)(2,1)S(1)} %get-tuple-element.6.grad_ref), channel_id=1, source_target_pairs={{16,0},{32,16},{48,32},{64,48},{80,64},{96,80},{112,96},{128,112},... | collective-permute-start | bytes 786440 | tf_op jit(solution)/shard_map/ppermute | solution.py:42
  67.0 0.8 copy-start.5
  68.6 17.6 %collective-permute-start.4 = (bf16[4,1,128,256]{3,2,1,0:T(8,128)(2,1)}, bf16[4,1,128,256]{3,2,1,0:T(8,128)(2,1)}, u32[]{:S(2)}, u32[]{:S(2)}) collective-permute-start(bf16[4,1,128,256]{3,2,1,0:T(8,128)(2,1)} %get-tuple-element.9), channel_id=1, source_target_pairs={{0,1},{1,2},{2,3},{3,4},{4,5},{5,6},{6,7},{7,8},{8,9},{9,10},{10,1... | collective-permute-start | bytes 786440 | tf_op jit(solution)/shard_map/ppermute | solution.py:42
  71.8 14.4 %collective-permute-start.5 = (bf16[4,1,128,256]{3,2,1,0:T(8,128)(2,1)}, bf16[4,1,128,256]{3,2,1,0:T(8,128)(2,1)}, u32[]{:S(2)}, u32[]{:S(2)}) collective-permute-start(bf16[4,1,128,256]{3,2,1,0:T(8,128)(2,1)} %get-tuple-element.10), channel_id=1, source_target_pairs={{1,0},{2,1},{3,2},{4,3},{5,4},{6,5},{7,6},{8,7},{9,8},{10,9},{11,1... | collective-permute-start | bytes 786440 | tf_op jit(solution)/shard_map/ppermute | solution.py:42
  73.1 14.4 %copy-start.1 = (bf16[3,3,3,256,256]{4,3,2,1,0:T(8,128)(2,1)S(1)}, bf16[3,3,3,256,256]{4,3,2,1,0:T(8,128)(2,1)}, u32[]{:S(2)}) copy-start(bf16[3,3,3,256,256]{4,3,2,1,0:T(8,128)(2,1)} %w_ref.3) | copy-start | bytes 10616836
  77.4 17.7 %all-to-all-start.1 = ((f32[8,2,3456]{2,1,0:T(2,128)}), f32[8,2,3456]{2,1,0:T(2,128)}, u32[]{:S(2)}, u32[]{:S(2)}) async-start(f32[8,2,3456]{2,1,0:T(2,128)} %all_to_all.14), calls=%async_computation.1 | async-start | bytes 442368 | tf_op jit(solution)/shard_map/all_to_all | solution.py:32
  86.1 1.4 %copy-start.3 = (bf16[2,2,128,256]{3,2,1,0:T(8,128)(2,1)S(1)}, bf16[2,2,128,256]{3,2,1,0:T(8,128)(2,1)}, u32[]{:S(2)}) copy-start(bf16[2,2,128,256]{3,2,1,0:T(8,128)(2,1)} %cot_ref.3) | copy-start | bytes 786436

commit v2 on v1

--- a/solution.py
+++ b/solution.py
@@ -42,10 +42,10 @@
     return lax.ppermute(value, axis, [(source, source + steps) for source in range(leading, last)])
 
 
-def with_rows(x):
-    before = shifted(x[:, -1:], "space", 1)
-    after = shifted(x[:, :1], "space", -1)
-    return jnp.concatenate([before, x, after], axis=1)
+def with_rows(first, second):
+    before = shifted(jnp.concatenate([first[:, -1:], second[:, -1:]], axis=0), "space", 1)
+    after = shifted(jnp.concatenate([first[:, :1], second[:, :1]], axis=0), "space", -1)
+    return jnp.concatenate([before, jnp.concatenate([first, second], axis=0), after], axis=1)
 
 
 def shift_cols(value, steps):
@@ -113,16 +113,60 @@
             )
             parts.append(turned.astype(jnp.bfloat16))
         flipped.append(jnp.concatenate(parts, axis=1))
-    for a in range(3):
-        for b in range(3):
-            cells = jnp.concatenate(
-                [block_of(mine_ref, a, b), block_of(theirs_ref, a, b)], axis=0
-            )
+    turned = jnp.concatenate(flipped, axis=0)
+    taps = [(a, b) for a in range(3) for b in range(3)]
+    for start in range(0, 9, 2):
+        some = taps[start : start + 2]
+        cells = jnp.concatenate(
+            [
+                jnp.concatenate([block_of(mine_ref, a, b) for a, b in some], axis=1),
+                jnp.concatenate([block_of(theirs_ref, a, b) for a, b in some], axis=1),
+            ],
+            axis=0,
+        )
+        terms = jnp.dot(turned, cells, preferred_element_type=jnp.float32).astype(jnp.bfloat16)
+        for i in range(len(some)):
             for c in range(3):
-                tap = (a * 3 + b) * 3 + c
-                out_ref[:, tap * 128 : (tap + 1) * 128] = jnp.dot(
-                    flipped[c], cells, preferred_element_type=jnp.float32
-                ).astype(jnp.bfloat16)
+                tap = (start + i) * 3 + c
+                out_ref[:, tap * 128 : (tap + 1) * 128] = terms[
+                    c * 256 : (c + 1) * 256, i * 128 : (i + 1) * 128
+                ]
+
+
+def edge_kernel(first_ref, second_ref, last_ref, leading_ref):
+    for i, ref in enumerate((first_ref, second_ref)):
+        last_ref[2 * i : 2 * i + 2] = ref[:, 1:]
+        leading_ref[2 * i : 2 * i + 2] = ref[:, :1]
+
+
+def plane_kernel(got_ref, out_ref):
+    total = got_ref[0].astype(jnp.float32)
+    for i in range(1, 16):
+        total += got_ref[i].astype(jnp.float32)
+    for z in range(8):
+        out_ref[z] = total[2 * z : 2 * z + 2].astype(out_ref.dtype)
+
+
+def line_kernel(got_ref, out_ref):
+    total = got_ref[0].astype(jnp.float32)
+    for i in range(1, 8):
+        total += got_ref[i].astype(jnp.float32)
+    total *= 1.0 / math.sqrt(32.0 * 32.0 * 128.0)
+    for i in range(8):
+        out_ref[i] = total
+
+
+def share_kernel(mine_ref, other_ref, out_ref):
+    core = lax.axis_index("tm") % 2
+    for tap in range(27):
+        lanes = slice(tap * 128, (tap + 1) * 128)
+        mine = jnp.concatenate([mine_ref[q, :, lanes] for q in range(8)], axis=0)
+        other = jnp.concatenate([other_ref[q, :, lanes] for q in range(8)], axis=0)
+        out_ref[tap] = jnp.where(
+            core == 0,
+            jnp.concatenate([mine, other], axis=1),
+            jnp.concatenate([other, mine], axis=1),
+        )
 
 
 def call(kernel, shapes, flops):
@@ -145,7 +189,7 @@
     flops = 2 * 512 * 6912 * 256
 
     carried = shifted(frames_in, "tm", 1)
-    ext = with_rows(jnp.concatenate([carried, frames_in], axis=0))
+    ext = with_rows(carried, frames_in)
     low, high = ext[..., :128], ext[..., 128:]
     mine = jnp.where(core == 0, low, high)
     theirs = flip_core(jnp.where(core == 0, high, low))
@@ -156,18 +200,34 @@
     terms = call(weight_kernel, jax.ShapeDtypeStruct((256, 3456), jnp.bfloat16), flops)(
         mine, theirs, grad_pre, grad_other, order
     )
+    follow = shifted(grad_pre, "tm", -1)
     got = exchange(terms, ("x_lo", "x_hi", "y")).reshape(16, 16, 3456)
-    plane = jnp.sum(got.astype(jnp.float32), axis=0)
+    plane = pl.pallas_call(
+        plane_kernel,
+        out_shape=jax.ShapeDtypeStruct((8, 2, 3456), jnp.bfloat16),
+        grid=(3,),
+        in_specs=[pl.BlockSpec((16, 16, 1152), lambda i: (0, 0, i))],
+        out_specs=pl.BlockSpec((8, 2, 1152), lambda i: (0, 0, i)),
+        compiler_params=VMEM,
+    )(got)
+    held, follow, plane = lax.optimization_barrier((grad_pre, follow, plane))
+    edge = jax.ShapeDtypeStruct((4, 1, 128, 256), jnp.bfloat16)
+    last, leading = call(edge_kernel, (edge, edge), flops)(held, follow)
     got = exchange(plane, ("z",)).reshape(8, 2, 3456)
-    scale = 1.0 / math.sqrt(32.0 * 32.0 * 128.0)
-    total = jnp.sum(got, axis=0) * jnp.float32(scale)
-    share = lax.all_gather(total, "tm", axis=0, tiled=False)
-    share = share.reshape(8, 2, 2, 27, 128).transpose(0, 2, 3, 1, 4)
-    grad_weight = share.reshape(16, 3, 3, 3, 256)
-
-    follow = shifted(grad_pre, "tm", -1)
-    grad_ext = with_rows(jnp.concatenate([grad_pre, follow], axis=0))
+    got, _, _ = lax.optimization_barrier((got, last, leading))
+    before = shifted(last, "space", 1)
+    after = shifted(leading, "space", -1)
+    grad_ext = jnp.concatenate([before, jnp.concatenate([held, follow], axis=0), after], axis=1)
+    copies = call(line_kernel, jax.ShapeDtypeStruct((8, 2, 3456), jnp.float32), 100000)(got)
+    copies, grad_ext = lax.optimization_barrier((copies, grad_ext))
+    share = exchange(copies, ("x_hi", "y")).reshape(8, 2, 3456)
     grad_input = call(backward_kernel, block, flops)(grad_ext, weight, cotangent)
+    share, grad_input = lax.optimization_barrier((share, grad_input))
+    other = flip_core(share)
+    share = call(share_kernel, jax.ShapeDtypeStruct((27, 16, 256), jnp.float32), 100000)(
+        share, other
+    )
+    grad_weight = share.transpose(1, 0, 2).reshape(16, 3, 3, 3, 256)
     return (output, grad_input, grad_weight)
 
 

time: 124 us -> 105 us (0.85)
  blocking collectives: 25.2 us -> 16.9 us
  other arithmetic: 5.15 us -> 0.39 us
  local copies, waits for them, and re-layouts: 6.29 us -> 3.03 us
  waiting for transfers between devices: 37.5 us -> 35.3 us
    all_gather x1 -> x0, blocking collectives: 25.2 us -> none  [local(): share = lax.all_gather(total, 'tm', axis=0, tiled=False)]
    ppermute x6, waiting for transfers between devices: 31.4 us -> 9.78 us  [shifted(): lax.ppermute(value, axis, [(source, source + steps) for source in range(l...]
    all_to_all x2, waiting for transfers between devices: 4.87 us -> 23.2 us  [exchange(): lax.all_to_all(value, BOTH, 0, 0, tiled=True, axis_index_groups=groups_of...]
    all_to_all x0 -> x1, blocking collectives: none -> 16.9 us  [exchange(): lax.all_to_all(value, BOTH, 0, 0, tiled=True, axis_index_groups=groups_of...]
    reduce_sum x2 -> x0, other arithmetic: 3.59 us -> none  [the longest x1 2.57 us: local(): plane = jnp.sum(got.astype(jnp.float32), axis=0)]
    ppermute x2 -> x3, starting transfers between devices: 0.57 us -> 2.77 us  [flip_core(): return lax.ppermute(value, 'tm', [(i, i ^ 1) for i in range(16)])]
    pallas_call x0 -> x4, Pallas kernels: none -> 2.14 us  [the longest x1 0.9 us: local(): call(share_kernel, jax.ShapeDtypeStruct((27, 16, 256), jnp.float32), 100000)]
    all_to_all x2, starting transfers between devices: 20.3 us -> 18.4 us  [exchange(): lax.all_to_all(value, BOTH, 0, 0, tiled=True, axis_index_groups=groups_of...]
  transfers between devices with their start and end apart: 10 -> 11, of which waited for: 6 -> 8; matrix products, arithmetic and copies ran while one was open for 4% -> 1% of each run, Pallas kernels for 5% -> 7%
where the time goes in v2:
time: 105 us
  starting transfers between devices  36.5 us (35%)
  waiting for transfers between devices  35.3 us (34%)
  blocking collectives  16.9 us (16%)
  Pallas kernels  11.7 us (11%)
  local copies, waits for them, and re-layouts  3.03 us (3%)
    all_to_all x2, waiting for transfers between devices, exchange(): lax.all_to_all(value, BOTH, 0, 0, tiled=True, axis_index_groups=groups_of...  23.2 us
    all_to_all x2, starting transfers between devices, exchange(): lax.all_to_all(value, BOTH, 0, 0, tiled=True, axis_index_groups=groups_of...  18.4 us
    all_to_all x1, blocking collectives, exchange(): lax.all_to_all(value, BOTH, 0, 0, tiled=True, axis_index_groups=groups_of...  16.9 us
    ppermute x6, starting transfers between devices, shifted(): lax.ppermute(value, axis, [(source, source + steps) for source in range(l...  15.3 us
    ppermute x6, waiting for transfers between devices, shifted(): lax.ppermute(value, axis, [(source, source + steps) for source in range(l...  9.78 us
    pallas_call x1, Pallas kernels, local(): call(weight_kernel, jax.ShapeDtypeStruct((256, 3456), jnp.bfloat16), flops)  3.9 us
    pallas_call x1, Pallas kernels, local(): call(forward_kernel, (block, block), flops)(ext, weight, cotangent)  2.9 us
    ppermute x3, starting transfers between devices, flip_core(): return lax.ppermute(value, 'tm', [(i, i ^ 1) for i in range(16)])  2.77 us
  transfers between devices with their start and end apart: 11, of which 8 were waited for; matrix products, arithmetic and copies ran while one was open for 1% of the time, Pallas kernels for 7%

profile of v2, /device:TPU:1, one launch (start us, length us, event | category | flops | bytes accessed | tf_op | source)
XLA Modules:
  0.0 104.6 jit_solution(2053404364766118383)
XLA Ops:
  0.6 0.0 copy-start.4
  0.6 4.7 %collective-permute-start = (bf16[2,2,128,256]{3,2,1,0:T(8,128)(2,1)}, bf16[2,2,128,256]{3,2,1,0:T(8,128)(2,1)S(1)}, u32[]{:S(2)}, u32[]{:S(2)}) collective-permute-start(bf16[2,2,128,256]{3,2,1,0:T(8,128)(2,1)} %param.4), channel_id=1, source_target_pairs={{0,16},{16,32},{32,48},{48,64},{64,80},{80,96},{96,112},{112,128},... | collective-permute-start | bytes 786440 | tf_op jit(solution)/shard_map/ppermute | solution.py:42
  5.4 1.0 fusion.1
  6.4 2.6 %collective-permute-done = bf16[2,2,128,256]{3,2,1,0:T(8,128)(2,1)S(1)} collective-permute-done((bf16[2,2,128,256]{3,2,1,0:T(8,128)(2,1)}, bf16[2,2,128,256]{3,2,1,0:T(8,128)(2,1)S(1)}, u32[]{:S(2)}, u32[]{:S(2)}) %collective-permute-start) | collective-permute-done | bytes 262176 | tf_op jit(solution)/shard_map/ppermute | solution.py:42
  9.0 3.6 %collective-permute-start.1 = (bf16[4,1,128,256]{3,2,1,0:T(8,128)(2,1)S(1)}, bf16[4,1,128,256]{3,2,1,0:T(8,128)(2,1)S(1)}, u32[]{:S(2)}, u32[]{:S(2)}) collective-permute-start(bf16[4,1,128,256]{3,2,1,0:T(8,128)(2,1)S(1)} %pad_maximum_fusion.2), channel_id=1, source_target_pairs={{0,1},{1,2},{2,3},{3,4},{4,5},{5,6},{6,7},{7,8},{8,9},{9,10},{10,1... | collective-permute-start | bytes 786440 | tf_op jit(solution)/shard_map/ppermute | solution.py:42
  12.6 1.3 %collective-permute-start.2 = (bf16[4,1,128,256]{3,2,1,0:T(8,128)(2,1)S(1)}, bf16[4,1,128,256]{3,2,1,0:T(8,128)(2,1)S(1)}, u32[]{:S(2)}, u32[]{:S(2)}) collective-permute-start(bf16[4,1,128,256]{3,2,1,0:T(8,128)(2,1)S(1)} %pad_maximum_fusion.3), channel_id=1, source_target_pairs={{1,0},{2,1},{3,2},{4,3},{5,4},{6,5},{7,6},{8,7},{9,8},{10,9},{11,1... | collective-permute-start | bytes 786440 | tf_op jit(solution)/shard_map/ppermute | solution.py:42
  14.0 0.0 copy-start
  14.0 0.0 copy-start.2
  14.0 1.9 %collective-permute-done.1 = bf16[4,1,128,256]{3,2,1,0:T(8,128)(2,1)S(1)} collective-permute-done((bf16[4,1,128,256]{3,2,1,0:T(8,128)(2,1)S(1)}, bf16[4,1,128,256]{3,2,1,0:T(8,128)(2,1)S(1)}, u32[]{:S(2)}, u32[]{:S(2)}) %collective-permute-start.1) | collective-permute-done | bytes 262176 | tf_op jit(solution)/shard_map/ppermute | solution.py:42
  15.9 4.0 %collective-permute-done.2 = bf16[4,1,128,256]{3,2,1,0:T(8,128)(2,1)S(1)} collective-permute-done((bf16[4,1,128,256]{3,2,1,0:T(8,128)(2,1)S(1)}, bf16[4,1,128,256]{3,2,1,0:T(8,128)(2,1)S(1)}, u32[]{:S(2)}, u32[]{:S(2)}) %collective-permute-start.2) | collective-permute-done | bytes 262176 | tf_op jit(solution)/shard_map/ppermute | solution.py:42
  19.9 0.0 copy-done.4
  19.9 0.1 pad_maximum_fusion.ext_ref
  20.1 0.1 broadcast_select_fusion
  20.1 0.0 copy-start.3
  20.2 0.1 collective-permute-start.4
  20.3 0.0 copy-done
  20.3 0.0 copy-done.2
  20.3 2.9 %shard_map.67 = (bf16[2,2,128,256]{3,2,1,0:T(8,128)(2,1)}, bf16[2,2,128,256]{3,2,1,0:T(8,128)(2,1)S(1)}) custom-call(bf16[4,4,128,256]{3,2,1,0:T(8,128)(2,1)S(1)} %pad_maximum_fusion.ext_ref, bf16[3,3,3,256,256]{4,3,2,1,0:T(8,128)(2,1)S(1)} %copy-done, bf16[2,2,128,256]{3,2,1,0:T(8,128)(2,1)S(1)} %copy-done.2), custom_call_target="tpu_custom_call" | custom-call | flops 1811939328 | bytes 5000000 | tf_op jit(solution)/shard_map/pallas_call | solution.py:196
  23.2 0.5 collective-permute-start.5
  23.7 1.2 %collective-permute-done.5.grad2_ref = bf16[2,2,128,256]{3,2,1,0:T(8,128)(2,1)S(1)} collective-permute-done((bf16[2,2,128,256]{3,2,1,0:T(8,128)(2,1)S(1)}, bf16[2,2,128,256]{3,2,1,0:T(8,128)(2,1)S(1)}, u32[]{:S(2)}, u32[]{:S(2)}) %collective-permute-start.5) | collective-permute-done | bytes 262176 | tf_op jit(solution)/shard_map/ppermute | solution.py:36
  24.8 0.0 collective-permute-done.4.theirs_ref
  24.8 0.0 copy-done.3
  24.8 3.9 %shard_map.68 = bf16[256,3456]{1,0:T(8,128)(2,1)} custom-call(bf16[4,4,128,128]{3,2,1,0:T(8,128)(2,1)S(1)} %get-tuple-element.28.mine_ref, bf16[4,4,128,128]{3,2,1,0:T(8,128)(2,1)S(1)} %collective-permute-done.4.theirs_ref, bf16[2,2,128,256]{3,2,1,0:T(8,128)(2,1)S(1)} %get-tuple-element.18.grad_ref.first_ref, ...), custom_call_target="tpu_custom_call" | custom-call | flops 1811939328 | bytes 5000000 | tf_op jit(solution)/shard_map/pallas_call | solution.py:200
  28.7 11.5 %all-to-all-start = ((bf16[16,16,3456]{2,1,0:T(8,128)(2,1)}), bf16[16,16,3456]{2,1,0:T(8,128)(2,1)S(1)}, u32[]{:S(2)}, u32[]{:S(2)}) async-start(bf16[16,16,3456]{2,1,0:T(8,128)(2,1)} %bitcast), calls=%async_computation | async-start | bytes 3538944 | tf_op jit(solution)/shard_map/all_to_all | solution.py:32
  40.2 2.3 %collective-permute-start.3 = (bf16[2,2,128,256]{3,2,1,0:T(8,128)(2,1)S(1)}, bf16[2,2,128,256]{3,2,1,0:T(8,128)(2,1)S(1)}, u32[]{:S(2)}, u32[]{:S(2)}) collective-permute-start(bf16[2,2,128,256]{3,2,1,0:T(8,128)(2,1)S(1)} %get-tuple-element.18.grad_ref.first_ref), channel_id=1, source_target_pairs={{16,0},{32,16},{48,32},{64,48},{80,64},{96,80},{112,96},{128,112},... | collective-permute-start | bytes 786440 | tf_op jit(solution)/shard_map/ppermute | solution.py:42
  42.6 20.5 %all-to-all-done.got_ref = bf16[16,16,3456]{2,1,0:T(8,128)(2,1)S(1)} async-done(((bf16[16,16,3456]{2,1,0:T(8,128)(2,1)}), bf16[16,16,3456]{2,1,0:T(8,128)(2,1)S(1)}, u32[]{:S(2)}, u32[]{:S(2)}) %all-to-all-start) | async-done | bytes 1769504 | tf_op jit(solution)/shard_map/all_to_all | solution.py:32
  63.1 0.5 shard_map.69
  63.6 1.2 %collective-permute-done.3.second_ref = bf16[2,2,128,256]{3,2,1,0:T(8,128)(2,1)S(1)} collective-permute-done((bf16[2,2,128,256]{3,2,1,0:T(8,128)(2,1)S(1)}, bf16[2,2,128,256]{3,2,1,0:T(8,128)(2,1)S(1)}, u32[]{:S(2)}, u32[]{:S(2)}) %collective-permute-start.3) | collective-permute-done | bytes 262176 | tf_op jit(solution)/shard_map/ppermute | solution.py:42
  64.9 2.1 %collective-permute-start.6 = (bf16[4,1,128,256]{3,2,1,0:T(8,128)(2,1)S(1)}, bf16[4,1,128,256]{3,2,1,0:T(8,128)(2,1)S(1)}, u32[]{:S(2)}, u32[]{:S(2)}) collective-permute-start(bf16[4,1,128,256]{3,2,1,0:T(8,128)(2,1)S(1)} %get-tuple-element.20), channel_id=1, source_target_pairs={{0,1},{1,2},{2,3},{3,4},{4,5},{5,6},{6,7},{7,8},{8,9},{9,10},{10,1... | collective-permute-start | bytes 786440 | tf_op jit(solution)/shard_map/ppermute | solution.py:42
  67.0 1.3 %collective-permute-start.7 = (bf16[4,1,128,256]{3,2,1,0:T(8,128)(2,1)S(1)}, bf16[4,1,128,256]{3,2,1,0:T(8,128)(2,1)S(1)}, u32[]{:S(2)}, u32[]{:S(2)}) collective-permute-start(bf16[4,1,128,256]{3,2,1,0:T(8,128)(2,1)S(1)} %get-tuple-element.21), channel_id=1, source_target_pairs={{1,0},{2,1},{3,2},{4,3},{5,4},{6,5},{7,6},{8,7},{9,8},{10,9},{11,1... | collective-permute-start | bytes 786440 | tf_op jit(solution)/shard_map/ppermute | solution.py:42
  68.3 16.9 %all_to_all.19.got_ref = bf16[8,2,3456]{2,1,0:T(2,128)(2,1)S(1)} all-to-all(bf16[8,2,3456]{2,1,0:T(2,128)(2,1)S(1)} %shard_map.69), channel_id=1, replica_groups={{0,1,2,3,4,5,6,7},{8,9,10,11,12,13,14,15},{16,17,18,19,20,21,22,23},{24..., dimensions={0} | all-to-all | bytes 221184 | tf_op jit(solution)/shard_map/all_to_all | solution.py:32
  85.2 0.7 shard_map.71
  85.9 0.0 collective-permute-done.6
  85.9 0.0 collective-permute-done.7
  85.9 0.1 pad_maximum_fusion.1.ext_ref
  86.1 6.9 %all-to-all-start.2 = ((f32[8,2,3456]{2,1,0:T(2,128)}), f32[8,2,3456]{2,1,0:T(2,128)S(1)}, u32[]{:S(2)}, u32[]{:S(2)}) async-start(f32[8,2,3456]{2,1,0:T(2,128)} %shard_map.71), calls=%async_computation.2 | async-start | bytes 442368 | tf_op jit(solution)/shard_map/all_to_all | solution.py:32
  93.0 0.0 copy-start.1
  93.0 2.0 %copy-done.1 = bf16[3,3,3,256,256]{4,3,2,1,0:T(8,128)(2,1)S(1)} copy-done((bf16[3,3,3,256,256]{4,3,2,1,0:T(8,128)(2,1)S(1)}, bf16[3,3,3,256,256]{4,3,2,1,0:T(8,128)(2,1)}, u32[]{:S(2)}) %copy-start.1) | copy-done | bytes 3538968
  95.0 2.7 %shard_map.72 = bf16[2,2,128,256]{3,2,1,0:T(8,128)(2,1)} custom-call(bf16[4,4,128,256]{3,2,1,0:T(8,128)(2,1)S(1)} %pad_maximum_fusion.1.ext_ref, bf16[3,3,3,256,256]{4,3,2,1,0:T(8,128)(2,1)S(1)} %copy-done.1, bf16[2,2,128,256]{3,2,1,0:T(8,128)(2,1)S(1)} %copy-done.2), custom_call_target="tpu_custom_call" | custom-call | flops 1811939328 | bytes 5000000 | tf_op jit(solution)/shard_map/pallas_call | solution.py:224
  97.7 2.7 %all-to-all-done.2.mine_ref = f32[8,2,3456]{2,1,0:T(2,128)S(1)} async-done(((f32[8,2,3456]{2,1,0:T(2,128)}), f32[8,2,3456]{2,1,0:T(2,128)S(1)}, u32[]{:S(2)}, u32[]{:S(2)}) %all-to-all-start.2) | async-done | bytes 221216 | tf_op jit(solution)/shard_map/all_to_all | solution.py:32
  100.4 2.2 %collective-permute-start.8 = (f32[8,2,3456]{2,1,0:T(2,128)S(1)}, f32[8,2,3456]{2,1,0:T(2,128)S(1)}, u32[]{:S(2)}, u32[]{:S(2)}) collective-permute-start(f32[8,2,3456]{2,1,0:T(2,128)S(1)} %all-to-all-done.2.mine_ref), channel_id=1, source_target_pairs={{0,16},{16,0},{32,48},{48,32},{64,80},{80,64},{96,112},{112,96},{1... | collective-permute-start | bytes 663560 | tf_op jit(solution)/shard_map/ppermute | solution.py:36
  102.6 1.1 %collective-permute-done.8.other_ref = f32[8,2,3456]{2,1,0:T(2,128)S(1)} collective-permute-done((f32[8,2,3456]{2,1,0:T(2,128)S(1)}, f32[8,2,3456]{2,1,0:T(2,128)S(1)}, u32[]{:S(2)}, u32[]{:S(2)}) %collective-permute-start.8) | collective-permute-done | bytes 221216 | tf_op jit(solution)/shard_map/ppermute | solution.py:36
  103.7 0.9 shard_map.73
  (4 shorter events, 0.1 us)
Async XLA Ops:
  0.6 19.3 %copy-start.4 = (bf16[2,2,128,256]{3,2,1,0:T(8,128)(2,1)S(1)}, bf16[2,2,128,256]{3,2,1,0:T(8,128)(2,1)}, u32[]{:S(2)}) copy-start(bf16[2,2,128,256]{3,2,1,0:T(8,128)(2,1)} %param.4) | copy-start | bytes 786436
  0.6 8.3 %collective-permute-start = (bf16[2,2,128,256]{3,2,1,0:T(8,128)(2,1)}, bf16[2,2,128,256]{3,2,1,0:T(8,128)(2,1)S(1)}, u32[]{:S(2)}, u32[]{:S(2)}) collective-permute-start(bf16[2,2,128,256]{3,2,1,0:T(8,128)(2,1)} %param.4), channel_id=1, source_target_pairs={{0,16},{16,32},{32,48},{48,64},{64,80},{80,96},{96,112},{112,128},... | collective-permute-start | bytes 786440 | tf_op jit(solution)/shard_map/ppermute | solution.py:42
  9.0 6.8 %collective-permute-start.1 = (bf16[4,1,128,256]{3,2,1,0:T(8,128)(2,1)S(1)}, bf16[4,1,128,256]{3,2,1,0:T(8,128)(2,1)S(1)}, u32[]{:S(2)}, u32[]{:S(2)}) collective-permute-start(bf16[4,1,128,256]{3,2,1,0:T(8,128)(2,1)S(1)} %pad_maximum_fusion.2), channel_id=1, source_target_pairs={{0,1},{1,2},{2,3},{3,4},{4,5},{5,6},{6,7},{7,8},{8,9},{9,10},{10,1... | collective-permute-start | bytes 786440 | tf_op jit(solution)/shard_map/ppermute | solution.py:42
  12.6 7.3 %collective-permute-start.2 = (bf16[4,1,128,256]{3,2,1,0:T(8,128)(2,1)S(1)}, bf16[4,1,128,256]{3,2,1,0:T(8,128)(2,1)S(1)}, u32[]{:S(2)}, u32[]{:S(2)}) collective-permute-start(bf16[4,1,128,256]{3,2,1,0:T(8,128)(2,1)S(1)} %pad_maximum_fusion.3), channel_id=1, source_target_pairs={{1,0},{2,1},{3,2},{4,3},{5,4},{6,5},{7,6},{8,7},{9,8},{10,9},{11,1... | collective-permute-start | bytes 786440 | tf_op jit(solution)/shard_map/ppermute | solution.py:42
  14.0 6.3 %copy-start = (bf16[3,3,3,256,256]{4,3,2,1,0:T(8,128)(2,1)S(1)}, bf16[3,3,3,256,256]{4,3,2,1,0:T(8,128)(2,1)}, u32[]{:S(2)}) copy-start(bf16[3,3,3,256,256]{4,3,2,1,0:T(8,128)(2,1)} %w_ref.3) | copy-start | bytes 10616836
  14.0 6.3 %copy-start.2 = (bf16[2,2,128,256]{3,2,1,0:T(8,128)(2,1)S(1)}, bf16[2,2,128,256]{3,2,1,0:T(8,128)(2,1)}, u32[]{:S(2)}) copy-start(bf16[2,2,128,256]{3,2,1,0:T(8,128)(2,1)} %cot_ref.3) | copy-start | bytes 786436
  20.1 4.7 %copy-start.3 = (bf16[256,256]{1,0:T(8,128)(2,1)S(1)}, bf16[256,256]{1,0:T(8,128)(2,1)}, u32[]{:S(2)}) copy-start(bf16[256,256]{1,0:T(8,128)(2,1)} %constant.21.clone.order_ref) | copy-start | bytes 393220
  20.2 4.7 %collective-permute-start.4 = (bf16[4,4,128,128]{3,2,1,0:T(8,128)(2,1)S(1)}, bf16[4,4,128,128]{3,2,1,0:T(8,128)(2,1)S(1)}, u32[]{:S(2)}, u32[]{:S(2)}) collective-permute-start(bf16[4,4,128,128]{3,2,1,0:T(8,128)(2,1)S(1)} %get-tuple-element.27), channel_id=1, source_target_pairs={{0,16},{16,0},{32,48},{48,32},{64,80},{80,64},{96,112},{112,96},{1... | collective-permute-start | bytes 1572872 | tf_op jit(solution)/shard_map/ppermute | solution.py:36
  23.2 1.6 %collective-permute-start.5 = (bf16[2,2,128,256]{3,2,1,0:T(8,128)(2,1)S(1)}, bf16[2,2,128,256]{3,2,1,0:T(8,128)(2,1)S(1)}, u32[]{:S(2)}, u32[]{:S(2)}) collective-permute-start(bf16[2,2,128,256]{3,2,1,0:T(8,128)(2,1)S(1)} %get-tuple-element.18.grad_ref.first_ref), channel_id=1, source_target_pairs={{0,16},{16,0},{32,48},{48,32},{64,80},{80,64},{96,112},{112,96},{1... | collective-permute-start | bytes 786440 | tf_op jit(solution)/shard_map/ppermute | solution.py:36
  28.7 34.4 %all-to-all-start = ((bf16[16,16,3456]{2,1,0:T(8,128)(2,1)}), bf16[16,16,3456]{2,1,0:T(8,128)(2,1)S(1)}, u32[]{:S(2)}, u32[]{:S(2)}) async-start(bf16[16,16,3456]{2,1,0:T(8,128)(2,1)} %bitcast), calls=%async_computation | async-start | bytes 3538944 | tf_op jit(solution)/shard_map/all_to_all | solution.py:32
  40.2 24.6 %collective-permute-start.3 = (bf16[2,2,128,256]{3,2,1,0:T(8,128)(2,1)S(1)}, bf16[2,2,128,256]{3,2,1,0:T(8,128)(2,1)S(1)}, u32[]{:S(2)}, u32[]{:S(2)}) collective-permute-start(bf16[2,2,128,256]{3,2,1,0:T(8,128)(2,1)S(1)} %get-tuple-element.18.grad_ref.first_ref), channel_id=1, source_target_pairs={{16,0},{32,16},{48,32},{64,48},{80,64},{96,80},{112,96},{128,112},... | collective-permute-start | bytes 786440 | tf_op jit(solution)/shard_map/ppermute | solution.py:42
  64.9 21.0 %collective-permute-start.6 = (bf16[4,1,128,256]{3,2,1,0:T(8,128)(2,1)S(1)}, bf16[4,1,128,256]{3,2,1,0:T(8,128)(2,1)S(1)}, u32[]{:S(2)}, u32[]{:S(2)}) collective-permute-start(bf16[4,1,128,256]{3,2,1,0:T(8,128)(2,1)S(1)} %get-tuple-element.20), channel_id=1, source_target_pairs={{0,1},{1,2},{2,3},{3,4},{4,5},{5,6},{6,7},{7,8},{8,9},{9,10},{10,1... | collective-permute-start | bytes 786440 | tf_op jit(solution)/shard_map/ppermute | solution.py:42
  67.0 19.0 %collective-permute-start.7 = (bf16[4,1,128,256]{3,2,1,0:T(8,128)(2,1)S(1)}, bf16[4,1,128,256]{3,2,1,0:T(8,128)(2,1)S(1)}, u32[]{:S(2)}, u32[]{:S(2)}) collective-permute-start(bf16[4,1,128,256]{3,2,1,0:T(8,128)(2,1)S(1)} %get-tuple-element.21), channel_id=1, source_target_pairs={{1,0},{2,1},{3,2},{4,3},{5,4},{6,5},{7,6},{8,7},{9,8},{10,9},{11,1... | collective-permute-start | bytes 786440 | tf_op jit(solution)/shard_map/ppermute | solution.py:42
  86.1 14.3 %all-to-all-start.2 = ((f32[8,2,3456]{2,1,0:T(2,128)}), f32[8,2,3456]{2,1,0:T(2,128)S(1)}, u32[]{:S(2)}, u32[]{:S(2)}) async-start(f32[8,2,3456]{2,1,0:T(2,128)} %shard_map.71), calls=%async_computation.2 | async-start | bytes 442368 | tf_op jit(solution)/shard_map/all_to_all | solution.py:32
  93.0 2.0 %copy-start.1 = (bf16[3,3,3,256,256]{4,3,2,1,0:T(8,128)(2,1)S(1)}, bf16[3,3,3,256,256]{4,3,2,1,0:T(8,128)(2,1)}, u32[]{:S(2)}) copy-start(bf16[3,3,3,256,256]{4,3,2,1,0:T(8,128)(2,1)} %w_ref.3) | copy-start | bytes 10616836
  100.4 3.3 %collective-permute-start.8 = (f32[8,2,3456]{2,1,0:T(2,128)S(1)}, f32[8,2,3456]{2,1,0:T(2,128)S(1)}, u32[]{:S(2)}, u32[]{:S(2)}) collective-permute-start(f32[8,2,3456]{2,1,0:T(2,128)S(1)} %all-to-all-done.2.mine_ref), channel_id=1, source_target_pairs={{0,16},{16,0},{32,48},{48,32},{64,80},{80,64},{96,112},{112,96},{1... | collective-permute-start | bytes 663560 | tf_op jit(solution)/shard_map/ppermute | solution.py:36

commit v3 on v2

--- a/solution.py
+++ b/solution.py
@@ -11,7 +11,7 @@
 from jax.sharding import PartitionSpec as P
 
 BOTH = ("tm", "space")
-VMEM = pltpu.CompilerParams(vmem_limit_bytes=48 * 1024 * 1024)
+VMEM = pltpu.CompilerParams(vmem_limit_bytes=20 * 1024 * 1024)
 SIZES = {"x_hi": 2, "y": 4, "core": 2, "x_lo": 2, "z": 8}
 
 
@@ -42,12 +42,6 @@
     return lax.ppermute(value, axis, [(source, source + steps) for source in range(leading, last)])
 
 
-def with_rows(first, second):
-    before = shifted(jnp.concatenate([first[:, -1:], second[:, -1:]], axis=0), "space", 1)
-    after = shifted(jnp.concatenate([first[:, :1], second[:, :1]], axis=0), "space", -1)
-    return jnp.concatenate([before, jnp.concatenate([first, second], axis=0), after], axis=1)
-
-
 def shift_cols(value, steps):
     zero = jnp.zeros_like(value[:, :1])
     if steps == 1:
@@ -59,23 +53,49 @@
     return ref[a : a + 2, b : b + 2].reshape(512, -1)
 
 
-def forward_kernel(ext_ref, w_ref, cot_ref, out_ref, grad_ref):
+def near_kernel(carried_ref, own_ref, w_ref, part_ref):
     sums = []
     for c in range(3):
-        acc = jnp.zeros((512, 256), jnp.float32)
+        both = jnp.zeros((512, 256), jnp.float32)
+        upper = jnp.zeros((256, 256), jnp.float32)
+        lower = jnp.zeros((256, 256), jnp.float32)
         for a in range(3):
-            for b in range(3):
-                acc += jnp.dot(
-                    block_of(ext_ref, a, b), w_ref[a, b, c], preferred_element_type=jnp.float32
-                )
-        sums.append(acc.reshape(4, 128, 256))
-    preact = shift_cols(sums[0], 1) + sums[1] + shift_cols(sums[2], -1)
-    own = ext_ref[2:4, 1:3].reshape(4, 128, 256).astype(jnp.float32)
-    sigma = 1.0 / (1.0 + jnp.exp(-preact))
-    out_ref[...] = (own + preact * sigma).astype(jnp.bfloat16).reshape(2, 2, 128, 256)
-    cot = cot_ref[...].reshape(4, 128, 256).astype(jnp.float32)
-    grad = cot * sigma * (1.0 + preact * (1.0 - sigma))
-    grad_ref[...] = grad.astype(jnp.bfloat16).reshape(2, 2, 128, 256)
+            if a == 0:
+                block = carried_ref[...]
+            elif a == 1:
+                block = jnp.concatenate([carried_ref[1:], own_ref[:1]], axis=0)
+            else:
+                block = own_ref[...]
+            rows = [block[:, r].reshape(256, 256) for r in range(2)]
+            both += jnp.dot(
+                jnp.concatenate(rows, axis=0), w_ref[a, 1, c], preferred_element_type=jnp.float32
+            )
+            upper += jnp.dot(rows[1], w_ref[a, 2, c], preferred_element_type=jnp.float32)
+            lower += jnp.dot(rows[0], w_ref[a, 0, c], preferred_element_type=jnp.float32)
+        sums.append((both + jnp.concatenate([upper, lower], axis=0)).reshape(4, 128, 256))
+    part_ref[...] = shift_cols(sums[0], 1) + sums[1] + shift_cols(sums[2], -1)
+
+
+def forward_kernel(before_ref, after_ref, own_ref, part_ref, w_ref, cot_ref, out_ref, grad_ref):
+    sums = []
+    for c in range(3):
+        upper = jnp.zeros((256, 256), jnp.float32)
+        lower = jnp.zeros((256, 256), jnp.float32)
+        for a in range(3):
+            top = before_ref[a : a + 2].reshape(256, 256)
+            bottom = after_ref[a : a + 2].reshape(256, 256)
+            upper += jnp.dot(top, w_ref[a, 0, c], preferred_element_type=jnp.float32)
+            lower += jnp.dot(bottom, w_ref[a, 2, c], preferred_element_type=jnp.float32)
+        sums.append(jnp.concatenate([upper, lower], axis=0).reshape(4, 128, 256))
+    total = part_ref[...] + shift_cols(sums[0], 1) + sums[1] + shift_cols(sums[2], -1)
+    for row in range(2):
+        preact = total[2 * row : 2 * row + 2]
+        own = own_ref[:, row].astype(jnp.float32)
+        sigma = 1.0 / (1.0 + jnp.exp(-preact))
+        out_ref[:, row] = (own + preact * sigma).astype(jnp.bfloat16)
+        cot = cot_ref[:, row].astype(jnp.float32)
+        grad = cot * sigma * (1.0 + preact * (1.0 - sigma))
+        grad_ref[:, row] = grad.astype(jnp.bfloat16)
 
 
 def backward_kernel(ext_ref, w_ref, cot_ref, out_ref):
@@ -96,47 +116,49 @@
     out_ref[...] = (cot + total).astype(jnp.bfloat16).reshape(2, 2, 128, 256)
 
 
-def weight_kernel(mine_ref, theirs_ref, grad_ref, grad2_ref, order_ref, out_ref):
-    order = order_ref[...]
-    flipped = []
+def turned_grad(grad_ref, order_ref):
+    parts = []
     for steps in (-1, 0, 1):
-        parts = []
-        for ref in (grad_ref, grad2_ref):
-            value = ref[...].reshape(4, 128, 256)
-            if steps:
-                value = shift_cols(value.astype(jnp.float32), steps).astype(jnp.bfloat16)
-            turned = lax.dot_general(
-                order,
-                value.reshape(512, 256),
-                (((1,), (1,)), ((), ())),
-                preferred_element_type=jnp.float32,
-            )
-            parts.append(turned.astype(jnp.bfloat16))
-        flipped.append(jnp.concatenate(parts, axis=1))
-    turned = jnp.concatenate(flipped, axis=0)
-    taps = [(a, b) for a in range(3) for b in range(3)]
+        value = grad_ref[...].reshape(4, 128, 256)
+        if steps:
+            value = shift_cols(value.astype(jnp.float32), steps).astype(jnp.bfloat16)
+        turned = lax.dot_general(
+            order_ref[...],
+            value.reshape(512, 256),
+            (((1,), (1,)), ((), ())),
+            preferred_element_type=jnp.float32,
+        )
+        parts.append(turned.astype(jnp.bfloat16))
+    return jnp.concatenate(parts, axis=0)
+
+
+TAPS = [(a, b) for a in range(3) for b in range(3)]
+
+
+def own_terms_kernel(cells_ref, grad_ref, order_ref, out_ref):
+    turned = turned_grad(grad_ref, order_ref)
     for start in range(0, 9, 2):
-        some = taps[start : start + 2]
-        cells = jnp.concatenate(
-            [
-                jnp.concatenate([block_of(mine_ref, a, b) for a, b in some], axis=1),
-                jnp.concatenate([block_of(theirs_ref, a, b) for a, b in some], axis=1),
-            ],
-            axis=0,
+        some = TAPS[start : start + 2]
+        cells = jnp.concatenate([block_of(cells_ref, a, b) for a, b in some], axis=1)
+        out_ref[:, start * 128 : (start + len(some)) * 128] = jnp.dot(
+            turned, cells, preferred_element_type=jnp.float32
         )
-        terms = jnp.dot(turned, cells, preferred_element_type=jnp.float32).astype(jnp.bfloat16)
+
+
+def terms_kernel(cells_ref, grad_ref, order_ref, part_ref, out_ref):
+    turned = turned_grad(grad_ref, order_ref)
+    for start in range(0, 9, 2):
+        some = TAPS[start : start + 2]
+        cells = jnp.concatenate([block_of(cells_ref, a, b) for a, b in some], axis=1)
+        terms = jnp.dot(turned, cells, preferred_element_type=jnp.float32)
+        terms += part_ref[:, start * 128 : (start + len(some)) * 128]
+        terms = terms.astype(jnp.bfloat16)
         for i in range(len(some)):
             for c in range(3):
                 tap = (start + i) * 3 + c
                 out_ref[:, tap * 128 : (tap + 1) * 128] = terms[
                     c * 256 : (c + 1) * 256, i * 128 : (i + 1) * 128
                 ]
-
-
-def edge_kernel(first_ref, second_ref, last_ref, leading_ref):
-    for i, ref in enumerate((first_ref, second_ref)):
-        last_ref[2 * i : 2 * i + 2] = ref[:, 1:]
-        leading_ref[2 * i : 2 * i + 2] = ref[:, :1]
 
 
 def plane_kernel(got_ref, out_ref):
@@ -189,18 +211,32 @@
     flops = 2 * 512 * 6912 * 256
 
     carried = shifted(frames_in, "tm", 1)
-    ext = with_rows(carried, frames_in)
+    before = shifted(jnp.concatenate([carried[:, 1:], frames_in[:, 1:]], axis=0), "space", 1)
+    after = shifted(jnp.concatenate([carried[:, :1], frames_in[:, :1]], axis=0), "space", -1)
+    part = jax.ShapeDtypeStruct((4, 128, 256), jnp.float32)
+    part = call(near_kernel, part, flops)(carried, frames_in, weight)
+    before, after, part = lax.optimization_barrier((before, after, part))
+    ext = jnp.concatenate(
+        [before, jnp.concatenate([carried, frames_in], axis=0), after], axis=1
+    )
     low, high = ext[..., :128], ext[..., 128:]
     mine = jnp.where(core == 0, low, high)
     theirs = flip_core(jnp.where(core == 0, high, low))
-    output, grad_pre = call(forward_kernel, (block, block), flops)(ext, weight, cotangent)
-
+    output, grad_pre = call(forward_kernel, (block, block), flops // 3)(
+        before, after, frames_in, part, weight, cotangent
+    )
     grad_other = flip_core(grad_pre)
     order = jnp.asarray(row_order(), jnp.bfloat16)
-    terms = call(weight_kernel, jax.ShapeDtypeStruct((256, 3456), jnp.bfloat16), flops)(
-        mine, theirs, grad_pre, grad_other, order
-    )
-    follow = shifted(grad_pre, "tm", -1)
+    own_terms = call(own_terms_kernel, jax.ShapeDtypeStruct((768, 1152), jnp.float32), flops // 2)(
+        mine, grad_pre, order
+    )
+    terms = call(terms_kernel, jax.ShapeDtypeStruct((256, 3456), jnp.bfloat16), flops // 2)(
+        theirs, grad_other, order, own_terms
+    )
+    above = shifted(grad_pre[:, 1:], "space", 1)
+    below = shifted(grad_pre[:, :1], "space", -1)
+    tall = jnp.concatenate([above, grad_pre, below], axis=1)
+    follow = shifted(tall, "tm", -1)
     got = exchange(terms, ("x_lo", "x_hi", "y")).reshape(16, 16, 3456)
     plane = pl.pallas_call(
         plane_kernel,
@@ -210,16 +246,10 @@
         out_specs=pl.BlockSpec((8, 2, 1152), lambda i: (0, 0, i)),
         compiler_params=VMEM,
     )(got)
-    held, follow, plane = lax.optimization_barrier((grad_pre, follow, plane))
-    edge = jax.ShapeDtypeStruct((4, 1, 128, 256), jnp.bfloat16)
-    last, leading = call(edge_kernel, (edge, edge), flops)(held, follow)
     got = exchange(plane, ("z",)).reshape(8, 2, 3456)
-    got, _, _ = lax.optimization_barrier((got, last, leading))
-    before = shifted(last, "space", 1)
-    after = shifted(leading, "space", -1)
-    grad_ext = jnp.concatenate([before, jnp.concatenate([held, follow], axis=0), after], axis=1)
     copies = call(line_kernel, jax.ShapeDtypeStruct((8, 2, 3456), jnp.float32), 100000)(got)
-    copies, grad_ext = lax.optimization_barrier((copies, grad_ext))
+    copies, tall, follow = lax.optimization_barrier((copies, tall, follow))
+    grad_ext = jnp.concatenate([tall, follow], axis=0)
     share = exchange(copies, ("x_hi", "y")).reshape(8, 2, 3456)
     grad_input = call(backward_kernel, block, flops)(grad_ext, weight, cotangent)
     share, grad_input = lax.optimization_barrier((share, grad_input))

time: 105 us -> 97 us (0.924)
  waiting for transfers between devices: 35.3 us -> 28.2 us
  blocking collectives: 16.9 us -> 10.2 us
  local copies, waits for them, and re-layouts: 3.03 us -> 6.09 us
  starting transfers between devices: 36.5 us -> 38.7 us
    all_to_all x1, blocking collectives: 16.9 us -> 10.2 us  [exchange(): lax.all_to_all(value, BOTH, 0, 0, tiled=True, axis_index_groups=groups_of...]
    all_to_all x2, waiting for transfers between devices: 23.2 us -> 17.9 us  [exchange(): lax.all_to_all(value, BOTH, 0, 0, tiled=True, axis_index_groups=groups_of...]
    unnamed x10 -> x16, local copies, waits for them, and re-layouts: 2.02 us -> 5.05 us
    ppermute x3, starting transfers between devices: 2.77 us -> 4.04 us  [flip_core(): return lax.ppermute(value, 'tm', [(i, i ^ 1) for i in range(16)])]
    ppermute x3, waiting for transfers between devices: 2.27 us -> 1.11 us  [flip_core(): return lax.ppermute(value, 'tm', [(i, i ^ 1) for i in range(16)])]
    pallas_call x3 -> x4, Pallas kernels: 6.83 us -> 7.23 us  [the longest x1 2.67 us: local(): call(terms_kernel, jax.ShapeDtypeStruct((256, 3456), jnp.bfloat16), flops...]
  transfers between devices with their start and end apart: 11 -> 11, of which waited for: 8 -> 7; matrix products, arithmetic and copies ran while one was open for 1% -> 1% of each run, Pallas kernels for 7% -> 9%
where the time goes in v3:
time: 97 us; the launch traced here: 96.4 us
  starting transfers between devices  38.7 us (40%)
  waiting for transfers between devices  28.2 us (29%)
  Pallas kernels  12.1 us (12%)
  blocking collectives  10.2 us (11%)
  local copies, waits for them, and re-layouts  6.09 us (6%)
    all_to_all x2, starting transfers between devices, exchange(): lax.all_to_all(value, BOTH, 0, 0, tiled=True, axis_index_groups=groups_of...  19 us
    all_to_all x2, waiting for transfers between devices, exchange(): lax.all_to_all(value, BOTH, 0, 0, tiled=True, axis_index_groups=groups_of...  17.9 us
    ppermute x6, starting transfers between devices, shifted(): lax.ppermute(value, axis, [(source, source + steps) for source in range(l...  15.6 us
    all_to_all x1, blocking collectives, exchange(): lax.all_to_all(value, BOTH, 0, 0, tiled=True, axis_index_groups=groups_of...  10.2 us
    ppermute x6, waiting for transfers between devices, shifted(): lax.ppermute(value, axis, [(source, source + steps) for source in range(l...  9.14 us
    unnamed x16, local copies, waits for them, and re-layouts  5.05 us
    ppermute x3, starting transfers between devices, flip_core(): return lax.ppermute(value, 'tm', [(i, i ^ 1) for i in range(16)])  4.04 us
    pallas_call x1, Pallas kernels, local(): call(backward_kernel, block, flops)(grad_ext, weight, cotangent)  2.73 us
  transfers between devices with their start and end apart: 11, of which 7 were waited for; matrix products, arithmetic and copies ran while one was open for 1% of the time, Pallas kernels for 9%

profile of v3, /device:TPU:1, one launch (start us, length us, event | category | flops | bytes accessed | tf_op | source)
XLA Modules:
  0.0 96.4 jit_solution(3578080570975027564)
XLA Ops:
  0.6 4.6 %collective-permute-start = (bf16[2,2,128,256]{3,2,1,0:T(8,128)(2,1)}, bf16[2,2,128,256]{3,2,1,0:T(8,128)(2,1)S(1)}, u32[]{:S(2)}, u32[]{:S(2)}) collective-permute-start(bf16[2,2,128,256]{3,2,1,0:T(8,128)(2,1)} %own_ref.3), channel_id=1, source_target_pairs={{0,16},{16,32},{32,48},{48,64},{64,80},{80,96},{96,112},{112,128},... | collective-permute-start | bytes 786440 | tf_op jit(solution)/shard_map/ppermute | solution.py:42
  5.2 1.0 %fusion.2 = (bf16[2,1,128,256]{3,2,1,0:T(8,128)(2,1)S(1)}, bf16[2,1,128,256]{3,2,1,0:T(8,128)(2,1)S(1)}) fusion(bf16[2,2,128,256]{3,2,1,0:T(8,128)(2,1)} %own_ref.3), kind=kLoop, calls=%fused_computation.11 | loop fusion | bytes 524288 | tf_op jit(solution)/shard_map/slice | solution.py:215
  6.2 2.6 %collective-permute-done.carried_ref = bf16[2,2,128,256]{3,2,1,0:T(8,128)(2,1)S(1)} collective-permute-done((bf16[2,2,128,256]{3,2,1,0:T(8,128)(2,1)}, bf16[2,2,128,256]{3,2,1,0:T(8,128)(2,1)S(1)}, u32[]{:S(2)}, u32[]{:S(2)}) %collective-permute-start) | collective-permute-done | bytes 262176 | tf_op jit(solution)/shard_map/ppermute | solution.py:42
  8.9 3.6 %collective-permute-start.1 = (bf16[4,1,128,256]{3,2,1,0:T(8,128)(2,1)S(1)}, bf16[4,1,128,256]{3,2,1,0:T(8,128)(2,1)S(1)}, u32[]{:S(2)}, u32[]{:S(2)}) collective-permute-start(bf16[4,1,128,256]{3,2,1,0:T(8,128)(2,1)S(1)} %pad_maximum_fusion.2), channel_id=1, source_target_pairs={{0,1},{1,2},{2,3},{3,4},{4,5},{5,6},{6,7},{7,8},{8,9},{9,10},{10,1... | collective-permute-start | bytes 786440 | tf_op jit(solution)/shard_map/ppermute | solution.py:42
  12.5 0.0 copy-start.4
  12.5 1.4 %collective-permute-start.2 = (bf16[4,1,128,256]{3,2,1,0:T(8,128)(2,1)S(1)}, bf16[4,1,128,256]{3,2,1,0:T(8,128)(2,1)S(1)}, u32[]{:S(2)}, u32[]{:S(2)}) collective-permute-start(bf16[4,1,128,256]{3,2,1,0:T(8,128)(2,1)S(1)} %pad_maximum_fusion.3), channel_id=1, source_target_pairs={{1,0},{2,1},{3,2},{4,3},{5,4},{6,5},{7,6},{8,7},{9,8},{10,9},{11,1... | collective-permute-start | bytes 786440 | tf_op jit(solution)/shard_map/ppermute | solution.py:42
  14.0 0.0 copy-start
  14.0 2.0 %copy-done = bf16[3,3,3,256,256]{4,3,2,1,0:T(8,128)(2,1)S(1)} copy-done((bf16[3,3,3,256,256]{4,3,2,1,0:T(8,128)(2,1)S(1)}, bf16[3,3,3,256,256]{4,3,2,1,0:T(8,128)(2,1)}, u32[]{:S(2)}) %copy-start) | copy-done | bytes 3538968
  16.0 0.9 copy-done.3
  16.9 1.4 %shard_map.67.part_ref = f32[4,128,256]{2,1,0:T(8,128)S(1)} custom-call(bf16[2,2,128,256]{3,2,1,0:T(8,128)(2,1)S(1)} %collective-permute-done.carried_ref, bf16[2,2,128,256]{3,2,1,0:T(8,128)(2,1)S(1)} %copy-done.3, bf16[3,3,3,256,256]{4,3,2,1,0:T(8,128)(2,1)S(1)} %copy-done), custom_call_target="tpu_custom_call" | custom-call | flops 1811939328 | bytes 5000000 | tf_op jit(solution)/shard_map/pallas_call | solution.py:217
  18.3 0.0 copy-start.1
  18.3 0.0 copy-start.6
  18.3 0.0 collective-permute-done.1.before_ref
  18.3 1.6 %collective-permute-done.2.after_ref = bf16[4,1,128,256]{3,2,1,0:T(8,128)(2,1)S(1)} collective-permute-done((bf16[4,1,128,256]{3,2,1,0:T(8,128)(2,1)S(1)}, bf16[4,1,128,256]{3,2,1,0:T(8,128)(2,1)S(1)}, u32[]{:S(2)}, u32[]{:S(2)}) %collective-permute-start.2) | collective-permute-done | bytes 262176 | tf_op jit(solution)/shard_map/ppermute | solution.py:42
  19.9 0.0 copy-done.4
  19.9 0.1 pad_maximum_fusion
  20.1 0.0 copy-start.5
  20.1 0.1 broadcast_select_fusion
  20.2 0.1 collective-permute-start.3
  20.3 0.0 copy-done.1
  20.3 0.0 copy-done.6
  20.3 1.7 %shard_map.68 = (bf16[2,2,128,256]{3,2,1,0:T(8,128)(2,1)}, bf16[2,2,128,256]{3,2,1,0:T(8,128)(2,1)S(1)}) custom-call(bf16[4,1,128,256]{3,2,1,0:T(8,128)(2,1)S(1)} %collective-permute-done.1.before_ref, bf16[4,1,128,256]{3,2,1,0:T(8,128)(2,1)S(1)} %collective-permute-done.2.after_ref, bf16[2,2,128,256]{3,2,1,0:T(8,128)(2,1)S(1)} %copy-done.4, ...), custom_call_target="tpu_custom_call" | custom-call | flops 603979776 | bytes 5000000 | tf_op jit(solution)/shard_map/pallas_call | solution.py:225
  22.1 0.4 collective-permute-start.4
  22.5 0.0 copy-done.5
  22.5 1.4 %shard_map.69.part_ref = f32[768,1152]{1,0:T(8,128)S(1)} custom-call(bf16[4,4,128,128]{3,2,1,0:T(8,128)(2,1)S(1)} %get-tuple-element.23.cells_ref, bf16[2,2,128,256]{3,2,1,0:T(8,128)(2,1)S(1)} %get-tuple-element.17.grad_ref, bf16[256,256]{1,0:T(8,128)(2,1)S(1)} %copy-done.5), custom_call_target="tpu_custom_call" | custom-call | flops 905969664 | bytes 5000000 | tf_op jit(solution)/shard_map/pallas_call | solution.py:230
  24.0 0.0 collective-permute-done.4.grad_ref
  24.0 0.0 collective-permute-done.3.cells_ref
  24.0 2.7 %shard_map.70 = bf16[256,3456]{1,0:T(8,128)(2,1)} custom-call(bf16[4,4,128,128]{3,2,1,0:T(8,128)(2,1)S(1)} %collective-permute-done.3.cells_ref, bf16[2,2,128,256]{3,2,1,0:T(8,128)(2,1)S(1)} %collective-permute-done.4.grad_ref, bf16[256,256]{1,0:T(8,128)(2,1)S(1)} %copy-done.5, f32[768,1152]{1,0:T(8,128)S(1)} %shard_map.69.part_ref), custom_call_target="tpu_custom_call" | custom-call | flops 905969664 | bytes 5000000 | tf_op jit(solution)/shard_map/pallas_call | solution.py:233
  26.6 13.3 %all-to-all-start = ((bf16[16,16,3456]{2,1,0:T(8,128)(2,1)}), bf16[16,16,3456]{2,1,0:T(8,128)(2,1)S(1)}, u32[]{:S(2)}, u32[]{:S(2)}) async-start(bf16[16,16,3456]{2,1,0:T(8,128)(2,1)} %bitcast), calls=%async_computation | async-start | bytes 3538944 | tf_op jit(solution)/shard_map/all_to_all | solution.py:32
  40.0 1.3 %collective-permute-start.5 = (bf16[2,1,128,256]{3,2,1,0:T(8,128)(2,1)S(1)}, bf16[2,1,128,256]{3,2,1,0:T(8,128)(2,1)S(1)}, u32[]{:S(2)}, u32[]{:S(2)}) collective-permute-start(bf16[2,1,128,256]{3,2,1,0:T(8,128)(2,1)S(1)} %get-tuple-element.26), channel_id=1, source_target_pairs={{0,1},{1,2},{2,3},{3,4},{4,5},{5,6},{6,7},{7,8},{8,9},{9,10},{10,1... | collective-permute-start | bytes 393224 | tf_op jit(solution)/shard_map/ppermute | solution.py:42
  41.3 1.3 %collective-permute-start.6 = (bf16[2,1,128,256]{3,2,1,0:T(8,128)(2,1)S(1)}, bf16[2,1,128,256]{3,2,1,0:T(8,128)(2,1)S(1)}, u32[]{:S(2)}, u32[]{:S(2)}) collective-permute-start(bf16[2,1,128,256]{3,2,1,0:T(8,128)(2,1)S(1)} %get-tuple-element.25), channel_id=1, source_target_pairs={{1,0},{2,1},{3,2},{4,3},{5,4},{6,5},{7,6},{8,7},{9,8},{10,9},{11,1... | collective-permute-start | bytes 393224 | tf_op jit(solution)/shard_map/ppermute | solution.py:42
  42.6 1.5 %collective-permute-done.5 = bf16[2,1,128,256]{3,2,1,0:T(8,128)(2,1)S(1)} collective-permute-done((bf16[2,1,128,256]{3,2,1,0:T(8,128)(2,1)S(1)}, bf16[2,1,128,256]{3,2,1,0:T(8,128)(2,1)S(1)}, u32[]{:S(2)}, u32[]{:S(2)}) %collective-permute-start.5) | collective-permute-done | bytes 131104 | tf_op jit(solution)/shard_map/ppermute | solution.py:42
  44.2 3.4 %collective-permute-done.6 = bf16[2,1,128,256]{3,2,1,0:T(8,128)(2,1)S(1)} collective-permute-done((bf16[2,1,128,256]{3,2,1,0:T(8,128)(2,1)S(1)}, bf16[2,1,128,256]{3,2,1,0:T(8,128)(2,1)S(1)}, u32[]{:S(2)}, u32[]{:S(2)}) %collective-permute-start.6) | collective-permute-done | bytes 131104 | tf_op jit(solution)/shard_map/ppermute | solution.py:42
  47.6 3.4 %collective-permute-start.7 = (bf16[2,4,128,256]{3,2,1,0:T(8,128)(2,1)S(1)}, bf16[2,4,128,256]{3,2,1,0:T(8,128)(2,1)S(1)}, u32[]{:S(2)}, u32[]{:S(2)}) collective-permute-start(bf16[2,4,128,256]{3,2,1,0:T(8,128)(2,1)S(1)} %constant_dynamic-update-slice_fusion), channel_id=1, source_target_pairs={{16,0},{32,16},{48,32},{64,48},{80,64},{96,80},{112,96},{128,112},... | collective-permute-start | bytes 1572872 | tf_op jit(solution)/shard_map/ppermute | solution.py:42
  51.1 15.2 %all-to-all-done.got_ref = bf16[16,16,3456]{2,1,0:T(8,128)(2,1)S(1)} async-done(((bf16[16,16,3456]{2,1,0:T(8,128)(2,1)}), bf16[16,16,3456]{2,1,0:T(8,128)(2,1)S(1)}, u32[]{:S(2)}, u32[]{:S(2)}) %all-to-all-start) | async-done | bytes 1769504 | tf_op jit(solution)/shard_map/all_to_all | solution.py:32
  66.3 0.5 shard_map.71
  66.8 10.2 %all_to_all.19.got_ref = bf16[8,2,3456]{2,1,0:T(2,128)(2,1)S(1)} all-to-all(bf16[8,2,3456]{2,1,0:T(2,128)(2,1)S(1)} %shard_map.71), channel_id=1, replica_groups={{0,1,2,3,4,5,6,7},{8,9,10,11,12,13,14,15},{16,17,18,19,20,21,22,23},{24..., dimensions={0} | all-to-all | bytes 221184 | tf_op jit(solution)/shard_map/all_to_all | solution.py:32
  77.0 0.7 shard_map.72
  77.7 0.0 collective-permute-done.7
  77.7 5.7 %all-to-all-start.2 = ((f32[8,2,3456]{2,1,0:T(2,128)}), f32[8,2,3456]{2,1,0:T(2,128)S(1)}, u32[]{:S(2)}, u32[]{:S(2)}) async-start(f32[8,2,3456]{2,1,0:T(2,128)} %shard_map.72), calls=%async_computation.2 | async-start | bytes 442368 | tf_op jit(solution)/shard_map/all_to_all | solution.py:32
  83.4 0.1 pad_maximum_fusion.1.ext_ref
  83.5 0.0 copy-start.2
  83.5 2.0 %copy-done.2 = bf16[3,3,3,256,256]{4,3,2,1,0:T(8,128)(2,1)S(1)} copy-done((bf16[3,3,3,256,256]{4,3,2,1,0:T(8,128)(2,1)S(1)}, bf16[3,3,3,256,256]{4,3,2,1,0:T(8,128)(2,1)}, u32[]{:S(2)}) %copy-start.2) | copy-done | bytes 3538968
  85.5 2.7 %shard_map.73 = bf16[2,2,128,256]{3,2,1,0:T(8,128)(2,1)} custom-call(bf16[4,4,128,256]{3,2,1,0:T(8,128)(2,1)S(1)} %pad_maximum_fusion.1.ext_ref, bf16[3,3,3,256,256]{4,3,2,1,0:T(8,128)(2,1)S(1)} %copy-done.2, bf16[2,2,128,256]{3,2,1,0:T(8,128)(2,1)S(1)} %copy-done.6), custom_call_target="tpu_custom_call" | custom-call | flops 1811939328 | bytes 5000000 | tf_op jit(solution)/shard_map/pallas_call | solution.py:254
  88.2 2.7 %all-to-all-done.2.mine_ref = f32[8,2,3456]{2,1,0:T(2,128)S(1)} async-done(((f32[8,2,3456]{2,1,0:T(2,128)}), f32[8,2,3456]{2,1,0:T(2,128)S(1)}, u32[]{:S(2)}, u32[]{:S(2)}) %all-to-all-start.2) | async-done | bytes 221216 | tf_op jit(solution)/shard_map/all_to_all | solution.py:32
  90.9 3.5 %collective-permute-start.8 = (f32[8,2,3456]{2,1,0:T(2,128)S(1)}, f32[8,2,3456]{2,1,0:T(2,128)S(1)}, u32[]{:S(2)}, u32[]{:S(2)}) collective-permute-start(f32[8,2,3456]{2,1,0:T(2,128)S(1)} %all-to-all-done.2.mine_ref), channel_id=1, source_target_pairs={{0,16},{16,0},{32,48},{48,32},{64,80},{80,64},{96,112},{112,96},{1... | collective-permute-start | bytes 663560 | tf_op jit(solution)/shard_map/ppermute | solution.py:36
  94.4 1.1 %collective-permute-done.8.other_ref = f32[8,2,3456]{2,1,0:T(2,128)S(1)} collective-permute-done((f32[8,2,3456]{2,1,0:T(2,128)S(1)}, f32[8,2,3456]{2,1,0:T(2,128)S(1)}, u32[]{:S(2)}, u32[]{:S(2)}) %collective-permute-start.8) | collective-permute-done | bytes 221216 | tf_op jit(solution)/shard_map/ppermute | solution.py:36
  95.5 0.9 shard_map.74
  (8 shorter events, 0.1 us)
Async XLA Ops:
  0.6 8.2 %collective-permute-start = (bf16[2,2,128,256]{3,2,1,0:T(8,128)(2,1)}, bf16[2,2,128,256]{3,2,1,0:T(8,128)(2,1)S(1)}, u32[]{:S(2)}, u32[]{:S(2)}) collective-permute-start(bf16[2,2,128,256]{3,2,1,0:T(8,128)(2,1)} %own_ref.3), channel_id=1, source_target_pairs={{0,16},{16,32},{32,48},{48,64},{64,80},{80,96},{96,112},{112,128},... | collective-permute-start | bytes 786440 | tf_op jit(solution)/shard_map/ppermute | solution.py:42
  8.9 9.4 %collective-permute-start.1 = (bf16[4,1,128,256]{3,2,1,0:T(8,128)(2,1)S(1)}, bf16[4,1,128,256]{3,2,1,0:T(8,128)(2,1)S(1)}, u32[]{:S(2)}, u32[]{:S(2)}) collective-permute-start(bf16[4,1,128,256]{3,2,1,0:T(8,128)(2,1)S(1)} %pad_maximum_fusion.2), channel_id=1, source_target_pairs={{0,1},{1,2},{2,3},{3,4},{4,5},{5,6},{6,7},{7,8},{8,9},{9,10},{10,1... | collective-permute-start | bytes 786440 | tf_op jit(solution)/shard_map/ppermute | solution.py:42
  12.5 7.5 %copy-start.4 = (bf16[2,2,128,256]{3,2,1,0:T(8,128)(2,1)S(1)}, bf16[2,2,128,256]{3,2,1,0:T(8,128)(2,1)}, u32[]{:S(2)}) copy-start(bf16[2,2,128,256]{3,2,1,0:T(8,128)(2,1)} %own_ref.3) | copy-start | bytes 786436
  12.5 7.4 %collective-permute-start.2 = (bf16[4,1,128,256]{3,2,1,0:T(8,128)(2,1)S(1)}, bf16[4,1,128,256]{3,2,1,0:T(8,128)(2,1)S(1)}, u32[]{:S(2)}, u32[]{:S(2)}) collective-permute-start(bf16[4,1,128,256]{3,2,1,0:T(8,128)(2,1)S(1)} %pad_maximum_fusion.3), channel_id=1, source_target_pairs={{1,0},{2,1},{3,2},{4,3},{5,4},{6,5},{7,6},{8,7},{9,8},{10,9},{11,1... | collective-permute-start | bytes 786440 | tf_op jit(solution)/shard_map/ppermute | solution.py:42
  14.0 2.0 %copy-start = (bf16[3,3,3,256,256]{4,3,2,1,0:T(8,128)(2,1)S(1)}, bf16[3,3,3,256,256]{4,3,2,1,0:T(8,128)(2,1)}, u32[]{:S(2)}) copy-start(bf16[3,3,3,256,256]{4,3,2,1,0:T(8,128)(2,1)} %w_ref.5) | copy-start | bytes 10616836
  16.0 0.9 copy-start.3
  18.3 2.0 %copy-start.1 = (bf16[3,3,3,256,256]{4,3,2,1,0:T(8,128)(2,1)S(1)}, bf16[3,3,3,256,256]{4,3,2,1,0:T(8,128)(2,1)}, u32[]{:S(2)}) copy-start(bf16[3,3,3,256,256]{4,3,2,1,0:T(8,128)(2,1)} %w_ref.5) | copy-start | bytes 10616836
  18.3 2.0 %copy-start.6 = (bf16[2,2,128,256]{3,2,1,0:T(8,128)(2,1)S(1)}, bf16[2,2,128,256]{3,2,1,0:T(8,128)(2,1)}, u32[]{:S(2)}) copy-start(bf16[2,2,128,256]{3,2,1,0:T(8,128)(2,1)} %cot_ref.3) | copy-start | bytes 786436
  20.1 2.4 %copy-start.5 = (bf16[256,256]{1,0:T(8,128)(2,1)S(1)}, bf16[256,256]{1,0:T(8,128)(2,1)}, u32[]{:S(2)}) copy-start(bf16[256,256]{1,0:T(8,128)(2,1)} %constant.21.clone.order_ref) | copy-start | bytes 393220
  20.2 3.8 %collective-permute-start.3 = (bf16[4,4,128,128]{3,2,1,0:T(8,128)(2,1)S(1)}, bf16[4,4,128,128]{3,2,1,0:T(8,128)(2,1)S(1)}, u32[]{:S(2)}, u32[]{:S(2)}) collective-permute-start(bf16[4,4,128,128]{3,2,1,0:T(8,128)(2,1)S(1)} %get-tuple-element.24), channel_id=1, source_target_pairs={{0,16},{16,0},{32,48},{48,32},{64,80},{80,64},{96,112},{112,96},{1... | collective-permute-start | bytes 1572872 | tf_op jit(solution)/shard_map/ppermute | solution.py:36
  22.1 1.9 %collective-permute-start.4 = (bf16[2,2,128,256]{3,2,1,0:T(8,128)(2,1)S(1)}, bf16[2,2,128,256]{3,2,1,0:T(8,128)(2,1)S(1)}, u32[]{:S(2)}, u32[]{:S(2)}) collective-permute-start(bf16[2,2,128,256]{3,2,1,0:T(8,128)(2,1)S(1)} %get-tuple-element.17.grad_ref), channel_id=1, source_target_pairs={{0,16},{16,0},{32,48},{48,32},{64,80},{80,64},{96,112},{112,96},{1... | collective-permute-start | bytes 786440 | tf_op jit(solution)/shard_map/ppermute | solution.py:36
  26.6 39.7 %all-to-all-start = ((bf16[16,16,3456]{2,1,0:T(8,128)(2,1)}), bf16[16,16,3456]{2,1,0:T(8,128)(2,1)S(1)}, u32[]{:S(2)}, u32[]{:S(2)}) async-start(bf16[16,16,3456]{2,1,0:T(8,128)(2,1)} %bitcast), calls=%async_computation | async-start | bytes 3538944 | tf_op jit(solution)/shard_map/all_to_all | solution.py:32
  40.0 4.1 %collective-permute-start.5 = (bf16[2,1,128,256]{3,2,1,0:T(8,128)(2,1)S(1)}, bf16[2,1,128,256]{3,2,1,0:T(8,128)(2,1)S(1)}, u32[]{:S(2)}, u32[]{:S(2)}) collective-permute-start(bf16[2,1,128,256]{3,2,1,0:T(8,128)(2,1)S(1)} %get-tuple-element.26), channel_id=1, source_target_pairs={{0,1},{1,2},{2,3},{3,4},{4,5},{5,6},{6,7},{7,8},{8,9},{9,10},{10,1... | collective-permute-start | bytes 393224 | tf_op jit(solution)/shard_map/ppermute | solution.py:42
  41.3 6.3 %collective-permute-start.6 = (bf16[2,1,128,256]{3,2,1,0:T(8,128)(2,1)S(1)}, bf16[2,1,128,256]{3,2,1,0:T(8,128)(2,1)S(1)}, u32[]{:S(2)}, u32[]{:S(2)}) collective-permute-start(bf16[2,1,128,256]{3,2,1,0:T(8,128)(2,1)S(1)} %get-tuple-element.25), channel_id=1, source_target_pairs={{1,0},{2,1},{3,2},{4,3},{5,4},{6,5},{7,6},{8,7},{9,8},{10,9},{11,1... | collective-permute-start | bytes 393224 | tf_op jit(solution)/shard_map/ppermute | solution.py:42
  47.6 30.1 %collective-permute-start.7 = (bf16[2,4,128,256]{3,2,1,0:T(8,128)(2,1)S(1)}, bf16[2,4,128,256]{3,2,1,0:T(8,128)(2,1)S(1)}, u32[]{:S(2)}, u32[]{:S(2)}) collective-permute-start(bf16[2,4,128,256]{3,2,1,0:T(8,128)(2,1)S(1)} %constant_dynamic-update-slice_fusion), channel_id=1, source_target_pairs={{16,0},{32,16},{48,32},{64,48},{80,64},{96,80},{112,96},{128,112},... | collective-permute-start | bytes 1572872 | tf_op jit(solution)/shard_map/ppermute | solution.py:42
  77.7 13.2 %all-to-all-start.2 = ((f32[8,2,3456]{2,1,0:T(2,128)}), f32[8,2,3456]{2,1,0:T(2,128)S(1)}, u32[]{:S(2)}, u32[]{:S(2)}) async-start(f32[8,2,3456]{2,1,0:T(2,128)} %shard_map.72), calls=%async_computation.2 | async-start | bytes 442368 | tf_op jit(solution)/shard_map/all_to_all | solution.py:32
  83.5 2.0 %copy-start.2 = (bf16[3,3,3,256,256]{4,3,2,1,0:T(8,128)(2,1)S(1)}, bf16[3,3,3,256,256]{4,3,2,1,0:T(8,128)(2,1)}, u32[]{:S(2)}) copy-start(bf16[3,3,3,256,256]{4,3,2,1,0:T(8,128)(2,1)} %w_ref.5) | copy-start | bytes 10616836
  90.9 4.6 %collective-permute-start.8 = (f32[8,2,3456]{2,1,0:T(2,128)S(1)}, f32[8,2,3456]{2,1,0:T(2,128)S(1)}, u32[]{:S(2)}, u32[]{:S(2)}) collective-permute-start(f32[8,2,3456]{2,1,0:T(2,128)S(1)} %all-to-all-done.2.mine_ref), channel_id=1, source_target_pairs={{0,16},{16,0},{32,48},{48,32},{64,80},{80,64},{96,112},{112,96},{1... | collective-permute-start | bytes 663560 | tf_op jit(solution)/shard_map/ppermute | solution.py:36

commit v4 on v3

--- a/solution.py
+++ b/solution.py
@@ -40,6 +40,18 @@
     count = lax.axis_size(axis)
     leading, last = (max(0, -steps), min(count, count - steps))
     return lax.ppermute(value, axis, [(source, source + steps) for source in range(leading, last)])
+
+
+def pairs(value, first):
+    links = [(i, i + 1) for i in range(first, 15, 2)]
+    return lax.ppermute(value, "space", links + [(j, i) for i, j in links])
+
+
+def row_halo(top, bottom):
+    even = lax.axis_index("space") % 2 == 0
+    near = pairs(jnp.where(even, bottom, top), 0)
+    far = pairs(jnp.where(even, top, bottom), 1)
+    return near, far
 
 
 def shift_cols(value, steps):
@@ -145,8 +157,9 @@
         )
 
 
-def terms_kernel(cells_ref, grad_ref, order_ref, part_ref, out_ref):
+def terms_kernel(cells_ref, grad_ref, order_ref, part_ref, out_ref, held_ref, sems):
     turned = turned_grad(grad_ref, order_ref)
+    copies = []
     for start in range(0, 9, 2):
         some = TAPS[start : start + 2]
         cells = jnp.concatenate([block_of(cells_ref, a, b) for a, b in some], axis=1)
@@ -156,9 +169,17 @@
         for i in range(len(some)):
             for c in range(3):
                 tap = (start + i) * 3 + c
-                out_ref[:, tap * 128 : (tap + 1) * 128] = terms[
+                held_ref[:, tap * 128 : (tap + 1) * 128] = terms[
                     c * 256 : (c + 1) * 256, i * 128 : (i + 1) * 128
                 ]
+        lanes = pl.ds(start * 384, len(some) * 384)
+        copy = pltpu.make_async_copy(
+            held_ref.at[:, lanes], out_ref.at[:, lanes], sems.at[start // 2]
+        )
+        copy.start()
+        copies.append(copy)
+    for copy in copies:
+        copy.wait()
 
 
 def plane_kernel(got_ref, out_ref):
@@ -211,11 +232,15 @@
     flops = 2 * 512 * 6912 * 256
 
     carried = shifted(frames_in, "tm", 1)
-    before = shifted(jnp.concatenate([carried[:, 1:], frames_in[:, 1:]], axis=0), "space", 1)
-    after = shifted(jnp.concatenate([carried[:, :1], frames_in[:, :1]], axis=0), "space", -1)
+    even = lax.axis_index("space") % 2 == 0
+    near, far = row_halo(
+        jnp.concatenate([carried[:, :1], frames_in[:, :1]], axis=0),
+        jnp.concatenate([carried[:, 1:], frames_in[:, 1:]], axis=0),
+    )
     part = jax.ShapeDtypeStruct((4, 128, 256), jnp.float32)
     part = call(near_kernel, part, flops)(carried, frames_in, weight)
-    before, after, part = lax.optimization_barrier((before, after, part))
+    near, far, part = lax.optimization_barrier((near, far, part))
+    before, after = jnp.where(even, far, near), jnp.where(even, near, far)
     ext = jnp.concatenate(
         [before, jnp.concatenate([carried, frames_in], axis=0), after], axis=1
     )
@@ -230,11 +255,16 @@
     own_terms = call(own_terms_kernel, jax.ShapeDtypeStruct((768, 1152), jnp.float32), flops // 2)(
         mine, grad_pre, order
     )
-    terms = call(terms_kernel, jax.ShapeDtypeStruct((256, 3456), jnp.bfloat16), flops // 2)(
-        theirs, grad_other, order, own_terms
-    )
-    above = shifted(grad_pre[:, 1:], "space", 1)
-    below = shifted(grad_pre[:, :1], "space", -1)
+    terms = pl.pallas_call(
+        terms_kernel,
+        out_shape=jax.ShapeDtypeStruct((256, 3456), jnp.bfloat16),
+        out_specs=pl.BlockSpec(memory_space=pl.ANY),
+        scratch_shapes=[pltpu.VMEM((256, 3456), jnp.bfloat16), pltpu.SemaphoreType.DMA((5,))],
+        compiler_params=VMEM,
+        cost_estimate=pl.CostEstimate(flops=flops // 2, bytes_accessed=5000000, transcendentals=0),
+    )(theirs, grad_other, order, own_terms)
+    near, far = row_halo(grad_pre[:, :1], grad_pre[:, 1:])
+    above, below = jnp.where(even, far, near), jnp.where(even, near, far)
     tall = jnp.concatenate([above, grad_pre, below], axis=1)
     follow = shifted(tall, "tm", -1)
     got = exchange(terms, ("x_lo", "x_hi", "y")).reshape(16, 16, 3456)

time: 97 us -> 95 us (0.979)
  starting transfers between devices: 38.7 us -> 34.9 us
  local copies, waits for them, and re-layouts: 6.09 us -> 7.55 us
    ppermute x6 -> x2, starting transfers between devices: 15.6 us -> 7.68 us  [shifted(): lax.ppermute(value, axis, [(source, source + steps) for source in range(l...]
    ppermute x6 -> x2, waiting for transfers between devices: 9.14 us -> 2.6 us  [shifted(): lax.ppermute(value, axis, [(source, source + steps) for source in range(l...]
    ppermute x0 -> x4, waiting for transfers between devices: none -> 4.72 us  [pairs(): return lax.ppermute(value, 'space', links + [(j, i) for i, j in links])]
    ppermute x0 -> x4, starting transfers between devices: none -> 3.15 us  [pairs(): return lax.ppermute(value, 'space', links + [(j, i) for i, j in links])]
    all_to_all x2, waiting for transfers between devices: 17.9 us -> 20.2 us  [exchange(): lax.all_to_all(value, BOTH, 0, 0, tiled=True, axis_index_groups=groups_of...]
    unnamed x16 -> x14, local copies, waits for them, and re-layouts: 5.05 us -> 6.54 us
    all_to_all x2, starting transfers between devices: 19 us -> 20.2 us  [exchange(): lax.all_to_all(value, BOTH, 0, 0, tiled=True, axis_index_groups=groups_of...]
  transfers between devices with their start and end apart: 11 -> 11, of which waited for: 7 -> 6; matrix products, arithmetic and copies ran while one was open for 1% -> 1% of each run, Pallas kernels for 9% -> 9%
where the time goes in v4:
time: 95 us; the launch traced here: 94.5 us
  starting transfers between devices  34.9 us (37%)
  waiting for transfers between devices  28.7 us (30%)
  Pallas kernels  11.8 us (12%)
  blocking collectives  10.2 us (11%)
  local copies, waits for them, and re-layouts  7.55 us (8%)
    all_to_all x2, waiting for transfers between devices, exchange(): lax.all_to_all(value, BOTH, 0, 0, tiled=True, axis_index_groups=groups_of...  20.2 us
    all_to_all x2, starting transfers between devices, exchange(): lax.all_to_all(value, BOTH, 0, 0, tiled=True, axis_index_groups=groups_of...  20.2 us
    all_to_all x1, blocking collectives, exchange(): lax.all_to_all(value, BOTH, 0, 0, tiled=True, axis_index_groups=groups_of...  10.2 us
    ppermute x2, starting transfers between devices, shifted(): lax.ppermute(value, axis, [(source, source + steps) for source in range(l...  7.68 us
    unnamed x14, local copies, waits for them, and re-layouts  6.54 us
    ppermute x4, waiting for transfers between devices, pairs(): return lax.ppermute(value, 'space', links + [(j, i) for i, j in links])  4.72 us
    ppermute x3, starting transfers between devices, flip_core(): return lax.ppermute(value, 'tm', [(i, i ^ 1) for i in range(16)])  3.85 us
    ppermute x4, starting transfers between devices, pairs(): return lax.ppermute(value, 'space', links + [(j, i) for i, j in links])  3.15 us
  transfers between devices with their start and end apart: 11, of which 6 were waited for; matrix products, arithmetic and copies ran while one was open for 1% of the time, Pallas kernels for 9%

profile of v4, /device:TPU:1, one launch (start us, length us, event | category | flops | bytes accessed | tf_op | source)
XLA Modules:
  0.0 94.5 jit_solution(5638198228195437400)
XLA Ops:
  0.6 4.6 %collective-permute-start = (bf16[2,2,128,256]{3,2,1,0:T(8,128)(2,1)}, bf16[2,2,128,256]{3,2,1,0:T(8,128)(2,1)S(1)}, u32[]{:S(2)}, u32[]{:S(2)}) collective-permute-start(bf16[2,2,128,256]{3,2,1,0:T(8,128)(2,1)} %own_ref.3), channel_id=1, source_target_pairs={{0,16},{16,32},{32,48},{48,64},{64,80},{80,96},{96,112},{112,128},... | collective-permute-start | bytes 786440 | tf_op jit(solution)/shard_map/ppermute | solution.py:42
  5.2 1.0 %fusion.1 = (bf16[2,1,128,256]{3,2,1,0:T(8,128)(2,1)S(1)}, bf16[2,1,128,256]{3,2,1,0:T(8,128)(2,1)S(1)}) fusion(bf16[2,2,128,256]{3,2,1,0:T(8,128)(2,1)} %own_ref.3), kind=kLoop, calls=%fused_computation.16 | loop fusion | bytes 524288 | tf_op jit(solution)/shard_map/slice | solution.py:238
  6.2 2.6 %collective-permute-done.carried_ref = bf16[2,2,128,256]{3,2,1,0:T(8,128)(2,1)S(1)} collective-permute-done((bf16[2,2,128,256]{3,2,1,0:T(8,128)(2,1)}, bf16[2,2,128,256]{3,2,1,0:T(8,128)(2,1)S(1)}, u32[]{:S(2)}, u32[]{:S(2)}) %collective-permute-start) | collective-permute-done | bytes 262176 | tf_op jit(solution)/shard_map/ppermute | solution.py:42
  8.9 0.1 broadcast_select_fusion.4
  8.9 1.7 %collective-permute-start.1 = (bf16[4,1,128,256]{3,2,1,0:T(8,128)(2,1)S(1)}, bf16[4,1,128,256]{3,2,1,0:T(8,128)(2,1)S(1)}, u32[]{:S(2)}, u32[]{:S(2)}) collective-permute-start(bf16[4,1,128,256]{3,2,1,0:T(8,128)(2,1)S(1)} %get-tuple-element.28), channel_id=1, source_target_pairs={{0,1},{2,3},{4,5},{6,7},{8,9},{10,11},{12,13},{14,15},{1,0},{3,2},... | collective-permute-start | bytes 786440 | tf_op jit(solution)/shard_map/ppermute | solution.py:47
  10.7 0.7 collective-permute-start.2
  11.3 0.0 copy-start
  11.3 2.0 %copy-done = bf16[3,3,3,256,256]{4,3,2,1,0:T(8,128)(2,1)S(1)} copy-done((bf16[3,3,3,256,256]{4,3,2,1,0:T(8,128)(2,1)S(1)}, bf16[3,3,3,256,256]{4,3,2,1,0:T(8,128)(2,1)}, u32[]{:S(2)}) %copy-start) | copy-done | bytes 3538968
  13.3 0.9 %copy-done.3 = bf16[2,2,128,256]{3,2,1,0:T(8,128)(2,1)S(1)} copy-done((bf16[2,2,128,256]{3,2,1,0:T(8,128)(2,1)S(1)}, bf16[2,2,128,256]{3,2,1,0:T(8,128)(2,1)}, u32[]{:S(2)}) %copy-start.3) | copy-done | bytes 262168
  14.3 1.4 %shard_map.67.part_ref = f32[4,128,256]{2,1,0:T(8,128)S(1)} custom-call(bf16[2,2,128,256]{3,2,1,0:T(8,128)(2,1)S(1)} %collective-permute-done.carried_ref, bf16[2,2,128,256]{3,2,1,0:T(8,128)(2,1)S(1)} %copy-done.3, bf16[3,3,3,256,256]{4,3,2,1,0:T(8,128)(2,1)S(1)} %copy-done), custom_call_target="tpu_custom_call" | custom-call | flops 1811939328 | bytes 5000000 | tf_op jit(solution)/shard_map/pallas_call | solution.py:241
  15.7 0.0 copy-start.1
  15.7 0.0 copy-start.6
  15.7 0.0 collective-permute-done.1
  15.7 0.0 collective-permute-done.2
  15.8 0.0 copy-done.4
  15.8 0.1 pad_maximum_fusion
  15.9 0.0 copy-start.5
  15.9 0.1 broadcast_select_fusion
  16.0 0.1 collective-permute-start.3
  16.1 1.6 %copy-done.1 = bf16[3,3,3,256,256]{4,3,2,1,0:T(8,128)(2,1)S(1)} copy-done((bf16[3,3,3,256,256]{4,3,2,1,0:T(8,128)(2,1)S(1)}, bf16[3,3,3,256,256]{4,3,2,1,0:T(8,128)(2,1)}, u32[]{:S(2)}) %copy-start.1) | copy-done | bytes 3538968
  17.7 0.0 copy-done.6
  17.7 1.7 %shard_map.68 = (bf16[2,2,128,256]{3,2,1,0:T(8,128)(2,1)}, bf16[2,2,128,256]{3,2,1,0:T(8,128)(2,1)S(1)}) custom-call(bf16[4,1,128,256]{3,2,1,0:T(8,128)(2,1)S(1)} %get-tuple-element.26.before_ref, bf16[4,1,128,256]{3,2,1,0:T(8,128)(2,1)S(1)} %get-tuple-element.25.after_ref, bf16[2,2,128,256]{3,2,1,0:T(8,128)(2,1)S(1)} %copy-done.4, ...), custom_call_target="tpu_custom_call" | custom-call | flops 603979776 | bytes 5000000 | tf_op jit(solution)/shard_map/pallas_call | solution.py:250
  19.5 0.0 collective-permute-start.4
  19.5 1.4 %shard_map.69.part_ref = f32[768,1152]{1,0:T(8,128)S(1)} custom-call(bf16[4,4,128,128]{3,2,1,0:T(8,128)(2,1)S(1)} %get-tuple-element.23.cells_ref, bf16[2,2,128,256]{3,2,1,0:T(8,128)(2,1)S(1)} %get-tuple-element.17.grad_ref, bf16[256,256]{1,0:T(8,128)(2,1)S(1)} %copy-done.5), custom_call_target="tpu_custom_call" | custom-call | flops 905969664 | bytes 5000000 | tf_op jit(solution)/shard_map/pallas_call | solution.py:255
  20.9 0.1 collective-permute-done.4.grad_ref
  21.0 0.0 collective-permute-done.3.cells_ref
  21.0 2.4 %shard_map.70 = bf16[256,3456]{1,0:T(8,128)(2,1)} custom-call(bf16[4,4,128,128]{3,2,1,0:T(8,128)(2,1)S(1)} %collective-permute-done.3.cells_ref, bf16[2,2,128,256]{3,2,1,0:T(8,128)(2,1)S(1)} %collective-permute-done.4.grad_ref, bf16[256,256]{1,0:T(8,128)(2,1)S(1)} %copy-done.5, f32[768,1152]{1,0:T(8,128)S(1)} %shard_map.69.part_ref), custom_call_target="tpu_custom_call" | custom-call | flops 905969664 | bytes 5000000 | tf_op jit(solution)/shard_map/pallas_call | solution.py:258
  23.4 15.3 %all-to-all-start = ((bf16[16,16,3456]{2,1,0:T(8,128)(2,1)}), bf16[16,16,3456]{2,1,0:T(8,128)(2,1)S(1)}, u32[]{:S(2)}, u32[]{:S(2)}) async-start(bf16[16,16,3456]{2,1,0:T(8,128)(2,1)} %bitcast), calls=%async_computation | async-start | bytes 3538944 | tf_op jit(solution)/shard_map/all_to_all | solution.py:32
  38.8 0.7 collective-permute-start.5
  39.5 0.1 collective-permute-start.6
  39.6 0.0 collective-permute-done.5
  39.6 4.7 %collective-permute-done.6 = bf16[2,1,128,256]{3,2,1,0:T(8,128)(2,1)S(1)} collective-permute-done((bf16[2,1,128,256]{3,2,1,0:T(8,128)(2,1)S(1)}, bf16[2,1,128,256]{3,2,1,0:T(8,128)(2,1)S(1)}, u32[]{:S(2)}, u32[]{:S(2)}) %collective-permute-start.6) | collective-permute-done | bytes 131104 | tf_op jit(solution)/shard_map/ppermute | solution.py:47
  44.3 0.1 pad_maximum_fusion.2
  44.4 3.1 %collective-permute-start.7 = (bf16[2,4,128,256]{3,2,1,0:T(8,128)(2,1)S(1)}, bf16[2,4,128,256]{3,2,1,0:T(8,128)(2,1)S(1)}, u32[]{:S(2)}, u32[]{:S(2)}) collective-permute-start(bf16[2,4,128,256]{3,2,1,0:T(8,128)(2,1)S(1)} %pad_maximum_fusion.2), channel_id=1, source_target_pairs={{16,0},{32,16},{48,32},{64,48},{80,64},{96,80},{112,96},{128,112},... | collective-permute-start | bytes 1572872 | tf_op jit(solution)/shard_map/ppermute | solution.py:42
  47.5 17.6 %all-to-all-done.got_ref = bf16[16,16,3456]{2,1,0:T(8,128)(2,1)S(1)} async-done(((bf16[16,16,3456]{2,1,0:T(8,128)(2,1)}), bf16[16,16,3456]{2,1,0:T(8,128)(2,1)S(1)}, u32[]{:S(2)}, u32[]{:S(2)}) %all-to-all-start) | async-done | bytes 1769504 | tf_op jit(solution)/shard_map/all_to_all | solution.py:32
  65.1 0.5 shard_map.71
  65.6 10.2 %all_to_all.19.got_ref = bf16[8,2,3456]{2,1,0:T(2,128)(2,1)S(1)} all-to-all(bf16[8,2,3456]{2,1,0:T(2,128)(2,1)S(1)} %shard_map.71), channel_id=1, replica_groups={{0,1,2,3,4,5,6,7},{8,9,10,11,12,13,14,15},{16,17,18,19,20,21,22,23},{24..., dimensions={0} | all-to-all | bytes 221184 | tf_op jit(solution)/shard_map/all_to_all | solution.py:32
  75.8 0.7 shard_map.72
  76.5 0.0 collective-permute-done.7
  76.5 4.8 %all-to-all-start.2 = ((f32[8,2,3456]{2,1,0:T(2,128)}), f32[8,2,3456]{2,1,0:T(2,128)S(1)}, u32[]{:S(2)}, u32[]{:S(2)}) async-start(f32[8,2,3456]{2,1,0:T(2,128)} %shard_map.72), calls=%async_computation.2 | async-start | bytes 442368 | tf_op jit(solution)/shard_map/all_to_all | solution.py:32
  81.3 0.1 pad_maximum_fusion.1.ext_ref
  81.4 0.0 copy-start.2
  81.4 2.0 %copy-done.2 = bf16[3,3,3,256,256]{4,3,2,1,0:T(8,128)(2,1)S(1)} copy-done((bf16[3,3,3,256,256]{4,3,2,1,0:T(8,128)(2,1)S(1)}, bf16[3,3,3,256,256]{4,3,2,1,0:T(8,128)(2,1)}, u32[]{:S(2)}) %copy-start.2) | copy-done | bytes 3538968
  83.4 2.7 %shard_map.73 = bf16[2,2,128,256]{3,2,1,0:T(8,128)(2,1)} custom-call(bf16[4,4,128,256]{3,2,1,0:T(8,128)(2,1)S(1)} %pad_maximum_fusion.1.ext_ref, bf16[3,3,3,256,256]{4,3,2,1,0:T(8,128)(2,1)S(1)} %copy-done.2, bf16[2,2,128,256]{3,2,1,0:T(8,128)(2,1)S(1)} %copy-done.6), custom_call_target="tpu_custom_call" | custom-call | flops 1811939328 | bytes 5000000 | tf_op jit(solution)/shard_map/pallas_call | solution.py:284
  86.1 2.6 %all-to-all-done.2.mine_ref = f32[8,2,3456]{2,1,0:T(2,128)S(1)} async-done(((f32[8,2,3456]{2,1,0:T(2,128)}), f32[8,2,3456]{2,1,0:T(2,128)S(1)}, u32[]{:S(2)}, u32[]{:S(2)}) %all-to-all-start.2) | async-done | bytes 221216 | tf_op jit(solution)/shard_map/all_to_all | solution.py:32
  88.8 3.8 %collective-permute-start.8 = (f32[8,2,3456]{2,1,0:T(2,128)S(1)}, f32[8,2,3456]{2,1,0:T(2,128)S(1)}, u32[]{:S(2)}, u32[]{:S(2)}) collective-permute-start(f32[8,2,3456]{2,1,0:T(2,128)S(1)} %all-to-all-done.2.mine_ref), channel_id=1, source_target_pairs={{0,16},{16,0},{32,48},{48,32},{64,80},{80,64},{96,112},{112,96},{1... | collective-permute-start | bytes 663560 | tf_op jit(solution)/shard_map/ppermute | solution.py:36
  92.5 1.1 %collective-permute-done.8.other_ref = f32[8,2,3456]{2,1,0:T(2,128)S(1)} collective-permute-done((f32[8,2,3456]{2,1,0:T(2,128)S(1)}, f32[8,2,3456]{2,1,0:T(2,128)S(1)}, u32[]{:S(2)}, u32[]{:S(2)}) %collective-permute-start.8) | collective-permute-done | bytes 221216 | tf_op jit(solution)/shard_map/ppermute | solution.py:36
  93.6 0.9 shard_map.74
  (7 shorter events, 0.1 us)
Async XLA Ops:
  0.6 8.2 %collective-permute-start = (bf16[2,2,128,256]{3,2,1,0:T(8,128)(2,1)}, bf16[2,2,128,256]{3,2,1,0:T(8,128)(2,1)S(1)}, u32[]{:S(2)}, u32[]{:S(2)}) collective-permute-start(bf16[2,2,128,256]{3,2,1,0:T(8,128)(2,1)} %own_ref.3), channel_id=1, source_target_pairs={{0,16},{16,32},{32,48},{48,64},{64,80},{80,96},{96,112},{112,128},... | collective-permute-start | bytes 786440 | tf_op jit(solution)/shard_map/ppermute | solution.py:42
  8.9 6.8 %collective-permute-start.1 = (bf16[4,1,128,256]{3,2,1,0:T(8,128)(2,1)S(1)}, bf16[4,1,128,256]{3,2,1,0:T(8,128)(2,1)S(1)}, u32[]{:S(2)}, u32[]{:S(2)}) collective-permute-start(bf16[4,1,128,256]{3,2,1,0:T(8,128)(2,1)S(1)} %get-tuple-element.28), channel_id=1, source_target_pairs={{0,1},{2,3},{4,5},{6,7},{8,9},{10,11},{12,13},{14,15},{1,0},{3,2},... | collective-permute-start | bytes 786440 | tf_op jit(solution)/shard_map/ppermute | solution.py:47
  10.7 5.1 %collective-permute-start.2 = (bf16[4,1,128,256]{3,2,1,0:T(8,128)(2,1)S(1)}, bf16[4,1,128,256]{3,2,1,0:T(8,128)(2,1)S(1)}, u32[]{:S(2)}, u32[]{:S(2)}) collective-permute-start(bf16[4,1,128,256]{3,2,1,0:T(8,128)(2,1)S(1)} %get-tuple-element.27), channel_id=1, source_target_pairs={{1,2},{3,4},{5,6},{7,8},{9,10},{11,12},{13,14},{2,1},{4,3},{6,5},{... | collective-permute-start | bytes 786440 | tf_op jit(solution)/shard_map/ppermute | solution.py:47
  11.3 2.0 %copy-start = (bf16[3,3,3,256,256]{4,3,2,1,0:T(8,128)(2,1)S(1)}, bf16[3,3,3,256,256]{4,3,2,1,0:T(8,128)(2,1)}, u32[]{:S(2)}) copy-start(bf16[3,3,3,256,256]{4,3,2,1,0:T(8,128)(2,1)} %w_ref.5) | copy-start | bytes 10616836
  13.3 0.9 %copy-start.3 = (bf16[2,2,128,256]{3,2,1,0:T(8,128)(2,1)S(1)}, bf16[2,2,128,256]{3,2,1,0:T(8,128)(2,1)}, u32[]{:S(2)}) copy-start(bf16[2,2,128,256]{3,2,1,0:T(8,128)(2,1)} %own_ref.3) | copy-start | bytes 786436
  14.3 1.5 %copy-start.4 = (bf16[2,2,128,256]{3,2,1,0:T(8,128)(2,1)S(1)}, bf16[2,2,128,256]{3,2,1,0:T(8,128)(2,1)}, u32[]{:S(2)}) copy-start(bf16[2,2,128,256]{3,2,1,0:T(8,128)(2,1)} %own_ref.3) | copy-start | bytes 786436
  15.7 2.0 %copy-start.1 = (bf16[3,3,3,256,256]{4,3,2,1,0:T(8,128)(2,1)S(1)}, bf16[3,3,3,256,256]{4,3,2,1,0:T(8,128)(2,1)}, u32[]{:S(2)}) copy-start(bf16[3,3,3,256,256]{4,3,2,1,0:T(8,128)(2,1)} %w_ref.5) | copy-start | bytes 10616836
  15.7 2.0 %copy-start.6 = (bf16[2,2,128,256]{3,2,1,0:T(8,128)(2,1)S(1)}, bf16[2,2,128,256]{3,2,1,0:T(8,128)(2,1)}, u32[]{:S(2)}) copy-start(bf16[2,2,128,256]{3,2,1,0:T(8,128)(2,1)} %cot_ref.3) | copy-start | bytes 786436
  15.9 3.5 %copy-start.5 = (bf16[256,256]{1,0:T(8,128)(2,1)S(1)}, bf16[256,256]{1,0:T(8,128)(2,1)}, u32[]{:S(2)}) copy-start(bf16[256,256]{1,0:T(8,128)(2,1)} %constant.31.clone.order_ref) | copy-start | bytes 393220
  16.0 5.0 %collective-permute-start.3 = (bf16[4,4,128,128]{3,2,1,0:T(8,128)(2,1)S(1)}, bf16[4,4,128,128]{3,2,1,0:T(8,128)(2,1)S(1)}, u32[]{:S(2)}, u32[]{:S(2)}) collective-permute-start(bf16[4,4,128,128]{3,2,1,0:T(8,128)(2,1)S(1)} %get-tuple-element.24), channel_id=1, source_target_pairs={{0,16},{16,0},{32,48},{48,32},{64,80},{80,64},{96,112},{112,96},{1... | collective-permute-start | bytes 1572872 | tf_op jit(solution)/shard_map/ppermute | solution.py:36
  19.5 1.5 %collective-permute-start.4 = (bf16[2,2,128,256]{3,2,1,0:T(8,128)(2,1)S(1)}, bf16[2,2,128,256]{3,2,1,0:T(8,128)(2,1)S(1)}, u32[]{:S(2)}, u32[]{:S(2)}) collective-permute-start(bf16[2,2,128,256]{3,2,1,0:T(8,128)(2,1)S(1)} %get-tuple-element.17.grad_ref), channel_id=1, source_target_pairs={{0,16},{16,0},{32,48},{48,32},{64,80},{80,64},{96,112},{112,96},{1... | collective-permute-start | bytes 786440 | tf_op jit(solution)/shard_map/ppermute | solution.py:36
  23.4 41.7 %all-to-all-start = ((bf16[16,16,3456]{2,1,0:T(8,128)(2,1)}), bf16[16,16,3456]{2,1,0:T(8,128)(2,1)S(1)}, u32[]{:S(2)}, u32[]{:S(2)}) async-start(bf16[16,16,3456]{2,1,0:T(8,128)(2,1)} %bitcast), calls=%async_computation | async-start | bytes 3538944 | tf_op jit(solution)/shard_map/all_to_all | solution.py:32
  38.8 0.8 collective-permute-start.5
  39.5 4.8 %collective-permute-start.6 = (bf16[2,1,128,256]{3,2,1,0:T(8,128)(2,1)S(1)}, bf16[2,1,128,256]{3,2,1,0:T(8,128)(2,1)S(1)}, u32[]{:S(2)}, u32[]{:S(2)}) collective-permute-start(bf16[2,1,128,256]{3,2,1,0:T(8,128)(2,1)S(1)} %get-tuple-element.32), channel_id=1, source_target_pairs={{0,1},{2,3},{4,5},{6,7},{8,9},{10,11},{12,13},{14,15},{1,0},{3,2},... | collective-permute-start | bytes 393224 | tf_op jit(solution)/shard_map/ppermute | solution.py:47
  44.4 32.1 %collective-permute-start.7 = (bf16[2,4,128,256]{3,2,1,0:T(8,128)(2,1)S(1)}, bf16[2,4,128,256]{3,2,1,0:T(8,128)(2,1)S(1)}, u32[]{:S(2)}, u32[]{:S(2)}) collective-permute-start(bf16[2,4,128,256]{3,2,1,0:T(8,128)(2,1)S(1)} %pad_maximum_fusion.2), channel_id=1, source_target_pairs={{16,0},{32,16},{48,32},{64,48},{80,64},{96,80},{112,96},{128,112},... | collective-permute-start | bytes 1572872 | tf_op jit(solution)/shard_map/ppermute | solution.py:42
  76.5 12.3 %all-to-all-start.2 = ((f32[8,2,3456]{2,1,0:T(2,128)}), f32[8,2,3456]{2,1,0:T(2,128)S(1)}, u32[]{:S(2)}, u32[]{:S(2)}) async-start(f32[8,2,3456]{2,1,0:T(2,128)} %shard_map.72), calls=%async_computation.2 | async-start | bytes 442368 | tf_op jit(solution)/shard_map/all_to_all | solution.py:32
  81.4 2.0 %copy-start.2 = (bf16[3,3,3,256,256]{4,3,2,1,0:T(8,128)(2,1)S(1)}, bf16[3,3,3,256,256]{4,3,2,1,0:T(8,128)(2,1)}, u32[]{:S(2)}) copy-start(bf16[3,3,3,256,256]{4,3,2,1,0:T(8,128)(2,1)} %w_ref.5) | copy-start | bytes 10616836
  88.8 4.9 %collective-permute-start.8 = (f32[8,2,3456]{2,1,0:T(2,128)S(1)}, f32[8,2,3456]{2,1,0:T(2,128)S(1)}, u32[]{:S(2)}, u32[]{:S(2)}) collective-permute-start(f32[8,2,3456]{2,1,0:T(2,128)S(1)} %all-to-all-done.2.mine_ref), channel_id=1, source_target_pairs={{0,16},{16,0},{32,48},{48,32},{64,80},{80,64},{96,112},{112,96},{1... | collective-permute-start | bytes 663560 | tf_op jit(solution)/shard_map/ppermute | solution.py:36

commit v5 on v4

--- a/solution.py
+++ b/solution.py
@@ -65,20 +65,31 @@
     return ref[a : a + 2, b : b + 2].reshape(512, -1)
 
 
-def near_kernel(carried_ref, own_ref, w_ref, part_ref):
+def edge_kernel(frames_ref, top_ref, bottom_ref, own_ref):
+    top_ref[...] = frames_ref[:, :1]
+    bottom_ref[...] = frames_ref[:, 1:]
+    own_ref[...] = frames_ref[...]
+
+
+def near_kernel(carried_ref, own_ref, w_from, part_ref, w_ref, sems):
+    copies = [
+        pltpu.make_async_copy(w_from.at[:, :, c], w_ref.at[:, :, c], sems.at[c]) for c in range(3)
+    ]
+    for copy in copies:
+        copy.start()
+    blocks = [
+        carried_ref[...],
+        jnp.concatenate([carried_ref[1:], own_ref[:1]], axis=0),
+        own_ref[...],
+    ]
     sums = []
     for c in range(3):
         both = jnp.zeros((512, 256), jnp.float32)
         upper = jnp.zeros((256, 256), jnp.float32)
         lower = jnp.zeros((256, 256), jnp.float32)
+        copies[c].wait()
         for a in range(3):
-            if a == 0:
-                block = carried_ref[...]
-            elif a == 1:
-                block = jnp.concatenate([carried_ref[1:], own_ref[:1]], axis=0)
-            else:
-                block = own_ref[...]
-            rows = [block[:, r].reshape(256, 256) for r in range(2)]
+            rows = [blocks[a][:, r].reshape(256, 256) for r in range(2)]
             both += jnp.dot(
                 jnp.concatenate(rows, axis=0), w_ref[a, 1, c], preferred_element_type=jnp.float32
             )
@@ -233,22 +244,37 @@
 
     carried = shifted(frames_in, "tm", 1)
     even = lax.axis_index("space") % 2 == 0
+    edge = jax.ShapeDtypeStruct((2, 1, 128, 256), jnp.bfloat16)
+    top, bottom, own = call(edge_kernel, (edge, edge, block), 100000)(frames_in)
     near, far = row_halo(
-        jnp.concatenate([carried[:, :1], frames_in[:, :1]], axis=0),
-        jnp.concatenate([carried[:, 1:], frames_in[:, 1:]], axis=0),
-    )
-    part = jax.ShapeDtypeStruct((4, 128, 256), jnp.float32)
-    part = call(near_kernel, part, flops)(carried, frames_in, weight)
+        jnp.concatenate([carried[:, :1], top], axis=0),
+        jnp.concatenate([carried[:, 1:], bottom], axis=0),
+    )
+    part = pl.pallas_call(
+        near_kernel,
+        out_shape=jax.ShapeDtypeStruct((4, 128, 256), jnp.float32),
+        in_specs=[
+            pl.BlockSpec(memory_space=pltpu.VMEM),
+            pl.BlockSpec(memory_space=pltpu.VMEM),
+            pl.BlockSpec(memory_space=pltpu.HBM),
+        ],
+        scratch_shapes=[
+            pltpu.VMEM((3, 3, 3, 256, 256), jnp.bfloat16),
+            pltpu.SemaphoreType.DMA((3,)),
+        ],
+        compiler_params=pltpu.CompilerParams(vmem_limit_bytes=50 * 1024 * 1024),
+        cost_estimate=pl.CostEstimate(flops=flops, bytes_accessed=5000000, transcendentals=0),
+    )(carried, own, weight)
     near, far, part = lax.optimization_barrier((near, far, part))
     before, after = jnp.where(even, far, near), jnp.where(even, near, far)
     ext = jnp.concatenate(
-        [before, jnp.concatenate([carried, frames_in], axis=0), after], axis=1
+        [before, jnp.concatenate([carried, own], axis=0), after], axis=1
     )
     low, high = ext[..., :128], ext[..., 128:]
     mine = jnp.where(core == 0, low, high)
     theirs = flip_core(jnp.where(core == 0, high, low))
     output, grad_pre = call(forward_kernel, (block, block), flops // 3)(
-        before, after, frames_in, part, weight, cotangent
+        before, after, own, part, weight, cotangent
     )
     grad_other = flip_core(grad_pre)
     order = jnp.asarray(row_order(), jnp.bfloat16)

time: 95 us -> 95 us (level)
  local copies, waits for them, and re-layouts: 7.55 us -> 4.57 us
  Pallas kernels: 11.8 us -> 14.3 us
  starting transfers between devices: 34.9 us -> 36 us
    pallas_call x1 -> x2, Pallas kernels: 1.39 us -> 3.84 us  [the longest x1 3.8 us: local(): pl.pallas_call(near_kernel, out_shape=jax.ShapeDtypeStruct((4, 128, 256),...]
    unnamed x14 -> x10, local copies, waits for them, and re-layouts: 6.54 us -> 4.55 us
    slice x1 -> x0, local copies, waits for them, and re-layouts: 0.99 us -> none  [local(): frames_in[:, 1:]]
  transfers between devices with their start and end apart: 11 -> 11, of which waited for: 6 -> 6; matrix products, arithmetic and copies ran while one was open for 1% -> 0% of each run, Pallas kernels for 9% -> 12%
where the time goes in v5:
time: 95 us; the launch traced here: 94.5 us
  starting transfers between devices  36 us (38%)
  waiting for transfers between devices  28.2 us (30%)
  Pallas kernels  14.3 us (15%)
  blocking collectives  10.2 us (11%)
  local copies, waits for them, and re-layouts  4.57 us (5%)
    all_to_all x2, starting transfers between devices, exchange(): lax.all_to_all(value, BOTH, 0, 0, tiled=True, axis_index_groups=groups_of...  20.2 us
    all_to_all x2, waiting for transfers between devices, exchange(): lax.all_to_all(value, BOTH, 0, 0, tiled=True, axis_index_groups=groups_of...  20.2 us
    all_to_all x1, blocking collectives, exchange(): lax.all_to_all(value, BOTH, 0, 0, tiled=True, axis_index_groups=groups_of...  10.2 us
    ppermute x2, starting transfers between devices, shifted(): lax.ppermute(value, axis, [(source, source + steps) for source in range(l...  7.68 us
    unnamed x10, local copies, waits for them, and re-layouts  4.55 us
    ppermute x3, starting transfers between devices, flip_core(): return lax.ppermute(value, 'tm', [(i, i ^ 1) for i in range(16)])  4.45 us
    ppermute x4, waiting for transfers between devices, pairs(): return lax.ppermute(value, 'space', links + [(j, i) for i, j in links])  4.22 us
    pallas_call x1, Pallas kernels, local(): pl.pallas_call(near_kernel, out_shape=jax.ShapeDtypeStruct((4, 128, 256),...  3.8 us
  transfers between devices with their start and end apart: 11, of which 6 were waited for; matrix products, arithmetic and copies ran while one was open for 0% of the time, Pallas kernels for 12%

profile of v5, /device:TPU:1, one launch (start us, length us, event | category | flops | bytes accessed | tf_op | source)
XLA Modules:
  0.0 94.5 jit_solution(7275365054285303013)
XLA Ops:
  0.6 4.6 %collective-permute-start = (bf16[2,2,128,256]{3,2,1,0:T(8,128)(2,1)}, bf16[2,2,128,256]{3,2,1,0:T(8,128)(2,1)S(1)}, u32[]{:S(2)}, u32[]{:S(2)}) collective-permute-start(bf16[2,2,128,256]{3,2,1,0:T(8,128)(2,1)} %frames_ref.1), channel_id=1, source_target_pairs={{0,16},{16,32},{32,48},{48,64},{64,80},{80,96},{96,112},{112,128},... | collective-permute-start | bytes 786440 | tf_op jit(solution)/shard_map/ppermute | solution.py:42
  5.2 0.0 copy-start.4
  5.2 1.0 %copy-done.4 = bf16[2,2,128,256]{3,2,1,0:T(8,128)(2,1)S(1)} copy-done((bf16[2,2,128,256]{3,2,1,0:T(8,128)(2,1)S(1)}, bf16[2,2,128,256]{3,2,1,0:T(8,128)(2,1)}, u32[]{:S(2)}) %copy-start.4) | copy-done | bytes 262168
  6.2 2.6 %collective-permute-done.carried_ref = bf16[2,2,128,256]{3,2,1,0:T(8,128)(2,1)S(1)} collective-permute-done((bf16[2,2,128,256]{3,2,1,0:T(8,128)(2,1)}, bf16[2,2,128,256]{3,2,1,0:T(8,128)(2,1)S(1)}, u32[]{:S(2)}, u32[]{:S(2)}) %collective-permute-start) | collective-permute-done | bytes 262176 | tf_op jit(solution)/shard_map/ppermute | solution.py:42
  8.9 0.1 broadcast_select_fusion.4
  8.9 1.7 %collective-permute-start.1 = (bf16[4,1,128,256]{3,2,1,0:T(8,128)(2,1)S(1)}, bf16[4,1,128,256]{3,2,1,0:T(8,128)(2,1)S(1)}, u32[]{:S(2)}, u32[]{:S(2)}) collective-permute-start(bf16[4,1,128,256]{3,2,1,0:T(8,128)(2,1)S(1)} %get-tuple-element.34), channel_id=1, source_target_pairs={{0,1},{2,3},{4,5},{6,7},{8,9},{10,11},{12,13},{14,15},{1,0},{3,2},... | collective-permute-start | bytes 786440 | tf_op jit(solution)/shard_map/ppermute | solution.py:47
  10.6 0.7 collective-permute-start.2
  11.3 3.8 %shard_map.68.part_ref = f32[4,128,256]{2,1,0:T(8,128)S(1)} custom-call(bf16[2,2,128,256]{3,2,1,0:T(8,128)(2,1)S(1)} %collective-permute-done.carried_ref, bf16[2,2,128,256]{3,2,1,0:T(8,128)(2,1)S(1)} %get-tuple-element.18.own_ref, bf16[3,3,3,256,256]{4,3,2,1,0:T(8,128)(2,1)} %w_ref.3), custom_call_target="tpu_custom_call" | custom-call | flops 1811939328 | bytes 5000000 | tf_op jit(solution)/shard_map/pallas_call | solution.py:253
  15.1 0.0 copy-start
  15.2 0.0 copy-start.3
  15.2 0.0 collective-permute-done.1
  15.2 0.0 collective-permute-done.2
  15.2 0.1 pad_maximum_fusion
  15.4 0.0 copy-start.2
  15.4 0.1 broadcast_select_fusion
  15.5 0.1 collective-permute-start.3
  15.6 1.6 %copy-done = bf16[3,3,3,256,256]{4,3,2,1,0:T(8,128)(2,1)S(1)} copy-done((bf16[3,3,3,256,256]{4,3,2,1,0:T(8,128)(2,1)S(1)}, bf16[3,3,3,256,256]{4,3,2,1,0:T(8,128)(2,1)}, u32[]{:S(2)}) %copy-start) | copy-done | bytes 3538968
  17.1 0.0 copy-done.3
  17.2 1.7 %shard_map.69 = (bf16[2,2,128,256]{3,2,1,0:T(8,128)(2,1)}, bf16[2,2,128,256]{3,2,1,0:T(8,128)(2,1)S(1)}) custom-call(bf16[4,1,128,256]{3,2,1,0:T(8,128)(2,1)S(1)} %get-tuple-element.32.before_ref, bf16[4,1,128,256]{3,2,1,0:T(8,128)(2,1)S(1)} %get-tuple-element.31.after_ref, bf16[2,2,128,256]{3,2,1,0:T(8,128)(2,1)S(1)} %get-tuple-element.18.own_ref, ...), custom_call_target="tpu_custom_call" | custom-call | flops 603979776 | bytes 5000000 | tf_op jit(solution)/shard_map/pallas_call | solution.py:276
  18.9 0.0 collective-permute-start.4
  18.9 0.0 copy-done.2
  18.9 1.4 %shard_map.70.part_ref = f32[768,1152]{1,0:T(8,128)S(1)} custom-call(bf16[4,4,128,128]{3,2,1,0:T(8,128)(2,1)S(1)} %get-tuple-element.29.cells_ref, bf16[2,2,128,256]{3,2,1,0:T(8,128)(2,1)S(1)} %get-tuple-element.23.grad_ref, bf16[256,256]{1,0:T(8,128)(2,1)S(1)} %copy-done.2), custom_call_target="tpu_custom_call" | custom-call | flops 905969664 | bytes 5000000 | tf_op jit(solution)/shard_map/pallas_call | solution.py:281
  20.4 0.1 collective-permute-done.4.grad_ref
  20.4 0.0 collective-permute-done.3.cells_ref
  20.4 2.4 %shard_map.71 = bf16[256,3456]{1,0:T(8,128)(2,1)} custom-call(bf16[4,4,128,128]{3,2,1,0:T(8,128)(2,1)S(1)} %collective-permute-done.3.cells_ref, bf16[2,2,128,256]{3,2,1,0:T(8,128)(2,1)S(1)} %collective-permute-done.4.grad_ref, bf16[256,256]{1,0:T(8,128)(2,1)S(1)} %copy-done.2, f32[768,1152]{1,0:T(8,128)S(1)} %shard_map.70.part_ref), custom_call_target="tpu_custom_call" | custom-call | flops 905969664 | bytes 5000000 | tf_op jit(solution)/shard_map/pallas_call | solution.py:284
  22.9 15.3 %all-to-all-start = ((bf16[16,16,3456]{2,1,0:T(8,128)(2,1)}), bf16[16,16,3456]{2,1,0:T(8,128)(2,1)S(1)}, u32[]{:S(2)}, u32[]{:S(2)}) async-start(bf16[16,16,3456]{2,1,0:T(8,128)(2,1)} %bitcast), calls=%async_computation | async-start | bytes 3538944 | tf_op jit(solution)/shard_map/all_to_all | solution.py:32
  38.3 0.7 collective-permute-start.5
  38.9 0.6 collective-permute-start.6
  39.6 0.0 collective-permute-done.5
  39.6 4.2 %collective-permute-done.6 = bf16[2,1,128,256]{3,2,1,0:T(8,128)(2,1)S(1)} collective-permute-done((bf16[2,1,128,256]{3,2,1,0:T(8,128)(2,1)S(1)}, bf16[2,1,128,256]{3,2,1,0:T(8,128)(2,1)S(1)}, u32[]{:S(2)}, u32[]{:S(2)}) %collective-permute-start.6) | collective-permute-done | bytes 131104 | tf_op jit(solution)/shard_map/ppermute | solution.py:47
  43.8 0.1 pad_maximum_fusion.2
  43.9 3.1 %collective-permute-start.7 = (bf16[2,4,128,256]{3,2,1,0:T(8,128)(2,1)S(1)}, bf16[2,4,128,256]{3,2,1,0:T(8,128)(2,1)S(1)}, u32[]{:S(2)}, u32[]{:S(2)}) collective-permute-start(bf16[2,4,128,256]{3,2,1,0:T(8,128)(2,1)S(1)} %pad_maximum_fusion.2), channel_id=1, source_target_pairs={{16,0},{32,16},{48,32},{64,48},{80,64},{96,80},{112,96},{128,112},... | collective-permute-start | bytes 1572872 | tf_op jit(solution)/shard_map/ppermute | solution.py:42
  47.0 17.6 %all-to-all-done.got_ref = bf16[16,16,3456]{2,1,0:T(8,128)(2,1)S(1)} async-done(((bf16[16,16,3456]{2,1,0:T(8,128)(2,1)}), bf16[16,16,3456]{2,1,0:T(8,128)(2,1)S(1)}, u32[]{:S(2)}, u32[]{:S(2)}) %all-to-all-start) | async-done | bytes 1769504 | tf_op jit(solution)/shard_map/all_to_all | solution.py:32
  64.5 0.5 shard_map.72
  65.0 10.2 %all_to_all.19.got_ref = bf16[8,2,3456]{2,1,0:T(2,128)(2,1)S(1)} all-to-all(bf16[8,2,3456]{2,1,0:T(2,128)(2,1)S(1)} %shard_map.72), channel_id=1, replica_groups={{0,1,2,3,4,5,6,7},{8,9,10,11,12,13,14,15},{16,17,18,19,20,21,22,23},{24..., dimensions={0} | all-to-all | bytes 221184 | tf_op jit(solution)/shard_map/all_to_all | solution.py:32
  75.2 0.7 shard_map.73
  75.9 0.0 collective-permute-done.7
  75.9 4.8 %all-to-all-start.2 = ((f32[8,2,3456]{2,1,0:T(2,128)}), f32[8,2,3456]{2,1,0:T(2,128)S(1)}, u32[]{:S(2)}, u32[]{:S(2)}) async-start(f32[8,2,3456]{2,1,0:T(2,128)} %shard_map.73), calls=%async_computation.2 | async-start | bytes 442368 | tf_op jit(solution)/shard_map/all_to_all | solution.py:32
  80.8 0.1 pad_maximum_fusion.1.ext_ref
  80.9 0.0 copy-start.1
  80.9 2.0 %copy-done.1 = bf16[3,3,3,256,256]{4,3,2,1,0:T(8,128)(2,1)S(1)} copy-done((bf16[3,3,3,256,256]{4,3,2,1,0:T(8,128)(2,1)S(1)}, bf16[3,3,3,256,256]{4,3,2,1,0:T(8,128)(2,1)}, u32[]{:S(2)}) %copy-start.1) | copy-done | bytes 3538968
  82.9 2.7 %shard_map.74 = bf16[2,2,128,256]{3,2,1,0:T(8,128)(2,1)} custom-call(bf16[4,4,128,256]{3,2,1,0:T(8,128)(2,1)S(1)} %pad_maximum_fusion.1.ext_ref, bf16[3,3,3,256,256]{4,3,2,1,0:T(8,128)(2,1)S(1)} %copy-done.1, bf16[2,2,128,256]{3,2,1,0:T(8,128)(2,1)S(1)} %copy-done.3), custom_call_target="tpu_custom_call" | custom-call | flops 1811939328 | bytes 5000000 | tf_op jit(solution)/shard_map/pallas_call | solution.py:310
  85.6 2.6 %all-to-all-done.2.mine_ref = f32[8,2,3456]{2,1,0:T(2,128)S(1)} async-done(((f32[8,2,3456]{2,1,0:T(2,128)}), f32[8,2,3456]{2,1,0:T(2,128)S(1)}, u32[]{:S(2)}, u32[]{:S(2)}) %all-to-all-start.2) | async-done | bytes 221216 | tf_op jit(solution)/shard_map/all_to_all | solution.py:32
  88.2 4.4 %collective-permute-start.8 = (f32[8,2,3456]{2,1,0:T(2,128)S(1)}, f32[8,2,3456]{2,1,0:T(2,128)S(1)}, u32[]{:S(2)}, u32[]{:S(2)}) collective-permute-start(f32[8,2,3456]{2,1,0:T(2,128)S(1)} %all-to-all-done.2.mine_ref), channel_id=1, source_target_pairs={{0,16},{16,0},{32,48},{48,32},{64,80},{80,64},{96,112},{112,96},{1... | collective-permute-start | bytes 663560 | tf_op jit(solution)/shard_map/ppermute | solution.py:36
  92.5 1.1 %collective-permute-done.8.other_ref = f32[8,2,3456]{2,1,0:T(2,128)S(1)} collective-permute-done((f32[8,2,3456]{2,1,0:T(2,128)S(1)}, f32[8,2,3456]{2,1,0:T(2,128)S(1)}, u32[]{:S(2)}, u32[]{:S(2)}) %collective-permute-start.8) | collective-permute-done | bytes 221216 | tf_op jit(solution)/shard_map/ppermute | solution.py:36
  93.6 0.9 shard_map.75
  (5 shorter events, 0.1 us)
Async XLA Ops:
  0.6 8.2 %collective-permute-start = (bf16[2,2,128,256]{3,2,1,0:T(8,128)(2,1)}, bf16[2,2,128,256]{3,2,1,0:T(8,128)(2,1)S(1)}, u32[]{:S(2)}, u32[]{:S(2)}) collective-permute-start(bf16[2,2,128,256]{3,2,1,0:T(8,128)(2,1)} %frames_ref.1), channel_id=1, source_target_pairs={{0,16},{16,32},{32,48},{48,64},{64,80},{80,96},{96,112},{112,128},... | collective-permute-start | bytes 786440 | tf_op jit(solution)/shard_map/ppermute | solution.py:42
  5.2 1.0 %copy-start.4 = (bf16[2,2,128,256]{3,2,1,0:T(8,128)(2,1)S(1)}, bf16[2,2,128,256]{3,2,1,0:T(8,128)(2,1)}, u32[]{:S(2)}) copy-start(bf16[2,2,128,256]{3,2,1,0:T(8,128)(2,1)} %frames_ref.1) | copy-start | bytes 786436
  8.9 6.3 %collective-permute-start.1 = (bf16[4,1,128,256]{3,2,1,0:T(8,128)(2,1)S(1)}, bf16[4,1,128,256]{3,2,1,0:T(8,128)(2,1)S(1)}, u32[]{:S(2)}, u32[]{:S(2)}) collective-permute-start(bf16[4,1,128,256]{3,2,1,0:T(8,128)(2,1)S(1)} %get-tuple-element.34), channel_id=1, source_target_pairs={{0,1},{2,3},{4,5},{6,7},{8,9},{10,11},{12,13},{14,15},{1,0},{3,2},... | collective-permute-start | bytes 786440 | tf_op jit(solution)/shard_map/ppermute | solution.py:47
  10.6 4.5 %collective-permute-start.2 = (bf16[4,1,128,256]{3,2,1,0:T(8,128)(2,1)S(1)}, bf16[4,1,128,256]{3,2,1,0:T(8,128)(2,1)S(1)}, u32[]{:S(2)}, u32[]{:S(2)}) collective-permute-start(bf16[4,1,128,256]{3,2,1,0:T(8,128)(2,1)S(1)} %get-tuple-element.33), channel_id=1, source_target_pairs={{1,2},{3,4},{5,6},{7,8},{9,10},{11,12},{13,14},{2,1},{4,3},{6,5},{... | collective-permute-start | bytes 786440 | tf_op jit(solution)/shard_map/ppermute | solution.py:47
  15.1 2.0 %copy-start = (bf16[3,3,3,256,256]{4,3,2,1,0:T(8,128)(2,1)S(1)}, bf16[3,3,3,256,256]{4,3,2,1,0:T(8,128)(2,1)}, u32[]{:S(2)}) copy-start(bf16[3,3,3,256,256]{4,3,2,1,0:T(8,128)(2,1)} %w_ref.3) | copy-start | bytes 10616836
  15.2 2.0 %copy-start.3 = (bf16[2,2,128,256]{3,2,1,0:T(8,128)(2,1)S(1)}, bf16[2,2,128,256]{3,2,1,0:T(8,128)(2,1)}, u32[]{:S(2)}) copy-start(bf16[2,2,128,256]{3,2,1,0:T(8,128)(2,1)} %cot_ref.3) | copy-start | bytes 786436
  15.4 3.5 %copy-start.2 = (bf16[256,256]{1,0:T(8,128)(2,1)S(1)}, bf16[256,256]{1,0:T(8,128)(2,1)}, u32[]{:S(2)}) copy-start(bf16[256,256]{1,0:T(8,128)(2,1)} %constant.31.clone.order_ref) | copy-start | bytes 393220
  15.5 5.0 %collective-permute-start.3 = (bf16[4,4,128,128]{3,2,1,0:T(8,128)(2,1)S(1)}, bf16[4,4,128,128]{3,2,1,0:T(8,128)(2,1)S(1)}, u32[]{:S(2)}, u32[]{:S(2)}) collective-permute-start(bf16[4,4,128,128]{3,2,1,0:T(8,128)(2,1)S(1)} %get-tuple-element.30), channel_id=1, source_target_pairs={{0,16},{16,0},{32,48},{48,32},{64,80},{80,64},{96,112},{112,96},{1... | collective-permute-start | bytes 1572872 | tf_op jit(solution)/shard_map/ppermute | solution.py:36
  18.9 1.5 %collective-permute-start.4 = (bf16[2,2,128,256]{3,2,1,0:T(8,128)(2,1)S(1)}, bf16[2,2,128,256]{3,2,1,0:T(8,128)(2,1)S(1)}, u32[]{:S(2)}, u32[]{:S(2)}) collective-permute-start(bf16[2,2,128,256]{3,2,1,0:T(8,128)(2,1)S(1)} %get-tuple-element.23.grad_ref), channel_id=1, source_target_pairs={{0,16},{16,0},{32,48},{48,32},{64,80},{80,64},{96,112},{112,96},{1... | collective-permute-start | bytes 786440 | tf_op jit(solution)/shard_map/ppermute | solution.py:36
  22.9 41.6 %all-to-all-start = ((bf16[16,16,3456]{2,1,0:T(8,128)(2,1)}), bf16[16,16,3456]{2,1,0:T(8,128)(2,1)S(1)}, u32[]{:S(2)}, u32[]{:S(2)}) async-start(bf16[16,16,3456]{2,1,0:T(8,128)(2,1)} %bitcast), calls=%async_computation | async-start | bytes 3538944 | tf_op jit(solution)/shard_map/all_to_all | solution.py:32
  38.3 1.3 %collective-permute-start.5 = (bf16[2,1,128,256]{3,2,1,0:T(8,128)(2,1)S(1)}, bf16[2,1,128,256]{3,2,1,0:T(8,128)(2,1)S(1)}, u32[]{:S(2)}, u32[]{:S(2)}) collective-permute-start(bf16[2,1,128,256]{3,2,1,0:T(8,128)(2,1)S(1)} %get-tuple-element.37), channel_id=1, source_target_pairs={{1,2},{3,4},{5,6},{7,8},{9,10},{11,12},{13,14},{2,1},{4,3},{6,5},{... | collective-permute-start | bytes 393224 | tf_op jit(solution)/shard_map/ppermute | solution.py:47
  38.9 4.8 %collective-permute-start.6 = (bf16[2,1,128,256]{3,2,1,0:T(8,128)(2,1)S(1)}, bf16[2,1,128,256]{3,2,1,0:T(8,128)(2,1)S(1)}, u32[]{:S(2)}, u32[]{:S(2)}) collective-permute-start(bf16[2,1,128,256]{3,2,1,0:T(8,128)(2,1)S(1)} %get-tuple-element.38), channel_id=1, source_target_pairs={{0,1},{2,3},{4,5},{6,7},{8,9},{10,11},{12,13},{14,15},{1,0},{3,2},... | collective-permute-start | bytes 393224 | tf_op jit(solution)/shard_map/ppermute | solution.py:47
  43.9 32.1 %collective-permute-start.7 = (bf16[2,4,128,256]{3,2,1,0:T(8,128)(2,1)S(1)}, bf16[2,4,128,256]{3,2,1,0:T(8,128)(2,1)S(1)}, u32[]{:S(2)}, u32[]{:S(2)}) collective-permute-start(bf16[2,4,128,256]{3,2,1,0:T(8,128)(2,1)S(1)} %pad_maximum_fusion.2), channel_id=1, source_target_pairs={{16,0},{32,16},{48,32},{64,48},{80,64},{96,80},{112,96},{128,112},... | collective-permute-start | bytes 1572872 | tf_op jit(solution)/shard_map/ppermute | solution.py:42
  75.9 12.2 %all-to-all-start.2 = ((f32[8,2,3456]{2,1,0:T(2,128)}), f32[8,2,3456]{2,1,0:T(2,128)S(1)}, u32[]{:S(2)}, u32[]{:S(2)}) async-start(f32[8,2,3456]{2,1,0:T(2,128)} %shard_map.73), calls=%async_computation.2 | async-start | bytes 442368 | tf_op jit(solution)/shard_map/all_to_all | solution.py:32
  80.9 2.0 %copy-start.1 = (bf16[3,3,3,256,256]{4,3,2,1,0:T(8,128)(2,1)S(1)}, bf16[3,3,3,256,256]{4,3,2,1,0:T(8,128)(2,1)}, u32[]{:S(2)}) copy-start(bf16[3,3,3,256,256]{4,3,2,1,0:T(8,128)(2,1)} %w_ref.3) | copy-start | bytes 10616836
  88.2 5.5 %collective-permute-start.8 = (f32[8,2,3456]{2,1,0:T(2,128)S(1)}, f32[8,2,3456]{2,1,0:T(2,128)S(1)}, u32[]{:S(2)}, u32[]{:S(2)}) collective-permute-start(f32[8,2,3456]{2,1,0:T(2,128)S(1)} %all-to-all-done.2.mine_ref), channel_id=1, source_target_pairs={{0,16},{16,0},{32,48},{48,32},{64,80},{80,64},{96,112},{112,96},{1... | collective-permute-start | bytes 663560 | tf_op jit(solution)/shard_map/ppermute | solution.py:36

commit v6 on v5

--- a/solution.py
+++ b/solution.py
@@ -303,12 +303,12 @@
         compiler_params=VMEM,
     )(got)
     got = exchange(plane, ("z",)).reshape(8, 2, 3456)
+    tall, follow, _ = lax.optimization_barrier((tall, follow, plane))
+    grad_ext = jnp.concatenate([tall, follow], axis=0)
+    grad_input = call(backward_kernel, block, flops)(grad_ext, weight, cotangent)
+    got, grad_input = lax.optimization_barrier((got, grad_input))
     copies = call(line_kernel, jax.ShapeDtypeStruct((8, 2, 3456), jnp.float32), 100000)(got)
-    copies, tall, follow = lax.optimization_barrier((copies, tall, follow))
-    grad_ext = jnp.concatenate([tall, follow], axis=0)
     share = exchange(copies, ("x_hi", "y")).reshape(8, 2, 3456)
-    grad_input = call(backward_kernel, block, flops)(grad_ext, weight, cotangent)
-    share, grad_input = lax.optimization_barrier((share, grad_input))
     other = flip_core(share)
     share = call(share_kernel, jax.ShapeDtypeStruct((27, 16, 256), jnp.float32), 100000)(
         share, other

time: 95 us -> 95.3 us (level)
  starting transfers between devices: 36 us -> 33.7 us
  blocking collectives: 10.2 us -> 12.1 us
    all_to_all x1, blocking collectives: 10.2 us -> 12.1 us  [exchange(): lax.all_to_all(value, BOTH, 0, 0, tiled=True, axis_index_groups=groups_of...]
    all_to_all x2, starting transfers between devices: 20.2 us -> 18.7 us  [exchange(): lax.all_to_all(value, BOTH, 0, 0, tiled=True, axis_index_groups=groups_of...]
    pallas_call x1, Pallas kernels: 0.5 us -> 1.54 us  [local(): pl.pallas_call(plane_kernel, out_shape=jax.ShapeDtypeStruct((8, 2, 3456),...]
where the time goes in v6:
time: 95.3 us; the launch traced here: 94.9 us
  starting transfers between devices  33.7 us (35%)
  waiting for transfers between devices  28.5 us (30%)
  Pallas kernels  14.6 us (15%)
  blocking collectives  12.1 us (13%)
  local copies, waits for them, and re-layouts  4.57 us (5%)
    all_to_all x2, waiting for transfers between devices, exchange(): lax.all_to_all(value, BOTH, 0, 0, tiled=True, axis_index_groups=groups_of...  20.4 us
    all_to_all x2, starting transfers between devices, exchange(): lax.all_to_all(value, BOTH, 0, 0, tiled=True, axis_index_groups=groups_of...  18.7 us
    all_to_all x1, blocking collectives, exchange(): lax.all_to_all(value, BOTH, 0, 0, tiled=True, axis_index_groups=groups_of...  12.1 us
    ppermute x2, starting transfers between devices, shifted(): lax.ppermute(value, axis, [(source, source + steps) for source in range(l...  7.68 us
    unnamed x10, local copies, waits for them, and re-layouts  4.55 us
    ppermute x4, waiting for transfers between devices, pairs(): return lax.ppermute(value, 'space', links + [(j, i) for i, j in links])  4.22 us
    pallas_call x1, Pallas kernels, local(): pl.pallas_call(near_kernel, out_shape=jax.ShapeDtypeStruct((4, 128, 256),...  3.8 us
    ppermute x4, starting transfers between devices, pairs(): return lax.ppermute(value, 'space', links + [(j, i) for i, j in links])  3.67 us
  transfers between devices with their start and end apart: 11, of which 6 were waited for; matrix products, arithmetic and copies ran while one was open for 0% of the time, Pallas kernels for 12%

profile of v6, /device:TPU:1, one launch (start us, length us, event | category | flops | bytes accessed | tf_op | source)
XLA Modules:
  0.0 94.9 jit_solution(9946828321384959015)
XLA Ops:
  0.6 4.6 %collective-permute-start = (bf16[2,2,128,256]{3,2,1,0:T(8,128)(2,1)}, bf16[2,2,128,256]{3,2,1,0:T(8,128)(2,1)S(1)}, u32[]{:S(2)}, u32[]{:S(2)}) collective-permute-start(bf16[2,2,128,256]{3,2,1,0:T(8,128)(2,1)} %frames_ref.1), channel_id=1, source_target_pairs={{0,16},{16,32},{32,48},{48,64},{64,80},{80,96},{96,112},{112,128},... | collective-permute-start | bytes 786440 | tf_op jit(solution)/shard_map/ppermute | solution.py:42
  5.2 0.0 copy-start.4
  5.2 1.0 %copy-done.4 = bf16[2,2,128,256]{3,2,1,0:T(8,128)(2,1)S(1)} copy-done((bf16[2,2,128,256]{3,2,1,0:T(8,128)(2,1)S(1)}, bf16[2,2,128,256]{3,2,1,0:T(8,128)(2,1)}, u32[]{:S(2)}) %copy-start.4) | copy-done | bytes 262168
  6.2 2.6 %collective-permute-done.carried_ref = bf16[2,2,128,256]{3,2,1,0:T(8,128)(2,1)S(1)} collective-permute-done((bf16[2,2,128,256]{3,2,1,0:T(8,128)(2,1)}, bf16[2,2,128,256]{3,2,1,0:T(8,128)(2,1)S(1)}, u32[]{:S(2)}, u32[]{:S(2)}) %collective-permute-start) | collective-permute-done | bytes 262176 | tf_op jit(solution)/shard_map/ppermute | solution.py:42
  8.9 0.1 broadcast_select_fusion.4
  8.9 1.7 %collective-permute-start.1 = (bf16[4,1,128,256]{3,2,1,0:T(8,128)(2,1)S(1)}, bf16[4,1,128,256]{3,2,1,0:T(8,128)(2,1)S(1)}, u32[]{:S(2)}, u32[]{:S(2)}) collective-permute-start(bf16[4,1,128,256]{3,2,1,0:T(8,128)(2,1)S(1)} %get-tuple-element.32), channel_id=1, source_target_pairs={{0,1},{2,3},{4,5},{6,7},{8,9},{10,11},{12,13},{14,15},{1,0},{3,2},... | collective-permute-start | bytes 786440 | tf_op jit(solution)/shard_map/ppermute | solution.py:47
  10.6 0.7 collective-permute-start.2
  11.3 3.8 %shard_map.68.part_ref = f32[4,128,256]{2,1,0:T(8,128)S(1)} custom-call(bf16[2,2,128,256]{3,2,1,0:T(8,128)(2,1)S(1)} %collective-permute-done.carried_ref, bf16[2,2,128,256]{3,2,1,0:T(8,128)(2,1)S(1)} %get-tuple-element.17.own_ref, bf16[3,3,3,256,256]{4,3,2,1,0:T(8,128)(2,1)} %w_ref.3), custom_call_target="tpu_custom_call" | custom-call | flops 1811939328 | bytes 5000000 | tf_op jit(solution)/shard_map/pallas_call | solution.py:253
  15.1 0.0 copy-start
  15.2 0.0 copy-start.3
  15.2 0.0 collective-permute-done.1
  15.2 0.0 collective-permute-done.2
  15.2 0.1 pad_maximum_fusion
  15.4 0.0 copy-start.2
  15.4 0.1 broadcast_select_fusion
  15.5 0.1 collective-permute-start.3
  15.6 1.6 %copy-done = bf16[3,3,3,256,256]{4,3,2,1,0:T(8,128)(2,1)S(1)} copy-done((bf16[3,3,3,256,256]{4,3,2,1,0:T(8,128)(2,1)S(1)}, bf16[3,3,3,256,256]{4,3,2,1,0:T(8,128)(2,1)}, u32[]{:S(2)}) %copy-start) | copy-done | bytes 3538968
  17.1 0.0 copy-done.3
  17.2 1.7 %shard_map.69 = (bf16[2,2,128,256]{3,2,1,0:T(8,128)(2,1)}, bf16[2,2,128,256]{3,2,1,0:T(8,128)(2,1)S(1)}) custom-call(bf16[4,1,128,256]{3,2,1,0:T(8,128)(2,1)S(1)} %get-tuple-element.30.before_ref, bf16[4,1,128,256]{3,2,1,0:T(8,128)(2,1)S(1)} %get-tuple-element.29.after_ref, bf16[2,2,128,256]{3,2,1,0:T(8,128)(2,1)S(1)} %get-tuple-element.17.own_ref, ...), custom_call_target="tpu_custom_call" | custom-call | flops 603979776 | bytes 5000000 | tf_op jit(solution)/shard_map/pallas_call | solution.py:276
  18.9 0.0 collective-permute-start.4
  18.9 0.0 copy-done.2
  18.9 1.4 %shard_map.70.part_ref = f32[768,1152]{1,0:T(8,128)S(1)} custom-call(bf16[4,4,128,128]{3,2,1,0:T(8,128)(2,1)S(1)} %get-tuple-element.27.cells_ref, bf16[2,2,128,256]{3,2,1,0:T(8,128)(2,1)S(1)} %get-tuple-element.22.grad_ref, bf16[256,256]{1,0:T(8,128)(2,1)S(1)} %copy-done.2), custom_call_target="tpu_custom_call" | custom-call | flops 905969664 | bytes 5000000 | tf_op jit(solution)/shard_map/pallas_call | solution.py:281
  20.4 0.1 collective-permute-done.4.grad_ref
  20.4 0.0 collective-permute-done.3.cells_ref
  20.4 2.4 %shard_map.71 = bf16[256,3456]{1,0:T(8,128)(2,1)} custom-call(bf16[4,4,128,128]{3,2,1,0:T(8,128)(2,1)S(1)} %collective-permute-done.3.cells_ref, bf16[2,2,128,256]{3,2,1,0:T(8,128)(2,1)S(1)} %collective-permute-done.4.grad_ref, bf16[256,256]{1,0:T(8,128)(2,1)S(1)} %copy-done.2, f32[768,1152]{1,0:T(8,128)S(1)} %shard_map.70.part_ref), custom_call_target="tpu_custom_call" | custom-call | flops 905969664 | bytes 5000000 | tf_op jit(solution)/shard_map/pallas_call | solution.py:284
  22.9 15.3 %all-to-all-start = ((bf16[16,16,3456]{2,1,0:T(8,128)(2,1)}), bf16[16,16,3456]{2,1,0:T(8,128)(2,1)S(1)}, u32[]{:S(2)}, u32[]{:S(2)}) async-start(bf16[16,16,3456]{2,1,0:T(8,128)(2,1)} %bitcast), calls=%async_computation | async-start | bytes 3538944 | tf_op jit(solution)/shard_map/all_to_all | solution.py:32
  38.3 0.7 collective-permute-start.5
  38.9 0.6 collective-permute-start.6
  39.6 0.0 collective-permute-done.5
  39.6 4.2 %collective-permute-done.6 = bf16[2,1,128,256]{3,2,1,0:T(8,128)(2,1)S(1)} collective-permute-done((bf16[2,1,128,256]{3,2,1,0:T(8,128)(2,1)S(1)}, bf16[2,1,128,256]{3,2,1,0:T(8,128)(2,1)S(1)}, u32[]{:S(2)}, u32[]{:S(2)}) %collective-permute-start.6) | collective-permute-done | bytes 131104 | tf_op jit(solution)/shard_map/ppermute | solution.py:47
  43.8 0.1 pad_maximum_fusion.2
  43.9 3.1 %collective-permute-start.7 = (bf16[2,4,128,256]{3,2,1,0:T(8,128)(2,1)S(1)}, bf16[2,4,128,256]{3,2,1,0:T(8,128)(2,1)S(1)}, u32[]{:S(2)}, u32[]{:S(2)}) collective-permute-start(bf16[2,4,128,256]{3,2,1,0:T(8,128)(2,1)S(1)} %pad_maximum_fusion.2), channel_id=1, source_target_pairs={{16,0},{32,16},{48,32},{64,48},{80,64},{96,80},{112,96},{128,112},... | collective-permute-start | bytes 1572872 | tf_op jit(solution)/shard_map/ppermute | solution.py:42
  47.0 17.6 %all-to-all-done.got_ref = bf16[16,16,3456]{2,1,0:T(8,128)(2,1)S(1)} async-done(((bf16[16,16,3456]{2,1,0:T(8,128)(2,1)}), bf16[16,16,3456]{2,1,0:T(8,128)(2,1)S(1)}, u32[]{:S(2)}, u32[]{:S(2)}) %all-to-all-start) | async-done | bytes 1769504 | tf_op jit(solution)/shard_map/all_to_all | solution.py:32
  64.5 1.5 %shard_map.72 = bf16[8,2,3456]{2,1,0:T(2,128)(2,1)} custom-call(bf16[16,16,3456]{2,1,0:T(8,128)(2,1)S(1)} %all-to-all-done.got_ref), custom_call_target="tpu_custom_call" | custom-call | tf_op jit(solution)/shard_map/pallas_call | solution.py:297
  66.1 3.4 %all-to-all-start.1 = ((bf16[8,2,3456]{2,1,0:T(2,128)(2,1)}), bf16[8,2,3456]{2,1,0:T(2,128)(2,1)S(1)}, u32[]{:S(2)}, u32[]{:S(2)}) async-start(bf16[8,2,3456]{2,1,0:T(2,128)(2,1)} %shard_map.72), calls=%async_computation.1 | async-start | bytes 221184 | tf_op jit(solution)/shard_map/all_to_all | solution.py:32
  69.4 0.0 collective-permute-done.7
  69.4 0.1 pad_maximum_fusion.1.ext_ref
  69.5 0.0 copy-start.1
  69.6 2.0 %copy-done.1 = bf16[3,3,3,256,256]{4,3,2,1,0:T(8,128)(2,1)S(1)} copy-done((bf16[3,3,3,256,256]{4,3,2,1,0:T(8,128)(2,1)S(1)}, bf16[3,3,3,256,256]{4,3,2,1,0:T(8,128)(2,1)}, u32[]{:S(2)}) %copy-start.1) | copy-done | bytes 3538968
  71.5 2.7 %shard_map.73 = bf16[2,2,128,256]{3,2,1,0:T(8,128)(2,1)} custom-call(bf16[4,4,128,256]{3,2,1,0:T(8,128)(2,1)S(1)} %pad_maximum_fusion.1.ext_ref, bf16[3,3,3,256,256]{4,3,2,1,0:T(8,128)(2,1)S(1)} %copy-done.1, bf16[2,2,128,256]{3,2,1,0:T(8,128)(2,1)S(1)} %copy-done.3), custom_call_target="tpu_custom_call" | custom-call | flops 1811939328 | bytes 5000000 | tf_op jit(solution)/shard_map/pallas_call | solution.py:308
  74.3 2.9 %all-to-all-done.1.got_ref = bf16[8,2,3456]{2,1,0:T(2,128)(2,1)S(1)} async-done(((bf16[8,2,3456]{2,1,0:T(2,128)(2,1)}), bf16[8,2,3456]{2,1,0:T(2,128)(2,1)S(1)}, u32[]{:S(2)}, u32[]{:S(2)}) %all-to-all-start.1) | async-done | bytes 110624 | tf_op jit(solution)/shard_map/all_to_all | solution.py:32
  77.2 12.1 %all_to_all.19.mine_ref = f32[8,2,3456]{2,1,0:T(2,128)S(1)} all-to-all(f32[8,2,3456]{2,1,0:T(2,128)S(1)} %shard_map.74), channel_id=1, replica_groups={{0,32,64,96,128,160,192,224},{1,33,65,97,129,161,193,225},{2,34,66,98,1..., dimensions={0} | all-to-all | bytes 442368 | tf_op jit(solution)/shard_map/all_to_all | solution.py:32
  89.3 3.6 %collective-permute-start.8 = (f32[8,2,3456]{2,1,0:T(2,128)S(1)}, f32[8,2,3456]{2,1,0:T(2,128)S(1)}, u32[]{:S(2)}, u32[]{:S(2)}) collective-permute-start(f32[8,2,3456]{2,1,0:T(2,128)S(1)} %all_to_all.19.mine_ref), channel_id=1, source_target_pairs={{0,16},{16,0},{32,48},{48,32},{64,80},{80,64},{96,112},{112,96},{1... | collective-permute-start | bytes 663560 | tf_op jit(solution)/shard_map/ppermute | solution.py:36
  92.9 1.1 %collective-permute-done.8.other_ref = f32[8,2,3456]{2,1,0:T(2,128)S(1)} collective-permute-done((f32[8,2,3456]{2,1,0:T(2,128)S(1)}, f32[8,2,3456]{2,1,0:T(2,128)S(1)}, u32[]{:S(2)}, u32[]{:S(2)}) %collective-permute-start.8) | collective-permute-done | bytes 221216 | tf_op jit(solution)/shard_map/ppermute | solution.py:36
  94.0 0.9 shard_map.75
  (6 shorter events, 0.2 us)
Async XLA Ops:
  0.6 8.2 %collective-permute-start = (bf16[2,2,128,256]{3,2,1,0:T(8,128)(2,1)}, bf16[2,2,128,256]{3,2,1,0:T(8,128)(2,1)S(1)}, u32[]{:S(2)}, u32[]{:S(2)}) collective-permute-start(bf16[2,2,128,256]{3,2,1,0:T(8,128)(2,1)} %frames_ref.1), channel_id=1, source_target_pairs={{0,16},{16,32},{32,48},{48,64},{64,80},{80,96},{96,112},{112,128},... | collective-permute-start | bytes 786440 | tf_op jit(solution)/shard_map/ppermute | solution.py:42
  5.2 1.0 %copy-start.4 = (bf16[2,2,128,256]{3,2,1,0:T(8,128)(2,1)S(1)}, bf16[2,2,128,256]{3,2,1,0:T(8,128)(2,1)}, u32[]{:S(2)}) copy-start(bf16[2,2,128,256]{3,2,1,0:T(8,128)(2,1)} %frames_ref.1) | copy-start | bytes 786436
  8.9 6.3 %collective-permute-start.1 = (bf16[4,1,128,256]{3,2,1,0:T(8,128)(2,1)S(1)}, bf16[4,1,128,256]{3,2,1,0:T(8,128)(2,1)S(1)}, u32[]{:S(2)}, u32[]{:S(2)}) collective-permute-start(bf16[4,1,128,256]{3,2,1,0:T(8,128)(2,1)S(1)} %get-tuple-element.32), channel_id=1, source_target_pairs={{0,1},{2,3},{4,5},{6,7},{8,9},{10,11},{12,13},{14,15},{1,0},{3,2},... | collective-permute-start | bytes 786440 | tf_op jit(solution)/shard_map/ppermute | solution.py:47
  10.6 4.5 %collective-permute-start.2 = (bf16[4,1,128,256]{3,2,1,0:T(8,128)(2,1)S(1)}, bf16[4,1,128,256]{3,2,1,0:T(8,128)(2,1)S(1)}, u32[]{:S(2)}, u32[]{:S(2)}) collective-permute-start(bf16[4,1,128,256]{3,2,1,0:T(8,128)(2,1)S(1)} %get-tuple-element.31), channel_id=1, source_target_pairs={{1,2},{3,4},{5,6},{7,8},{9,10},{11,12},{13,14},{2,1},{4,3},{6,5},{... | collective-permute-start | bytes 786440 | tf_op jit(solution)/shard_map/ppermute | solution.py:47
  15.1 2.0 %copy-start = (bf16[3,3,3,256,256]{4,3,2,1,0:T(8,128)(2,1)S(1)}, bf16[3,3,3,256,256]{4,3,2,1,0:T(8,128)(2,1)}, u32[]{:S(2)}) copy-start(bf16[3,3,3,256,256]{4,3,2,1,0:T(8,128)(2,1)} %w_ref.3) | copy-start | bytes 10616836
  15.2 2.0 %copy-start.3 = (bf16[2,2,128,256]{3,2,1,0:T(8,128)(2,1)S(1)}, bf16[2,2,128,256]{3,2,1,0:T(8,128)(2,1)}, u32[]{:S(2)}) copy-start(bf16[2,2,128,256]{3,2,1,0:T(8,128)(2,1)} %cot_ref.3) | copy-start | bytes 786436
  15.4 3.5 %copy-start.2 = (bf16[256,256]{1,0:T(8,128)(2,1)S(1)}, bf16[256,256]{1,0:T(8,128)(2,1)}, u32[]{:S(2)}) copy-start(bf16[256,256]{1,0:T(8,128)(2,1)} %constant.31.clone.order_ref) | copy-start | bytes 393220
  15.5 5.0 %collective-permute-start.3 = (bf16[4,4,128,128]{3,2,1,0:T(8,128)(2,1)S(1)}, bf16[4,4,128,128]{3,2,1,0:T(8,128)(2,1)S(1)}, u32[]{:S(2)}, u32[]{:S(2)}) collective-permute-start(bf16[4,4,128,128]{3,2,1,0:T(8,128)(2,1)S(1)} %get-tuple-element.28), channel_id=1, source_target_pairs={{0,16},{16,0},{32,48},{48,32},{64,80},{80,64},{96,112},{112,96},{1... | collective-permute-start | bytes 1572872 | tf_op jit(solution)/shard_map/ppermute | solution.py:36
  18.9 1.5 %collective-permute-start.4 = (bf16[2,2,128,256]{3,2,1,0:T(8,128)(2,1)S(1)}, bf16[2,2,128,256]{3,2,1,0:T(8,128)(2,1)S(1)}, u32[]{:S(2)}, u32[]{:S(2)}) collective-permute-start(bf16[2,2,128,256]{3,2,1,0:T(8,128)(2,1)S(1)} %get-tuple-element.22.grad_ref), channel_id=1, source_target_pairs={{0,16},{16,0},{32,48},{48,32},{64,80},{80,64},{96,112},{112,96},{1... | collective-permute-start | bytes 786440 | tf_op jit(solution)/shard_map/ppermute | solution.py:36
  22.9 41.6 %all-to-all-start = ((bf16[16,16,3456]{2,1,0:T(8,128)(2,1)}), bf16[16,16,3456]{2,1,0:T(8,128)(2,1)S(1)}, u32[]{:S(2)}, u32[]{:S(2)}) async-start(bf16[16,16,3456]{2,1,0:T(8,128)(2,1)} %bitcast), calls=%async_computation | async-start | bytes 3538944 | tf_op jit(solution)/shard_map/all_to_all | solution.py:32
  38.3 1.3 %collective-permute-start.5 = (bf16[2,1,128,256]{3,2,1,0:T(8,128)(2,1)S(1)}, bf16[2,1,128,256]{3,2,1,0:T(8,128)(2,1)S(1)}, u32[]{:S(2)}, u32[]{:S(2)}) collective-permute-start(bf16[2,1,128,256]{3,2,1,0:T(8,128)(2,1)S(1)} %get-tuple-element.35), channel_id=1, source_target_pairs={{1,2},{3,4},{5,6},{7,8},{9,10},{11,12},{13,14},{2,1},{4,3},{6,5},{... | collective-permute-start | bytes 393224 | tf_op jit(solution)/shard_map/ppermute | solution.py:47
  38.9 4.8 %collective-permute-start.6 = (bf16[2,1,128,256]{3,2,1,0:T(8,128)(2,1)S(1)}, bf16[2,1,128,256]{3,2,1,0:T(8,128)(2,1)S(1)}, u32[]{:S(2)}, u32[]{:S(2)}) collective-permute-start(bf16[2,1,128,256]{3,2,1,0:T(8,128)(2,1)S(1)} %get-tuple-element.36), channel_id=1, source_target_pairs={{0,1},{2,3},{4,5},{6,7},{8,9},{10,11},{12,13},{14,15},{1,0},{3,2},... | collective-permute-start | bytes 393224 | tf_op jit(solution)/shard_map/ppermute | solution.py:47
  43.9 25.6 %collective-permute-start.7 = (bf16[2,4,128,256]{3,2,1,0:T(8,128)(2,1)S(1)}, bf16[2,4,128,256]{3,2,1,0:T(8,128)(2,1)S(1)}, u32[]{:S(2)}, u32[]{:S(2)}) collective-permute-start(bf16[2,4,128,256]{3,2,1,0:T(8,128)(2,1)S(1)} %pad_maximum_fusion.2), channel_id=1, source_target_pairs={{16,0},{32,16},{48,32},{64,48},{80,64},{96,80},{112,96},{128,112},... | collective-permute-start | bytes 1572872 | tf_op jit(solution)/shard_map/ppermute | solution.py:42
  66.1 11.1 %all-to-all-start.1 = ((bf16[8,2,3456]{2,1,0:T(2,128)(2,1)}), bf16[8,2,3456]{2,1,0:T(2,128)(2,1)S(1)}, u32[]{:S(2)}, u32[]{:S(2)}) async-start(bf16[8,2,3456]{2,1,0:T(2,128)(2,1)} %shard_map.72), calls=%async_computation.1 | async-start | bytes 221184 | tf_op jit(solution)/shard_map/all_to_all | solution.py:32
  69.5 2.0 %copy-start.1 = (bf16[3,3,3,256,256]{4,3,2,1,0:T(8,128)(2,1)S(1)}, bf16[3,3,3,256,256]{4,3,2,1,0:T(8,128)(2,1)}, u32[]{:S(2)}) copy-start(bf16[3,3,3,256,256]{4,3,2,1,0:T(8,128)(2,1)} %w_ref.3) | copy-start | bytes 10616836
  89.3 4.7 %collective-permute-start.8 = (f32[8,2,3456]{2,1,0:T(2,128)S(1)}, f32[8,2,3456]{2,1,0:T(2,128)S(1)}, u32[]{:S(2)}, u32[]{:S(2)}) collective-permute-start(f32[8,2,3456]{2,1,0:T(2,128)S(1)} %all_to_all.19.mine_ref), channel_id=1, source_target_pairs={{0,16},{16,0},{32,48},{48,32},{64,80},{80,64},{96,112},{112,96},{1... | collective-permute-start | bytes 663560 | tf_op jit(solution)/shard_map/ppermute | solution.py:36

commit v7 on v5

--- a/solution.py
+++ b/solution.py
@@ -71,12 +71,9 @@
     own_ref[...] = frames_ref[...]
 
 
-def near_kernel(carried_ref, own_ref, w_from, part_ref, w_ref, sems):
-    copies = [
-        pltpu.make_async_copy(w_from.at[:, :, c], w_ref.at[:, :, c], sems.at[c]) for c in range(3)
-    ]
-    for copy in copies:
-        copy.start()
+def near_kernel(carried_ref, own_ref, w_ref, part_ref, held_ref):
+    held_ref[:, 0] = w_ref[:, 0]
+    held_ref[:, 1] = w_ref[:, 2]
     blocks = [
         carried_ref[...],
         jnp.concatenate([carried_ref[1:], own_ref[:1]], axis=0),
@@ -87,7 +84,6 @@
         both = jnp.zeros((512, 256), jnp.float32)
         upper = jnp.zeros((256, 256), jnp.float32)
         lower = jnp.zeros((256, 256), jnp.float32)
-        copies[c].wait()
         for a in range(3):
             rows = [blocks[a][:, r].reshape(256, 256) for r in range(2)]
             both += jnp.dot(
@@ -99,16 +95,19 @@
     part_ref[...] = shift_cols(sums[0], 1) + sums[1] + shift_cols(sums[2], -1)
 
 
-def forward_kernel(before_ref, after_ref, own_ref, part_ref, w_ref, cot_ref, out_ref, grad_ref):
+def forward_kernel(near_ref, far_ref, own_ref, part_ref, w_ref, cot_ref, out_ref, grad_ref):
+    even = lax.axis_index("space") % 2 == 0
+    near, far = near_ref[...].reshape(4, 128, 256), far_ref[...].reshape(4, 128, 256)
+    above, below = jnp.where(even, far, near), jnp.where(even, near, far)
     sums = []
     for c in range(3):
         upper = jnp.zeros((256, 256), jnp.float32)
         lower = jnp.zeros((256, 256), jnp.float32)
         for a in range(3):
-            top = before_ref[a : a + 2].reshape(256, 256)
-            bottom = after_ref[a : a + 2].reshape(256, 256)
+            top = above[a : a + 2].reshape(256, 256)
+            bottom = below[a : a + 2].reshape(256, 256)
             upper += jnp.dot(top, w_ref[a, 0, c], preferred_element_type=jnp.float32)
-            lower += jnp.dot(bottom, w_ref[a, 2, c], preferred_element_type=jnp.float32)
+            lower += jnp.dot(bottom, w_ref[a, 1, c], preferred_element_type=jnp.float32)
         sums.append(jnp.concatenate([upper, lower], axis=0).reshape(4, 128, 256))
     total = part_ref[...] + shift_cols(sums[0], 1) + sums[1] + shift_cols(sums[2], -1)
     for row in range(2):
@@ -250,22 +249,20 @@
         jnp.concatenate([carried[:, :1], top], axis=0),
         jnp.concatenate([carried[:, 1:], bottom], axis=0),
     )
-    part = pl.pallas_call(
+    part, held = call(
         near_kernel,
-        out_shape=jax.ShapeDtypeStruct((4, 128, 256), jnp.float32),
-        in_specs=[
-            pl.BlockSpec(memory_space=pltpu.VMEM),
-            pl.BlockSpec(memory_space=pltpu.VMEM),
-            pl.BlockSpec(memory_space=pltpu.HBM),
-        ],
-        scratch_shapes=[
-            pltpu.VMEM((3, 3, 3, 256, 256), jnp.bfloat16),
-            pltpu.SemaphoreType.DMA((3,)),
-        ],
-        compiler_params=pltpu.CompilerParams(vmem_limit_bytes=50 * 1024 * 1024),
-        cost_estimate=pl.CostEstimate(flops=flops, bytes_accessed=5000000, transcendentals=0),
+        (
+            jax.ShapeDtypeStruct((4, 128, 256), jnp.float32),
+            jax.ShapeDtypeStruct((3, 2, 3, 256, 256), jnp.bfloat16),
+        ),
+        flops,
     )(carried, own, weight)
     near, far, part = lax.optimization_barrier((near, far, part))
+    output, grad_pre = call(forward_kernel, (block, block), flops // 3)(
+        near, far, own, part, held, cotangent
+    )
+    near, far, grad_pre = lax.optimization_barrier((near, far, grad_pre))
+    grad_other = flip_core(grad_pre)
     before, after = jnp.where(even, far, near), jnp.where(even, near, far)
     ext = jnp.concatenate(
         [before, jnp.concatenate([carried, own], axis=0), after], axis=1
@@ -273,10 +270,6 @@
     low, high = ext[..., :128], ext[..., 128:]
     mine = jnp.where(core == 0, low, high)
     theirs = flip_core(jnp.where(core == 0, high, low))
-    output, grad_pre = call(forward_kernel, (block, block), flops // 3)(
-        before, after, own, part, weight, cotangent
-    )
-    grad_other = flip_core(grad_pre)
     order = jnp.asarray(row_order(), jnp.bfloat16)
     own_terms = call(own_terms_kernel, jax.ShapeDtypeStruct((768, 1152), jnp.float32), flops // 2)(
         mine, grad_pre, order

time: 95 us -> 95.4 us (level)
  starting transfers between devices: 36 us -> 39.5 us
  Pallas kernels: 14.3 us -> 12 us
  waiting for transfers between devices: 28.2 us -> 26.2 us
    pallas_call x1, Pallas kernels: 3.8 us -> 1.54 us  [local(): call(near_kernel, (jax.ShapeDtypeStruct((4, 128, 256), jnp.float32), jax....]
    all_to_all x2, starting transfers between devices: 20.2 us -> 21.9 us  [exchange(): lax.all_to_all(value, BOTH, 0, 0, tiled=True, axis_index_groups=groups_of...]
    all_to_all x2, waiting for transfers between devices: 20.2 us -> 19 us  [exchange(): lax.all_to_all(value, BOTH, 0, 0, tiled=True, axis_index_groups=groups_of...]
    ppermute x4, starting transfers between devices: 3.67 us -> 4.72 us  [pairs(): return lax.ppermute(value, 'space', links + [(j, i) for i, j in links])]
    ppermute x4, waiting for transfers between devices: 4.22 us -> 3.23 us  [pairs(): return lax.ppermute(value, 'space', links + [(j, i) for i, j in links])]
  transfers between devices with their start and end apart: 11 -> 11, of which waited for: 6 -> 7; matrix products, arithmetic and copies ran while one was open for 0% -> 0% of each run, Pallas kernels for 12% -> 7%
where the time goes in v7:
time: 95.4 us; the launch traced here: 94.9 us
  starting transfers between devices  39.5 us (41%)
  waiting for transfers between devices  26.2 us (27%)
  Pallas kernels  12 us (13%)
  blocking collectives  10.7 us (11%)
  local copies, waits for them, and re-layouts  5.05 us (5%)
    all_to_all x2, starting transfers between devices, exchange(): lax.all_to_all(value, BOTH, 0, 0, tiled=True, axis_index_groups=groups_of...  21.9 us
    all_to_all x2, waiting for transfers between devices, exchange(): lax.all_to_all(value, BOTH, 0, 0, tiled=True, axis_index_groups=groups_of...  19 us
    all_to_all x1, blocking collectives, exchange(): lax.all_to_all(value, BOTH, 0, 0, tiled=True, axis_index_groups=groups_of...  10.7 us
    ppermute x2, starting transfers between devices, shifted(): lax.ppermute(value, axis, [(source, source + steps) for source in range(l...  8.02 us
    unnamed x10, local copies, waits for them, and re-layouts  5.03 us
    ppermute x3, starting transfers between devices, flip_core(): return lax.ppermute(value, 'tm', [(i, i ^ 1) for i in range(16)])  4.9 us
    ppermute x4, starting transfers between devices, pairs(): return lax.ppermute(value, 'space', links + [(j, i) for i, j in links])  4.72 us
    ppermute x4, waiting for transfers between devices, pairs(): return lax.ppermute(value, 'space', links + [(j, i) for i, j in links])  3.23 us
  transfers between devices with their start and end apart: 11, of which 7 were waited for; matrix products, arithmetic and copies ran while one was open for 0% of the time, Pallas kernels for 7%

profile of v7, /device:TPU:1, one launch (start us, length us, event | category | flops | bytes accessed | tf_op | source)
XLA Modules:
  0.0 94.9 jit_solution(11287011458359183659)
XLA Ops:
  0.6 4.6 %collective-permute-start = (bf16[2,2,128,256]{3,2,1,0:T(8,128)(2,1)}, bf16[2,2,128,256]{3,2,1,0:T(8,128)(2,1)S(1)}, u32[]{:S(2)}, u32[]{:S(2)}) collective-permute-start(bf16[2,2,128,256]{3,2,1,0:T(8,128)(2,1)} %frames_ref.1), channel_id=1, source_target_pairs={{0,16},{16,32},{32,48},{48,64},{64,80},{80,96},{96,112},{112,128},... | collective-permute-start | bytes 786440 | tf_op jit(solution)/shard_map/ppermute | solution.py:42
  5.2 0.0 copy-start.1
  5.2 1.0 %copy-done.1 = bf16[2,2,128,256]{3,2,1,0:T(8,128)(2,1)S(1)} copy-done((bf16[2,2,128,256]{3,2,1,0:T(8,128)(2,1)S(1)}, bf16[2,2,128,256]{3,2,1,0:T(8,128)(2,1)}, u32[]{:S(2)}) %copy-start.1) | copy-done | bytes 262168
  6.2 2.6 %collective-permute-done.carried_ref = bf16[2,2,128,256]{3,2,1,0:T(8,128)(2,1)S(1)} collective-permute-done((bf16[2,2,128,256]{3,2,1,0:T(8,128)(2,1)}, bf16[2,2,128,256]{3,2,1,0:T(8,128)(2,1)S(1)}, u32[]{:S(2)}, u32[]{:S(2)}) %collective-permute-start) | collective-permute-done | bytes 262176 | tf_op jit(solution)/shard_map/ppermute | solution.py:42
  8.9 0.1 broadcast_select_fusion.4
  8.9 1.7 %collective-permute-start.1 = (bf16[4,1,128,256]{3,2,1,0:T(8,128)(2,1)S(1)}, bf16[4,1,128,256]{3,2,1,0:T(8,128)(2,1)S(1)}, u32[]{:S(2)}, u32[]{:S(2)}) collective-permute-start(bf16[4,1,128,256]{3,2,1,0:T(8,128)(2,1)S(1)} %get-tuple-element.44), channel_id=1, source_target_pairs={{0,1},{2,3},{4,5},{6,7},{8,9},{10,11},{12,13},{14,15},{1,0},{3,2},... | collective-permute-start | bytes 786440 | tf_op jit(solution)/shard_map/ppermute | solution.py:47
  10.6 0.7 collective-permute-start.2
  11.3 0.0 copy-start.3
  11.3 2.0 %copy-done.3 = bf16[3,3,3,256,256]{4,3,2,1,0:T(8,128)(2,1)S(1)} copy-done((bf16[3,3,3,256,256]{4,3,2,1,0:T(8,128)(2,1)S(1)}, bf16[3,3,3,256,256]{4,3,2,1,0:T(8,128)(2,1)}, u32[]{:S(2)}) %copy-start.3) | copy-done | bytes 3538968
  13.3 0.0 copy-start.2
  13.3 1.5 %shard_map.68 = (f32[4,128,256]{2,1,0:T(8,128)S(1)}, bf16[3,2,3,256,256]{4,3,2,1,0:T(8,128)(2,1)S(1)}) custom-call(bf16[2,2,128,256]{3,2,1,0:T(8,128)(2,1)S(1)} %collective-permute-done.carried_ref, bf16[2,2,128,256]{3,2,1,0:T(8,128)(2,1)S(1)} %get-tuple-element.23.own_ref, bf16[3,3,3,256,256]{4,3,2,1,0:T(8,128)(2,1)S(1)} %copy-done.3), custom_call_target="tpu_custom_call" | custom-call | flops 1811939328 | bytes 5000000 | tf_op jit(solution)/shard_map/pallas_call | solution.py:252
  14.9 0.3 collective-permute-done.1.near_ref
  15.2 0.0 collective-permute-done.2.far_ref
  15.2 0.0 copy-done.2
  15.2 1.8 %shard_map.69 = (bf16[2,2,128,256]{3,2,1,0:T(8,128)(2,1)}, bf16[2,2,128,256]{3,2,1,0:T(8,128)(2,1)S(1)}) custom-call(bf16[4,1,128,256]{3,2,1,0:T(8,128)(2,1)S(1)} %collective-permute-done.1.near_ref, bf16[4,1,128,256]{3,2,1,0:T(8,128)(2,1)S(1)} %collective-permute-done.2.far_ref, bf16[2,2,128,256]{3,2,1,0:T(8,128)(2,1)S(1)} %get-tuple-element.23.own_ref, ...), custom_call_target="tpu_custom_call" | custom-call | flops 603979776 | bytes 5000000 | tf_op jit(solution)/shard_map/pallas_call | solution.py:261
  17.0 0.0 copy-start
  17.0 0.1 pad_maximum_fusion
  17.1 0.1 broadcast_select_fusion
  17.2 0.1 collective-permute-start.3
  17.3 0.5 collective-permute-start.4
  17.8 0.1 copy-done
  17.9 1.4 %shard_map.70.part_ref = f32[768,1152]{1,0:T(8,128)S(1)} custom-call(bf16[4,4,128,128]{3,2,1,0:T(8,128)(2,1)S(1)} %get-tuple-element.39.cells_ref, bf16[2,2,128,256]{3,2,1,0:T(8,128)(2,1)S(1)} %get-tuple-element.33.grad_ref, bf16[256,256]{1,0:T(8,128)(2,1)S(1)} %copy-done), custom_call_target="tpu_custom_call" | custom-call | flops 905969664 | bytes 5000000 | tf_op jit(solution)/shard_map/pallas_call | solution.py:274
  19.3 0.3 collective-permute-done.4.grad_ref
  19.6 0.0 collective-permute-done.3.cells_ref
  19.6 2.4 %shard_map.71 = bf16[256,3456]{1,0:T(8,128)(2,1)} custom-call(bf16[4,4,128,128]{3,2,1,0:T(8,128)(2,1)S(1)} %collective-permute-done.3.cells_ref, bf16[2,2,128,256]{3,2,1,0:T(8,128)(2,1)S(1)} %collective-permute-done.4.grad_ref, bf16[256,256]{1,0:T(8,128)(2,1)S(1)} %copy-done, f32[768,1152]{1,0:T(8,128)S(1)} %shard_map.70.part_ref), custom_call_target="tpu_custom_call" | custom-call | flops 905969664 | bytes 5000000 | tf_op jit(solution)/shard_map/pallas_call | solution.py:277
  22.0 15.5 %all-to-all-start = ((bf16[16,16,3456]{2,1,0:T(8,128)(2,1)}), bf16[16,16,3456]{2,1,0:T(8,128)(2,1)S(1)}, u32[]{:S(2)}, u32[]{:S(2)}) async-start(bf16[16,16,3456]{2,1,0:T(8,128)(2,1)} %bitcast), calls=%async_computation | async-start | bytes 3538944 | tf_op jit(solution)/shard_map/all_to_all | solution.py:32
  37.5 0.7 collective-permute-start.5
  38.2 1.7 %collective-permute-start.6 = (bf16[2,1,128,256]{3,2,1,0:T(8,128)(2,1)S(1)}, bf16[2,1,128,256]{3,2,1,0:T(8,128)(2,1)S(1)}, u32[]{:S(2)}, u32[]{:S(2)}) collective-permute-start(bf16[2,1,128,256]{3,2,1,0:T(8,128)(2,1)S(1)} %get-tuple-element.48), channel_id=1, source_target_pairs={{0,1},{2,3},{4,5},{6,7},{8,9},{10,11},{12,13},{14,15},{1,0},{3,2},... | collective-permute-start | bytes 393224 | tf_op jit(solution)/shard_map/ppermute | solution.py:47
  39.9 0.0 collective-permute-done.5
  39.9 2.9 %collective-permute-done.6 = bf16[2,1,128,256]{3,2,1,0:T(8,128)(2,1)S(1)} collective-permute-done((bf16[2,1,128,256]{3,2,1,0:T(8,128)(2,1)S(1)}, bf16[2,1,128,256]{3,2,1,0:T(8,128)(2,1)S(1)}, u32[]{:S(2)}, u32[]{:S(2)}) %collective-permute-start.6) | collective-permute-done | bytes 131104 | tf_op jit(solution)/shard_map/ppermute | solution.py:47
  42.8 0.1 pad_maximum_fusion.2
  42.9 3.4 %collective-permute-start.7 = (bf16[2,4,128,256]{3,2,1,0:T(8,128)(2,1)S(1)}, bf16[2,4,128,256]{3,2,1,0:T(8,128)(2,1)S(1)}, u32[]{:S(2)}, u32[]{:S(2)}) collective-permute-start(bf16[2,4,128,256]{3,2,1,0:T(8,128)(2,1)S(1)} %pad_maximum_fusion.2), channel_id=1, source_target_pairs={{16,0},{32,16},{48,32},{64,48},{80,64},{96,80},{112,96},{128,112},... | collective-permute-start | bytes 1572872 | tf_op jit(solution)/shard_map/ppermute | solution.py:42
  46.3 16.5 %all-to-all-done.got_ref = bf16[16,16,3456]{2,1,0:T(8,128)(2,1)S(1)} async-done(((bf16[16,16,3456]{2,1,0:T(8,128)(2,1)}), bf16[16,16,3456]{2,1,0:T(8,128)(2,1)S(1)}, u32[]{:S(2)}, u32[]{:S(2)}) %all-to-all-start) | async-done | bytes 1769504 | tf_op jit(solution)/shard_map/all_to_all | solution.py:32
  62.8 0.5 shard_map.72
  63.3 10.7 %all_to_all.19.got_ref = bf16[8,2,3456]{2,1,0:T(2,128)(2,1)S(1)} all-to-all(bf16[8,2,3456]{2,1,0:T(2,128)(2,1)S(1)} %shard_map.72), channel_id=1, replica_groups={{0,1,2,3,4,5,6,7},{8,9,10,11,12,13,14,15},{16,17,18,19,20,21,22,23},{24..., dimensions={0} | all-to-all | bytes 221184 | tf_op jit(solution)/shard_map/all_to_all | solution.py:32
  74.0 0.7 shard_map.73
  74.8 0.0 collective-permute-done.7
  74.8 6.4 %all-to-all-start.2 = ((f32[8,2,3456]{2,1,0:T(2,128)}), f32[8,2,3456]{2,1,0:T(2,128)S(1)}, u32[]{:S(2)}, u32[]{:S(2)}) async-start(f32[8,2,3456]{2,1,0:T(2,128)} %shard_map.73), calls=%async_computation.2 | async-start | bytes 442368 | tf_op jit(solution)/shard_map/all_to_all | solution.py:32
  81.2 0.1 pad_maximum_fusion.1.ext_ref
  81.3 0.0 copy-start.4
  81.3 2.0 %copy-done.4 = bf16[3,3,3,256,256]{4,3,2,1,0:T(8,128)(2,1)S(1)} copy-done((bf16[3,3,3,256,256]{4,3,2,1,0:T(8,128)(2,1)S(1)}, bf16[3,3,3,256,256]{4,3,2,1,0:T(8,128)(2,1)}, u32[]{:S(2)}) %copy-start.4) | copy-done | bytes 3538968
  83.3 2.7 %shard_map.74 = bf16[2,2,128,256]{3,2,1,0:T(8,128)(2,1)} custom-call(bf16[4,4,128,256]{3,2,1,0:T(8,128)(2,1)S(1)} %pad_maximum_fusion.1.ext_ref, bf16[3,3,3,256,256]{4,3,2,1,0:T(8,128)(2,1)S(1)} %copy-done.4, bf16[2,2,128,256]{3,2,1,0:T(8,128)(2,1)S(1)} %copy-done.2), custom_call_target="tpu_custom_call" | custom-call | flops 1811939328 | bytes 5000000 | tf_op jit(solution)/shard_map/pallas_call | solution.py:303
  86.0 2.6 %all-to-all-done.2.mine_ref = f32[8,2,3456]{2,1,0:T(2,128)S(1)} async-done(((f32[8,2,3456]{2,1,0:T(2,128)}), f32[8,2,3456]{2,1,0:T(2,128)S(1)}, u32[]{:S(2)}, u32[]{:S(2)}) %all-to-all-start.2) | async-done | bytes 221216 | tf_op jit(solution)/shard_map/all_to_all | solution.py:32
  88.6 4.3 %collective-permute-start.8 = (f32[8,2,3456]{2,1,0:T(2,128)S(1)}, f32[8,2,3456]{2,1,0:T(2,128)S(1)}, u32[]{:S(2)}, u32[]{:S(2)}) collective-permute-start(f32[8,2,3456]{2,1,0:T(2,128)S(1)} %all-to-all-done.2.mine_ref), channel_id=1, source_target_pairs={{0,16},{16,0},{32,48},{48,32},{64,80},{80,64},{96,112},{112,96},{1... | collective-permute-start | bytes 663560 | tf_op jit(solution)/shard_map/ppermute | solution.py:36
  92.9 1.1 %collective-permute-done.8.other_ref = f32[8,2,3456]{2,1,0:T(2,128)S(1)} collective-permute-done((f32[8,2,3456]{2,1,0:T(2,128)S(1)}, f32[8,2,3456]{2,1,0:T(2,128)S(1)}, u32[]{:S(2)}, u32[]{:S(2)}) %collective-permute-start.8) | collective-permute-done | bytes 221216 | tf_op jit(solution)/shard_map/ppermute | solution.py:36
  94.0 0.9 shard_map.75
  (5 shorter events, 0.1 us)
Async XLA Ops:
  0.6 8.2 %collective-permute-start = (bf16[2,2,128,256]{3,2,1,0:T(8,128)(2,1)}, bf16[2,2,128,256]{3,2,1,0:T(8,128)(2,1)S(1)}, u32[]{:S(2)}, u32[]{:S(2)}) collective-permute-start(bf16[2,2,128,256]{3,2,1,0:T(8,128)(2,1)} %frames_ref.1), channel_id=1, source_target_pairs={{0,16},{16,32},{32,48},{48,64},{64,80},{80,96},{96,112},{112,128},... | collective-permute-start | bytes 786440 | tf_op jit(solution)/shard_map/ppermute | solution.py:42
  5.2 1.0 %copy-start.1 = (bf16[2,2,128,256]{3,2,1,0:T(8,128)(2,1)S(1)}, bf16[2,2,128,256]{3,2,1,0:T(8,128)(2,1)}, u32[]{:S(2)}) copy-start(bf16[2,2,128,256]{3,2,1,0:T(8,128)(2,1)} %frames_ref.1) | copy-start | bytes 786436
  8.9 6.3 %collective-permute-start.1 = (bf16[4,1,128,256]{3,2,1,0:T(8,128)(2,1)S(1)}, bf16[4,1,128,256]{3,2,1,0:T(8,128)(2,1)S(1)}, u32[]{:S(2)}, u32[]{:S(2)}) collective-permute-start(bf16[4,1,128,256]{3,2,1,0:T(8,128)(2,1)S(1)} %get-tuple-element.44), channel_id=1, source_target_pairs={{0,1},{2,3},{4,5},{6,7},{8,9},{10,11},{12,13},{14,15},{1,0},{3,2},... | collective-permute-start | bytes 786440 | tf_op jit(solution)/shard_map/ppermute | solution.py:47
  10.6 4.5 %collective-permute-start.2 = (bf16[4,1,128,256]{3,2,1,0:T(8,128)(2,1)S(1)}, bf16[4,1,128,256]{3,2,1,0:T(8,128)(2,1)S(1)}, u32[]{:S(2)}, u32[]{:S(2)}) collective-permute-start(bf16[4,1,128,256]{3,2,1,0:T(8,128)(2,1)S(1)} %get-tuple-element.43), channel_id=1, source_target_pairs={{1,2},{3,4},{5,6},{7,8},{9,10},{11,12},{13,14},{2,1},{4,3},{6,5},{... | collective-permute-start | bytes 786440 | tf_op jit(solution)/shard_map/ppermute | solution.py:47
  11.3 2.0 %copy-start.3 = (bf16[3,3,3,256,256]{4,3,2,1,0:T(8,128)(2,1)S(1)}, bf16[3,3,3,256,256]{4,3,2,1,0:T(8,128)(2,1)}, u32[]{:S(2)}) copy-start(bf16[3,3,3,256,256]{4,3,2,1,0:T(8,128)(2,1)} %w_ref.3) | copy-start | bytes 10616836
  13.3 1.8 %copy-start.2 = (bf16[2,2,128,256]{3,2,1,0:T(8,128)(2,1)S(1)}, bf16[2,2,128,256]{3,2,1,0:T(8,128)(2,1)}, u32[]{:S(2)}) copy-start(bf16[2,2,128,256]{3,2,1,0:T(8,128)(2,1)} %cot_ref.3) | copy-start | bytes 786436
  17.0 0.9 copy-start
  17.2 2.4 %collective-permute-start.3 = (bf16[4,4,128,128]{3,2,1,0:T(8,128)(2,1)S(1)}, bf16[4,4,128,128]{3,2,1,0:T(8,128)(2,1)S(1)}, u32[]{:S(2)}, u32[]{:S(2)}) collective-permute-start(bf16[4,4,128,128]{3,2,1,0:T(8,128)(2,1)S(1)} %get-tuple-element.40), channel_id=1, source_target_pairs={{0,16},{16,0},{32,48},{48,32},{64,80},{80,64},{96,112},{112,96},{1... | collective-permute-start | bytes 1572872 | tf_op jit(solution)/shard_map/ppermute | solution.py:36
  17.3 2.3 %collective-permute-start.4 = (bf16[2,2,128,256]{3,2,1,0:T(8,128)(2,1)S(1)}, bf16[2,2,128,256]{3,2,1,0:T(8,128)(2,1)S(1)}, u32[]{:S(2)}, u32[]{:S(2)}) collective-permute-start(bf16[2,2,128,256]{3,2,1,0:T(8,128)(2,1)S(1)} %get-tuple-element.33.grad_ref), channel_id=1, source_target_pairs={{0,16},{16,0},{32,48},{48,32},{64,80},{80,64},{96,112},{112,96},{1... | collective-permute-start | bytes 786440 | tf_op jit(solution)/shard_map/ppermute | solution.py:36
  22.0 40.8 %all-to-all-start = ((bf16[16,16,3456]{2,1,0:T(8,128)(2,1)}), bf16[16,16,3456]{2,1,0:T(8,128)(2,1)S(1)}, u32[]{:S(2)}, u32[]{:S(2)}) async-start(bf16[16,16,3456]{2,1,0:T(8,128)(2,1)} %bitcast), calls=%async_computation | async-start | bytes 3538944 | tf_op jit(solution)/shard_map/all_to_all | solution.py:32
  37.5 2.3 %collective-permute-start.5 = (bf16[2,1,128,256]{3,2,1,0:T(8,128)(2,1)S(1)}, bf16[2,1,128,256]{3,2,1,0:T(8,128)(2,1)S(1)}, u32[]{:S(2)}, u32[]{:S(2)}) collective-permute-start(bf16[2,1,128,256]{3,2,1,0:T(8,128)(2,1)S(1)} %get-tuple-element.47), channel_id=1, source_target_pairs={{1,2},{3,4},{5,6},{7,8},{9,10},{11,12},{13,14},{2,1},{4,3},{6,5},{... | collective-permute-start | bytes 393224 | tf_op jit(solution)/shard_map/ppermute | solution.py:47
  38.2 4.6 %collective-permute-start.6 = (bf16[2,1,128,256]{3,2,1,0:T(8,128)(2,1)S(1)}, bf16[2,1,128,256]{3,2,1,0:T(8,128)(2,1)S(1)}, u32[]{:S(2)}, u32[]{:S(2)}) collective-permute-start(bf16[2,1,128,256]{3,2,1,0:T(8,128)(2,1)S(1)} %get-tuple-element.48), channel_id=1, source_target_pairs={{0,1},{2,3},{4,5},{6,7},{8,9},{10,11},{12,13},{14,15},{1,0},{3,2},... | collective-permute-start | bytes 393224 | tf_op jit(solution)/shard_map/ppermute | solution.py:47
  42.9 31.8 %collective-permute-start.7 = (bf16[2,4,128,256]{3,2,1,0:T(8,128)(2,1)S(1)}, bf16[2,4,128,256]{3,2,1,0:T(8,128)(2,1)S(1)}, u32[]{:S(2)}, u32[]{:S(2)}) collective-permute-start(bf16[2,4,128,256]{3,2,1,0:T(8,128)(2,1)S(1)} %pad_maximum_fusion.2), channel_id=1, source_target_pairs={{16,0},{32,16},{48,32},{64,48},{80,64},{96,80},{112,96},{128,112},... | collective-permute-start | bytes 1572872 | tf_op jit(solution)/shard_map/ppermute | solution.py:42
  74.8 13.8 %all-to-all-start.2 = ((f32[8,2,3456]{2,1,0:T(2,128)}), f32[8,2,3456]{2,1,0:T(2,128)S(1)}, u32[]{:S(2)}, u32[]{:S(2)}) async-start(f32[8,2,3456]{2,1,0:T(2,128)} %shard_map.73), calls=%async_computation.2 | async-start | bytes 442368 | tf_op jit(solution)/shard_map/all_to_all | solution.py:32
  81.3 2.0 %copy-start.4 = (bf16[3,3,3,256,256]{4,3,2,1,0:T(8,128)(2,1)S(1)}, bf16[3,3,3,256,256]{4,3,2,1,0:T(8,128)(2,1)}, u32[]{:S(2)}) copy-start(bf16[3,3,3,256,256]{4,3,2,1,0:T(8,128)(2,1)} %w_ref.3) | copy-start | bytes 10616836
  88.6 5.4 %collective-permute-start.8 = (f32[8,2,3456]{2,1,0:T(2,128)S(1)}, f32[8,2,3456]{2,1,0:T(2,128)S(1)}, u32[]{:S(2)}, u32[]{:S(2)}) collective-permute-start(f32[8,2,3456]{2,1,0:T(2,128)S(1)} %all-to-all-done.2.mine_ref), channel_id=1, source_target_pairs={{0,16},{16,0},{32,48},{48,32},{64,80},{80,64},{96,112},{112,96},{1... | collective-permute-start | bytes 663560 | tf_op jit(solution)/shard_map/ppermute | solution.py:36

commit v8 on v7

--- a/solution.py
+++ b/solution.py
@@ -120,22 +120,58 @@
         grad_ref[:, row] = grad.astype(jnp.bfloat16)
 
 
-def backward_kernel(ext_ref, w_ref, cot_ref, out_ref):
+def back_terms(tall_ref, w_ref, whole, single, source, to):
     sums = []
     for c in range(3):
         acc = jnp.zeros((512, 256), jnp.float32)
-        for a in range(3):
-            for b in range(3):
-                acc += lax.dot_general(
-                    block_of(ext_ref, 2 - a, 2 - b),
-                    w_ref[a, b, c],
-                    (((1,), (1,)), ((), ())),
-                    preferred_element_type=jnp.float32,
-                )
-        sums.append(acc.reshape(4, 128, 256))
+        one = jnp.zeros((256, 256), jnp.float32)
+        for b in range(3):
+            block = tall_ref[:, 2 - b : 4 - b]
+            acc += lax.dot_general(
+                block.reshape(512, 256),
+                w_ref[whole, b, c],
+                (((1,), (1,)), ((), ())),
+                preferred_element_type=jnp.float32,
+            )
+            one += lax.dot_general(
+                block[source].reshape(256, 256),
+                w_ref[single, b, c],
+                (((1,), (1,)), ((), ())),
+                preferred_element_type=jnp.float32,
+            )
+        halves = [acc[:256], acc[256:]]
+        halves[to] += one
+        sums.append(jnp.concatenate(halves, axis=0).reshape(4, 128, 256))
     total = shift_cols(sums[0], -1) + sums[1] + shift_cols(sums[2], 1)
-    cot = cot_ref[...].reshape(4, 128, 256).astype(jnp.float32)
-    out_ref[...] = (cot + total).astype(jnp.bfloat16).reshape(2, 2, 128, 256)
+    return total.reshape(2, 2, 128, 256)
+
+
+def earlier_kernel(tall_ref, w_from, out_ref, w_ref, sem):
+    copy = pltpu.make_async_copy(w_from.at[0:2], w_ref, sem)
+    copy.start()
+    copy.wait()
+    out_ref[...] = back_terms(tall_ref, w_ref, 0, 1, 0, 1).astype(jnp.bfloat16)
+
+
+def backward_kernel(tall_ref, later_ref, w_from, cot_ref, out_ref, w_ref, sem):
+    copy = pltpu.make_async_copy(w_from.at[1:3], w_ref, sem)
+    copy.start()
+    copy.wait()
+    total = back_terms(tall_ref, w_ref, 1, 0, 1, 0) + later_ref[...].astype(jnp.float32)
+    out_ref[...] = (cot_ref[...].astype(jnp.float32) + total).astype(jnp.bfloat16)
+
+
+def call_back(kernel, n_before, n_after, flops):
+    on_chip = pl.BlockSpec(memory_space=pltpu.VMEM)
+    weights = pl.BlockSpec(memory_space=pltpu.HBM)
+    return pl.pallas_call(
+        kernel,
+        out_shape=jax.ShapeDtypeStruct((2, 2, 128, 256), jnp.bfloat16),
+        in_specs=[on_chip] * n_before + [weights] + [on_chip] * n_after,
+        scratch_shapes=[pltpu.VMEM((2, 3, 3, 256, 256), jnp.bfloat16), pltpu.SemaphoreType.DMA],
+        compiler_params=pltpu.CompilerParams(vmem_limit_bytes=50 * 1024 * 1024),
+        cost_estimate=pl.CostEstimate(flops=flops, bytes_accessed=5000000, transcendentals=0),
+    )
 
 
 def turned_grad(grad_ref, order_ref):
@@ -285,7 +321,8 @@
     near, far = row_halo(grad_pre[:, :1], grad_pre[:, 1:])
     above, below = jnp.where(even, far, near), jnp.where(even, near, far)
     tall = jnp.concatenate([above, grad_pre, below], axis=1)
-    follow = shifted(tall, "tm", -1)
+    earlier = call_back(earlier_kernel, 1, 0, flops // 2)(tall, weight)
+    follow = shifted(earlier, "tm", -1)
     got = exchange(terms, ("x_lo", "x_hi", "y")).reshape(16, 16, 3456)
     plane = pl.pallas_call(
         plane_kernel,
@@ -298,9 +335,10 @@
     got = exchange(plane, ("z",)).reshape(8, 2, 3456)
     copies = call(line_kernel, jax.ShapeDtypeStruct((8, 2, 3456), jnp.float32), 100000)(got)
     copies, tall, follow = lax.optimization_barrier((copies, tall, follow))
-    grad_ext = jnp.concatenate([tall, follow], axis=0)
     share = exchange(copies, ("x_hi", "y")).reshape(8, 2, 3456)
-    grad_input = call(backward_kernel, block, flops)(grad_ext, weight, cotangent)
+    grad_input = call_back(backward_kernel, 2, 1, flops // 2)(
+        tall, follow, weight, cotangent
+    )
     share, grad_input = lax.optimization_barrier((share, grad_input))
     other = flip_core(share)
     share = call(share_kernel, jax.ShapeDtypeStruct((27, 16, 256), jnp.float32), 100000)(

time: 95.4 us -> 95.5 us (level)
  Pallas kernels: 12 us -> 15.6 us
  local copies, waits for them, and re-layouts: 5.05 us -> 3.05 us
  waiting for transfers between devices: 26.2 us -> 24.7 us
    pallas_call x1 -> x2, Pallas kernels: 2.73 us -> 6.32 us  [the longest x1 3.53 us: local(): call_back(backward_kernel, 2, 1, flops // 2)]
    unnamed x10 -> x8, local copies, waits for them, and re-layouts: 5.03 us -> 3.03 us
    all_to_all x2, waiting for transfers between devices: 19 us -> 17.5 us  [exchange(): lax.all_to_all(value, BOTH, 0, 0, tiled=True, axis_index_groups=groups_of...]
  transfers between devices with their start and end apart: 11 -> 11, of which waited for: 7 -> 7; matrix products, arithmetic and copies ran while one was open for 0% -> 0% of each run, Pallas kernels for 7% -> 11%
where the time goes in v8:
time: 95.5 us; the launch traced here: 94.9 us
  starting transfers between devices  39.5 us (41%)
  waiting for transfers between devices  24.7 us (26%)
  Pallas kernels  15.6 us (16%)
  blocking collectives  10.7 us (11%)
  local copies, waits for them, and re-layouts  3.05 us (3%)
    all_to_all x2, starting transfers between devices, exchange(): lax.all_to_all(value, BOTH, 0, 0, tiled=True, axis_index_groups=groups_of...  21.9 us
    all_to_all x2, waiting for transfers between devices, exchange(): lax.all_to_all(value, BOTH, 0, 0, tiled=True, axis_index_groups=groups_of...  17.5 us
    all_to_all x1, blocking collectives, exchange(): lax.all_to_all(value, BOTH, 0, 0, tiled=True, axis_index_groups=groups_of...  10.7 us
    ppermute x2, starting transfers between devices, shifted(): lax.ppermute(value, axis, [(source, source + steps) for source in range(l...  8.02 us
    ppermute x3, starting transfers between devices, flip_core(): return lax.ppermute(value, 'tm', [(i, i ^ 1) for i in range(16)])  4.9 us
    ppermute x4, starting transfers between devices, pairs(): return lax.ppermute(value, 'space', links + [(j, i) for i, j in links])  4.72 us
    pallas_call x1, Pallas kernels, local(): call_back(backward_kernel, 2, 1, flops // 2)  3.53 us
    ppermute x4, waiting for transfers between devices, pairs(): return lax.ppermute(value, 'space', links + [(j, i) for i, j in links])  3.23 us
  transfers between devices with their start and end apart: 11, of which 7 were waited for; matrix products, arithmetic and copies ran while one was open for 0% of the time, Pallas kernels for 11%

profile of v8, /device:TPU:1, one launch (start us, length us, event | category | flops | bytes accessed | tf_op | source)
XLA Modules:
  0.0 94.9 jit_solution(754088918127452949)
XLA Ops:
  0.6 4.6 %collective-permute-start = (bf16[2,2,128,256]{3,2,1,0:T(8,128)(2,1)}, bf16[2,2,128,256]{3,2,1,0:T(8,128)(2,1)S(1)}, u32[]{:S(2)}, u32[]{:S(2)}) collective-permute-start(bf16[2,2,128,256]{3,2,1,0:T(8,128)(2,1)} %frames_ref.1), channel_id=1, source_target_pairs={{0,16},{16,32},{32,48},{48,64},{64,80},{80,96},{96,112},{112,128},... | collective-permute-start | bytes 786440 | tf_op jit(solution)/shard_map/ppermute | solution.py:42
  5.2 0.0 copy-start.3
  5.2 1.0 %copy-done.3 = bf16[2,2,128,256]{3,2,1,0:T(8,128)(2,1)S(1)} copy-done((bf16[2,2,128,256]{3,2,1,0:T(8,128)(2,1)S(1)}, bf16[2,2,128,256]{3,2,1,0:T(8,128)(2,1)}, u32[]{:S(2)}) %copy-start.3) | copy-done | bytes 262168
  6.2 2.6 %collective-permute-done.carried_ref = bf16[2,2,128,256]{3,2,1,0:T(8,128)(2,1)S(1)} collective-permute-done((bf16[2,2,128,256]{3,2,1,0:T(8,128)(2,1)}, bf16[2,2,128,256]{3,2,1,0:T(8,128)(2,1)S(1)}, u32[]{:S(2)}, u32[]{:S(2)}) %collective-permute-start) | collective-permute-done | bytes 262176 | tf_op jit(solution)/shard_map/ppermute | solution.py:42
  8.9 0.1 broadcast_select_fusion.4
  8.9 1.7 %collective-permute-start.1 = (bf16[4,1,128,256]{3,2,1,0:T(8,128)(2,1)S(1)}, bf16[4,1,128,256]{3,2,1,0:T(8,128)(2,1)S(1)}, u32[]{:S(2)}, u32[]{:S(2)}) collective-permute-start(bf16[4,1,128,256]{3,2,1,0:T(8,128)(2,1)S(1)} %get-tuple-element.44), channel_id=1, source_target_pairs={{0,1},{2,3},{4,5},{6,7},{8,9},{10,11},{12,13},{14,15},{1,0},{3,2},... | collective-permute-start | bytes 786440 | tf_op jit(solution)/shard_map/ppermute | solution.py:47
  10.6 0.7 collective-permute-start.2
  11.3 0.0 copy-start
  11.3 2.0 %copy-done = bf16[3,3,3,256,256]{4,3,2,1,0:T(8,128)(2,1)S(1)} copy-done((bf16[3,3,3,256,256]{4,3,2,1,0:T(8,128)(2,1)S(1)}, bf16[3,3,3,256,256]{4,3,2,1,0:T(8,128)(2,1)}, u32[]{:S(2)}) %copy-start) | copy-done | bytes 3538968
  13.3 0.0 copy-start.1
  13.3 1.5 %shard_map.68 = (f32[4,128,256]{2,1,0:T(8,128)S(1)}, bf16[3,2,3,256,256]{4,3,2,1,0:T(8,128)(2,1)S(1)}) custom-call(bf16[2,2,128,256]{3,2,1,0:T(8,128)(2,1)S(1)} %collective-permute-done.carried_ref, bf16[2,2,128,256]{3,2,1,0:T(8,128)(2,1)S(1)} %get-tuple-element.23.own_ref, bf16[3,3,3,256,256]{4,3,2,1,0:T(8,128)(2,1)S(1)} %copy-done), custom_call_target="tpu_custom_call" | custom-call | flops 1811939328 | bytes 5000000 | tf_op jit(solution)/shard_map/pallas_call | solution.py:288
  14.9 0.3 collective-permute-done.1.near_ref
  15.2 0.0 collective-permute-done.2.far_ref
  15.2 0.0 copy-done.1
  15.2 1.8 %shard_map.69 = (bf16[2,2,128,256]{3,2,1,0:T(8,128)(2,1)}, bf16[2,2,128,256]{3,2,1,0:T(8,128)(2,1)S(1)}) custom-call(bf16[4,1,128,256]{3,2,1,0:T(8,128)(2,1)S(1)} %collective-permute-done.1.near_ref, bf16[4,1,128,256]{3,2,1,0:T(8,128)(2,1)S(1)} %collective-permute-done.2.far_ref, bf16[2,2,128,256]{3,2,1,0:T(8,128)(2,1)S(1)} %get-tuple-element.23.own_ref, ...), custom_call_target="tpu_custom_call" | custom-call | flops 603979776 | bytes 5000000 | tf_op jit(solution)/shard_map/pallas_call | solution.py:297
  17.0 0.0 copy-start.2
  17.0 0.1 pad_maximum_fusion
  17.1 0.1 broadcast_select_fusion
  17.2 0.1 collective-permute-start.3
  17.3 0.5 collective-permute-start.4
  17.8 0.1 copy-done.2
  17.9 1.4 %shard_map.70.part_ref = f32[768,1152]{1,0:T(8,128)S(1)} custom-call(bf16[4,4,128,128]{3,2,1,0:T(8,128)(2,1)S(1)} %get-tuple-element.39.cells_ref, bf16[2,2,128,256]{3,2,1,0:T(8,128)(2,1)S(1)} %get-tuple-element.33.grad_ref, bf16[256,256]{1,0:T(8,128)(2,1)S(1)} %copy-done.2), custom_call_target="tpu_custom_call" | custom-call | flops 905969664 | bytes 5000000 | tf_op jit(solution)/shard_map/pallas_call | solution.py:310
  19.3 0.3 collective-permute-done.4.grad_ref
  19.6 0.0 collective-permute-done.3.cells_ref
  19.6 2.4 %shard_map.71 = bf16[256,3456]{1,0:T(8,128)(2,1)} custom-call(bf16[4,4,128,128]{3,2,1,0:T(8,128)(2,1)S(1)} %collective-permute-done.3.cells_ref, bf16[2,2,128,256]{3,2,1,0:T(8,128)(2,1)S(1)} %collective-permute-done.4.grad_ref, bf16[256,256]{1,0:T(8,128)(2,1)S(1)} %copy-done.2, f32[768,1152]{1,0:T(8,128)S(1)} %shard_map.70.part_ref), custom_call_target="tpu_custom_call" | custom-call | flops 905969664 | bytes 5000000 | tf_op jit(solution)/shard_map/pallas_call | solution.py:313
  22.0 15.5 %all-to-all-start = ((bf16[16,16,3456]{2,1,0:T(8,128)(2,1)}), bf16[16,16,3456]{2,1,0:T(8,128)(2,1)S(1)}, u32[]{:S(2)}, u32[]{:S(2)}) async-start(bf16[16,16,3456]{2,1,0:T(8,128)(2,1)} %bitcast), calls=%async_computation | async-start | bytes 3538944 | tf_op jit(solution)/shard_map/all_to_all | solution.py:32
  37.6 0.7 collective-permute-start.5
  38.3 1.7 %collective-permute-start.6 = (bf16[2,1,128,256]{3,2,1,0:T(8,128)(2,1)S(1)}, bf16[2,1,128,256]{3,2,1,0:T(8,128)(2,1)S(1)}, u32[]{:S(2)}, u32[]{:S(2)}) collective-permute-start(bf16[2,1,128,256]{3,2,1,0:T(8,128)(2,1)S(1)} %get-tuple-element.48), channel_id=1, source_target_pairs={{0,1},{2,3},{4,5},{6,7},{8,9},{10,11},{12,13},{14,15},{1,0},{3,2},... | collective-permute-start | bytes 393224 | tf_op jit(solution)/shard_map/ppermute | solution.py:47
  39.9 0.0 collective-permute-done.5
  39.9 2.9 %collective-permute-done.6 = bf16[2,1,128,256]{3,2,1,0:T(8,128)(2,1)S(1)} collective-permute-done((bf16[2,1,128,256]{3,2,1,0:T(8,128)(2,1)S(1)}, bf16[2,1,128,256]{3,2,1,0:T(8,128)(2,1)S(1)}, u32[]{:S(2)}, u32[]{:S(2)}) %collective-permute-start.6) | collective-permute-done | bytes 131104 | tf_op jit(solution)/shard_map/ppermute | solution.py:47
  42.9 0.1 pad_maximum_fusion.1.tall_ref
  43.0 2.8 %shard_map.74 = bf16[2,2,128,256]{3,2,1,0:T(8,128)(2,1)S(1)} custom-call(bf16[2,4,128,256]{3,2,1,0:T(8,128)(2,1)S(1)} %pad_maximum_fusion.1.tall_ref, bf16[3,3,3,256,256]{4,3,2,1,0:T(8,128)(2,1)} %w_from.3), custom_call_target="tpu_custom_call" | custom-call | flops 905969664 | bytes 5000000 | tf_op jit(solution)/shard_map/pallas_call | solution.py:324
  45.8 3.4 %collective-permute-start.7 = (bf16[2,2,128,256]{3,2,1,0:T(8,128)(2,1)S(1)}, bf16[2,2,128,256]{3,2,1,0:T(8,128)(2,1)S(1)}, u32[]{:S(2)}, u32[]{:S(2)}) collective-permute-start(bf16[2,2,128,256]{3,2,1,0:T(8,128)(2,1)S(1)} %shard_map.74), channel_id=1, source_target_pairs={{16,0},{32,16},{48,32},{64,48},{80,64},{96,80},{112,96},{128,112},... | collective-permute-start | bytes 786440 | tf_op jit(solution)/shard_map/ppermute | solution.py:42
  49.2 13.6 %all-to-all-done.got_ref = bf16[16,16,3456]{2,1,0:T(8,128)(2,1)S(1)} async-done(((bf16[16,16,3456]{2,1,0:T(8,128)(2,1)}), bf16[16,16,3456]{2,1,0:T(8,128)(2,1)S(1)}, u32[]{:S(2)}, u32[]{:S(2)}) %all-to-all-start) | async-done | bytes 1769504 | tf_op jit(solution)/shard_map/all_to_all | solution.py:32
  62.8 0.5 shard_map.72
  63.3 10.7 %all_to_all.19.got_ref = bf16[8,2,3456]{2,1,0:T(2,128)(2,1)S(1)} all-to-all(bf16[8,2,3456]{2,1,0:T(2,128)(2,1)S(1)} %shard_map.72), channel_id=1, replica_groups={{0,1,2,3,4,5,6,7},{8,9,10,11,12,13,14,15},{16,17,18,19,20,21,22,23},{24..., dimensions={0} | all-to-all | bytes 221184 | tf_op jit(solution)/shard_map/all_to_all | solution.py:32
  74.1 0.7 shard_map.73
  74.8 0.0 collective-permute-done.7.later_ref
  74.8 6.4 %all-to-all-start.2 = ((f32[8,2,3456]{2,1,0:T(2,128)}), f32[8,2,3456]{2,1,0:T(2,128)S(1)}, u32[]{:S(2)}, u32[]{:S(2)}) async-start(f32[8,2,3456]{2,1,0:T(2,128)} %shard_map.73), calls=%async_computation.2 | async-start | bytes 442368 | tf_op jit(solution)/shard_map/all_to_all | solution.py:32
  81.2 3.5 %shard_map.75 = bf16[2,2,128,256]{3,2,1,0:T(8,128)(2,1)} custom-call(bf16[2,4,128,256]{3,2,1,0:T(8,128)(2,1)S(1)} %pad_maximum_fusion.1.tall_ref, bf16[2,2,128,256]{3,2,1,0:T(8,128)(2,1)S(1)} %collective-permute-done.7.later_ref, bf16[3,3,3,256,256]{4,3,2,1,0:T(8,128)(2,1)} %w_from.3, bf16[2,2,128,256]{3,2,1,0:T(8,128)(2,1)S(1)} %copy-done.1), custom_call_target="tpu_custom_call" | custom-call | flops 905969664 | bytes 5000000 | tf_op jit(solution)/shard_map/pallas_call | solution.py:339
  84.7 3.9 %all-to-all-done.2.mine_ref = f32[8,2,3456]{2,1,0:T(2,128)S(1)} async-done(((f32[8,2,3456]{2,1,0:T(2,128)}), f32[8,2,3456]{2,1,0:T(2,128)S(1)}, u32[]{:S(2)}, u32[]{:S(2)}) %all-to-all-start.2) | async-done | bytes 221216 | tf_op jit(solution)/shard_map/all_to_all | solution.py:32
  88.6 4.3 %collective-permute-start.8 = (f32[8,2,3456]{2,1,0:T(2,128)S(1)}, f32[8,2,3456]{2,1,0:T(2,128)S(1)}, u32[]{:S(2)}, u32[]{:S(2)}) collective-permute-start(f32[8,2,3456]{2,1,0:T(2,128)S(1)} %all-to-all-done.2.mine_ref), channel_id=1, source_target_pairs={{0,16},{16,0},{32,48},{48,32},{64,80},{80,64},{96,112},{112,96},{1... | collective-permute-start | bytes 663560 | tf_op jit(solution)/shard_map/ppermute | solution.py:36
  92.9 1.1 %collective-permute-done.8.other_ref = f32[8,2,3456]{2,1,0:T(2,128)S(1)} collective-permute-done((f32[8,2,3456]{2,1,0:T(2,128)S(1)}, f32[8,2,3456]{2,1,0:T(2,128)S(1)}, u32[]{:S(2)}, u32[]{:S(2)}) %collective-permute-start.8) | collective-permute-done | bytes 221216 | tf_op jit(solution)/shard_map/ppermute | solution.py:36
  94.0 0.9 shard_map.76
  (5 shorter events, 0.1 us)
Async XLA Ops:
  0.6 8.2 %collective-permute-start = (bf16[2,2,128,256]{3,2,1,0:T(8,128)(2,1)}, bf16[2,2,128,256]{3,2,1,0:T(8,128)(2,1)S(1)}, u32[]{:S(2)}, u32[]{:S(2)}) collective-permute-start(bf16[2,2,128,256]{3,2,1,0:T(8,128)(2,1)} %frames_ref.1), channel_id=1, source_target_pairs={{0,16},{16,32},{32,48},{48,64},{64,80},{80,96},{96,112},{112,128},... | collective-permute-start | bytes 786440 | tf_op jit(solution)/shard_map/ppermute | solution.py:42
  5.2 1.0 %copy-start.3 = (bf16[2,2,128,256]{3,2,1,0:T(8,128)(2,1)S(1)}, bf16[2,2,128,256]{3,2,1,0:T(8,128)(2,1)}, u32[]{:S(2)}) copy-start(bf16[2,2,128,256]{3,2,1,0:T(8,128)(2,1)} %frames_ref.1) | copy-start | bytes 786436
  8.9 6.3 %collective-permute-start.1 = (bf16[4,1,128,256]{3,2,1,0:T(8,128)(2,1)S(1)}, bf16[4,1,128,256]{3,2,1,0:T(8,128)(2,1)S(1)}, u32[]{:S(2)}, u32[]{:S(2)}) collective-permute-start(bf16[4,1,128,256]{3,2,1,0:T(8,128)(2,1)S(1)} %get-tuple-element.44), channel_id=1, source_target_pairs={{0,1},{2,3},{4,5},{6,7},{8,9},{10,11},{12,13},{14,15},{1,0},{3,2},... | collective-permute-start | bytes 786440 | tf_op jit(solution)/shard_map/ppermute | solution.py:47
  10.6 4.5 %collective-permute-start.2 = (bf16[4,1,128,256]{3,2,1,0:T(8,128)(2,1)S(1)}, bf16[4,1,128,256]{3,2,1,0:T(8,128)(2,1)S(1)}, u32[]{:S(2)}, u32[]{:S(2)}) collective-permute-start(bf16[4,1,128,256]{3,2,1,0:T(8,128)(2,1)S(1)} %get-tuple-element.43), channel_id=1, source_target_pairs={{1,2},{3,4},{5,6},{7,8},{9,10},{11,12},{13,14},{2,1},{4,3},{6,5},{... | collective-permute-start | bytes 786440 | tf_op jit(solution)/shard_map/ppermute | solution.py:47
  11.3 2.0 %copy-start = (bf16[3,3,3,256,256]{4,3,2,1,0:T(8,128)(2,1)S(1)}, bf16[3,3,3,256,256]{4,3,2,1,0:T(8,128)(2,1)}, u32[]{:S(2)}) copy-start(bf16[3,3,3,256,256]{4,3,2,1,0:T(8,128)(2,1)} %w_from.3) | copy-start | bytes 10616836
  13.3 1.8 %copy-start.1 = (bf16[2,2,128,256]{3,2,1,0:T(8,128)(2,1)S(1)}, bf16[2,2,128,256]{3,2,1,0:T(8,128)(2,1)}, u32[]{:S(2)}) copy-start(bf16[2,2,128,256]{3,2,1,0:T(8,128)(2,1)} %cot_ref.3) | copy-start | bytes 786436
  17.0 0.9 copy-start.2
  17.2 2.4 %collective-permute-start.3 = (bf16[4,4,128,128]{3,2,1,0:T(8,128)(2,1)S(1)}, bf16[4,4,128,128]{3,2,1,0:T(8,128)(2,1)S(1)}, u32[]{:S(2)}, u32[]{:S(2)}) collective-permute-start(bf16[4,4,128,128]{3,2,1,0:T(8,128)(2,1)S(1)} %get-tuple-element.40), channel_id=1, source_target_pairs={{0,16},{16,0},{32,48},{48,32},{64,80},{80,64},{96,112},{112,96},{1... | collective-permute-start | bytes 1572872 | tf_op jit(solution)/shard_map/ppermute | solution.py:36
  17.3 2.3 %collective-permute-start.4 = (bf16[2,2,128,256]{3,2,1,0:T(8,128)(2,1)S(1)}, bf16[2,2,128,256]{3,2,1,0:T(8,128)(2,1)S(1)}, u32[]{:S(2)}, u32[]{:S(2)}) collective-permute-start(bf16[2,2,128,256]{3,2,1,0:T(8,128)(2,1)S(1)} %get-tuple-element.33.grad_ref), channel_id=1, source_target_pairs={{0,16},{16,0},{32,48},{48,32},{64,80},{80,64},{96,112},{112,96},{1... | collective-permute-start | bytes 786440 | tf_op jit(solution)/shard_map/ppermute | solution.py:36
  22.0 40.8 %all-to-all-start = ((bf16[16,16,3456]{2,1,0:T(8,128)(2,1)}), bf16[16,16,3456]{2,1,0:T(8,128)(2,1)S(1)}, u32[]{:S(2)}, u32[]{:S(2)}) async-start(bf16[16,16,3456]{2,1,0:T(8,128)(2,1)} %bitcast), calls=%async_computation | async-start | bytes 3538944 | tf_op jit(solution)/shard_map/all_to_all | solution.py:32
  37.6 2.3 %collective-permute-start.5 = (bf16[2,1,128,256]{3,2,1,0:T(8,128)(2,1)S(1)}, bf16[2,1,128,256]{3,2,1,0:T(8,128)(2,1)S(1)}, u32[]{:S(2)}, u32[]{:S(2)}) collective-permute-start(bf16[2,1,128,256]{3,2,1,0:T(8,128)(2,1)S(1)} %get-tuple-element.47), channel_id=1, source_target_pairs={{1,2},{3,4},{5,6},{7,8},{9,10},{11,12},{13,14},{2,1},{4,3},{6,5},{... | collective-permute-start | bytes 393224 | tf_op jit(solution)/shard_map/ppermute | solution.py:47
  38.3 4.6 %collective-permute-start.6 = (bf16[2,1,128,256]{3,2,1,0:T(8,128)(2,1)S(1)}, bf16[2,1,128,256]{3,2,1,0:T(8,128)(2,1)S(1)}, u32[]{:S(2)}, u32[]{:S(2)}) collective-permute-start(bf16[2,1,128,256]{3,2,1,0:T(8,128)(2,1)S(1)} %get-tuple-element.48), channel_id=1, source_target_pairs={{0,1},{2,3},{4,5},{6,7},{8,9},{10,11},{12,13},{14,15},{1,0},{3,2},... | collective-permute-start | bytes 393224 | tf_op jit(solution)/shard_map/ppermute | solution.py:47
  45.8 29.0 %collective-permute-start.7 = (bf16[2,2,128,256]{3,2,1,0:T(8,128)(2,1)S(1)}, bf16[2,2,128,256]{3,2,1,0:T(8,128)(2,1)S(1)}, u32[]{:S(2)}, u32[]{:S(2)}) collective-permute-start(bf16[2,2,128,256]{3,2,1,0:T(8,128)(2,1)S(1)} %shard_map.74), channel_id=1, source_target_pairs={{16,0},{32,16},{48,32},{64,48},{80,64},{96,80},{112,96},{128,112},... | collective-permute-start | bytes 786440 | tf_op jit(solution)/shard_map/ppermute | solution.py:42
  74.8 13.8 %all-to-all-start.2 = ((f32[8,2,3456]{2,1,0:T(2,128)}), f32[8,2,3456]{2,1,0:T(2,128)S(1)}, u32[]{:S(2)}, u32[]{:S(2)}) async-start(f32[8,2,3456]{2,1,0:T(2,128)} %shard_map.73), calls=%async_computation.2 | async-start | bytes 442368 | tf_op jit(solution)/shard_map/all_to_all | solution.py:32
  88.6 5.4 %collective-permute-start.8 = (f32[8,2,3456]{2,1,0:T(2,128)S(1)}, f32[8,2,3456]{2,1,0:T(2,128)S(1)}, u32[]{:S(2)}, u32[]{:S(2)}) collective-permute-start(f32[8,2,3456]{2,1,0:T(2,128)S(1)} %all-to-all-done.2.mine_ref), channel_id=1, source_target_pairs={{0,16},{16,0},{32,48},{48,32},{64,80},{80,64},{96,112},{112,96},{1... | collective-permute-start | bytes 663560 | tf_op jit(solution)/shard_map/ppermute | solution.py:36

commit v9 on v8

--- a/solution.py
+++ b/solution.py
@@ -28,8 +28,14 @@
     return groups
 
 
-def exchange(value, names):
-    return lax.all_to_all(value, BOTH, 0, 0, tiled=True, axis_index_groups=groups_of(names))
+Z_ORDER = (4, 5, 6, 7, 0, 1, 2, 3)
+
+
+def exchange(value, names, order=None):
+    groups = groups_of(names)
+    if order:
+        groups = [[group[i] for i in order] for group in groups]
+    return lax.all_to_all(value, BOTH, 0, 0, tiled=True, axis_index_groups=groups)
 
 
 def flip_core(value):
@@ -232,8 +238,8 @@
     total = got_ref[0].astype(jnp.float32)
     for i in range(1, 16):
         total += got_ref[i].astype(jnp.float32)
-    for z in range(8):
-        out_ref[z] = total[2 * z : 2 * z + 2].astype(out_ref.dtype)
+    for at, z in enumerate(Z_ORDER):
+        out_ref[at] = total[2 * z : 2 * z + 2].astype(out_ref.dtype)
 
 
 def line_kernel(got_ref, out_ref):
@@ -332,7 +338,7 @@
         out_specs=pl.BlockSpec((8, 2, 1152), lambda i: (0, 0, i)),
         compiler_params=VMEM,
     )(got)
-    got = exchange(plane, ("z",)).reshape(8, 2, 3456)
+    got = exchange(plane, ("z",), Z_ORDER).reshape(8, 2, 3456)
     copies = call(line_kernel, jax.ShapeDtypeStruct((8, 2, 3456), jnp.float32), 100000)(got)
     copies, tall, follow = lax.optimization_barrier((copies, tall, follow))
     share = exchange(copies, ("x_hi", "y")).reshape(8, 2, 3456)

time: 95.5 us -> 93.3 us (0.977)
  blocking collectives: 10.7 us -> 9.07 us
    all_to_all x1, blocking collectives: 10.7 us -> 9.07 us  [exchange(): lax.all_to_all(value, BOTH, 0, 0, tiled=True, axis_index_groups=groups)]
where the time goes in v9:
time: 93.3 us; the launch traced here: 92.8 us
  starting transfers between devices  39.1 us (42%)
  waiting for transfers between devices  24.7 us (26%)
  Pallas kernels  15.6 us (17%)
  blocking collectives  9.07 us (10%)
  local copies, waits for them, and re-layouts  3.05 us (3%)
    all_to_all x2, starting transfers between devices, exchange(): lax.all_to_all(value, BOTH, 0, 0, tiled=True, axis_index_groups=groups)  21.7 us
    all_to_all x2, waiting for transfers between devices, exchange(): lax.all_to_all(value, BOTH, 0, 0, tiled=True, axis_index_groups=groups)  17.5 us
    all_to_all x1, blocking collectives, exchange(): lax.all_to_all(value, BOTH, 0, 0, tiled=True, axis_index_groups=groups)  9.07 us
    ppermute x2, starting transfers between devices, shifted(): lax.ppermute(value, axis, [(source, source + steps) for source in range(l...  8.02 us
    ppermute x4, starting transfers between devices, pairs(): return lax.ppermute(value, 'space', links + [(j, i) for i, j in links])  4.72 us
    ppermute x3, starting transfers between devices, flip_core(): return lax.ppermute(value, 'tm', [(i, i ^ 1) for i in range(16)])  4.69 us
    pallas_call x1, Pallas kernels, local(): call_back(backward_kernel, 2, 1, flops // 2)  3.53 us
    ppermute x4, waiting for transfers between devices, pairs(): return lax.ppermute(value, 'space', links + [(j, i) for i, j in links])  3.23 us
  transfers between devices with their start and end apart: 11, of which 7 were waited for; matrix products, arithmetic and copies ran while one was open for 0% of the time, Pallas kernels for 11%

profile of v9, /device:TPU:1, one launch (start us, length us, event | category | flops | bytes accessed | tf_op | source)
XLA Modules:
  0.0 92.8 jit_solution(7584306749564733235)
XLA Ops:
  0.6 4.6 %collective-permute-start = (bf16[2,2,128,256]{3,2,1,0:T(8,128)(2,1)}, bf16[2,2,128,256]{3,2,1,0:T(8,128)(2,1)S(1)}, u32[]{:S(2)}, u32[]{:S(2)}) collective-permute-start(bf16[2,2,128,256]{3,2,1,0:T(8,128)(2,1)} %frames_ref.1), channel_id=1, source_target_pairs={{0,16},{16,32},{32,48},{48,64},{64,80},{80,96},{96,112},{112,128},... | collective-permute-start | bytes 786440 | tf_op jit(solution)/shard_map/ppermute | solution.py:48
  5.2 0.0 copy-start.3
  5.2 1.0 %copy-done.3 = bf16[2,2,128,256]{3,2,1,0:T(8,128)(2,1)S(1)} copy-done((bf16[2,2,128,256]{3,2,1,0:T(8,128)(2,1)S(1)}, bf16[2,2,128,256]{3,2,1,0:T(8,128)(2,1)}, u32[]{:S(2)}) %copy-start.3) | copy-done | bytes 262168
  6.2 2.6 %collective-permute-done.carried_ref = bf16[2,2,128,256]{3,2,1,0:T(8,128)(2,1)S(1)} collective-permute-done((bf16[2,2,128,256]{3,2,1,0:T(8,128)(2,1)}, bf16[2,2,128,256]{3,2,1,0:T(8,128)(2,1)S(1)}, u32[]{:S(2)}, u32[]{:S(2)}) %collective-permute-start) | collective-permute-done | bytes 262176 | tf_op jit(solution)/shard_map/ppermute | solution.py:48
  8.9 0.1 broadcast_select_fusion.4
  8.9 1.7 %collective-permute-start.1 = (bf16[4,1,128,256]{3,2,1,0:T(8,128)(2,1)S(1)}, bf16[4,1,128,256]{3,2,1,0:T(8,128)(2,1)S(1)}, u32[]{:S(2)}, u32[]{:S(2)}) collective-permute-start(bf16[4,1,128,256]{3,2,1,0:T(8,128)(2,1)S(1)} %get-tuple-element.44), channel_id=1, source_target_pairs={{0,1},{2,3},{4,5},{6,7},{8,9},{10,11},{12,13},{14,15},{1,0},{3,2},... | collective-permute-start | bytes 786440 | tf_op jit(solution)/shard_map/ppermute | solution.py:53
  10.6 0.7 collective-permute-start.2
  11.3 0.0 copy-start
  11.3 2.0 %copy-done = bf16[3,3,3,256,256]{4,3,2,1,0:T(8,128)(2,1)S(1)} copy-done((bf16[3,3,3,256,256]{4,3,2,1,0:T(8,128)(2,1)S(1)}, bf16[3,3,3,256,256]{4,3,2,1,0:T(8,128)(2,1)}, u32[]{:S(2)}) %copy-start) | copy-done | bytes 3538968
  13.3 0.0 copy-start.1
  13.3 1.5 %shard_map.68 = (f32[4,128,256]{2,1,0:T(8,128)S(1)}, bf16[3,2,3,256,256]{4,3,2,1,0:T(8,128)(2,1)S(1)}) custom-call(bf16[2,2,128,256]{3,2,1,0:T(8,128)(2,1)S(1)} %collective-permute-done.carried_ref, bf16[2,2,128,256]{3,2,1,0:T(8,128)(2,1)S(1)} %get-tuple-element.23.own_ref, bf16[3,3,3,256,256]{4,3,2,1,0:T(8,128)(2,1)S(1)} %copy-done), custom_call_target="tpu_custom_call" | custom-call | flops 1811939328 | bytes 5000000 | tf_op jit(solution)/shard_map/pallas_call | solution.py:294
  14.9 0.3 collective-permute-done.1.near_ref
  15.2 0.0 collective-permute-done.2.far_ref
  15.2 0.0 copy-done.1
  15.2 1.8 %shard_map.69 = (bf16[2,2,128,256]{3,2,1,0:T(8,128)(2,1)}, bf16[2,2,128,256]{3,2,1,0:T(8,128)(2,1)S(1)}) custom-call(bf16[4,1,128,256]{3,2,1,0:T(8,128)(2,1)S(1)} %collective-permute-done.1.near_ref, bf16[4,1,128,256]{3,2,1,0:T(8,128)(2,1)S(1)} %collective-permute-done.2.far_ref, bf16[2,2,128,256]{3,2,1,0:T(8,128)(2,1)S(1)} %get-tuple-element.23.own_ref, ...), custom_call_target="tpu_custom_call" | custom-call | flops 603979776 | bytes 5000000 | tf_op jit(solution)/shard_map/pallas_call | solution.py:303
  17.0 0.0 copy-start.2
  17.0 0.1 pad_maximum_fusion
  17.1 0.1 broadcast_select_fusion
  17.2 0.1 collective-permute-start.3
  17.3 0.5 collective-permute-start.4
  17.8 0.1 copy-done.2
  17.9 1.4 %shard_map.70.part_ref = f32[768,1152]{1,0:T(8,128)S(1)} custom-call(bf16[4,4,128,128]{3,2,1,0:T(8,128)(2,1)S(1)} %get-tuple-element.39.cells_ref, bf16[2,2,128,256]{3,2,1,0:T(8,128)(2,1)S(1)} %get-tuple-element.33.grad_ref, bf16[256,256]{1,0:T(8,128)(2,1)S(1)} %copy-done.2), custom_call_target="tpu_custom_call" | custom-call | flops 905969664 | bytes 5000000 | tf_op jit(solution)/shard_map/pallas_call | solution.py:316
  19.3 0.3 collective-permute-done.4.grad_ref
  19.6 0.0 collective-permute-done.3.cells_ref
  19.6 2.4 %shard_map.71 = bf16[256,3456]{1,0:T(8,128)(2,1)} custom-call(bf16[4,4,128,128]{3,2,1,0:T(8,128)(2,1)S(1)} %collective-permute-done.3.cells_ref, bf16[2,2,128,256]{3,2,1,0:T(8,128)(2,1)S(1)} %collective-permute-done.4.grad_ref, bf16[256,256]{1,0:T(8,128)(2,1)S(1)} %copy-done.2, f32[768,1152]{1,0:T(8,128)S(1)} %shard_map.70.part_ref), custom_call_target="tpu_custom_call" | custom-call | flops 905969664 | bytes 5000000 | tf_op jit(solution)/shard_map/pallas_call | solution.py:319
  22.0 15.5 %all-to-all-start = ((bf16[16,16,3456]{2,1,0:T(8,128)(2,1)}), bf16[16,16,3456]{2,1,0:T(8,128)(2,1)S(1)}, u32[]{:S(2)}, u32[]{:S(2)}) async-start(bf16[16,16,3456]{2,1,0:T(8,128)(2,1)} %bitcast), calls=%async_computation | async-start | bytes 3538944 | tf_op jit(solution)/shard_map/all_to_all | solution.py:38
  37.6 0.7 collective-permute-start.5
  38.3 1.7 %collective-permute-start.6 = (bf16[2,1,128,256]{3,2,1,0:T(8,128)(2,1)S(1)}, bf16[2,1,128,256]{3,2,1,0:T(8,128)(2,1)S(1)}, u32[]{:S(2)}, u32[]{:S(2)}) collective-permute-start(bf16[2,1,128,256]{3,2,1,0:T(8,128)(2,1)S(1)} %get-tuple-element.48), channel_id=1, source_target_pairs={{0,1},{2,3},{4,5},{6,7},{8,9},{10,11},{12,13},{14,15},{1,0},{3,2},... | collective-permute-start | bytes 393224 | tf_op jit(solution)/shard_map/ppermute | solution.py:53
  39.9 0.0 collective-permute-done.5
  39.9 2.9 %collective-permute-done.6 = bf16[2,1,128,256]{3,2,1,0:T(8,128)(2,1)S(1)} collective-permute-done((bf16[2,1,128,256]{3,2,1,0:T(8,128)(2,1)S(1)}, bf16[2,1,128,256]{3,2,1,0:T(8,128)(2,1)S(1)}, u32[]{:S(2)}, u32[]{:S(2)}) %collective-permute-start.6) | collective-permute-done | bytes 131104 | tf_op jit(solution)/shard_map/ppermute | solution.py:53
  42.9 0.1 pad_maximum_fusion.1.tall_ref
  43.0 2.8 %shard_map.74 = bf16[2,2,128,256]{3,2,1,0:T(8,128)(2,1)S(1)} custom-call(bf16[2,4,128,256]{3,2,1,0:T(8,128)(2,1)S(1)} %pad_maximum_fusion.1.tall_ref, bf16[3,3,3,256,256]{4,3,2,1,0:T(8,128)(2,1)} %w_from.3), custom_call_target="tpu_custom_call" | custom-call | flops 905969664 | bytes 5000000 | tf_op jit(solution)/shard_map/pallas_call | solution.py:330
  45.8 3.4 %collective-permute-start.7 = (bf16[2,2,128,256]{3,2,1,0:T(8,128)(2,1)S(1)}, bf16[2,2,128,256]{3,2,1,0:T(8,128)(2,1)S(1)}, u32[]{:S(2)}, u32[]{:S(2)}) collective-permute-start(bf16[2,2,128,256]{3,2,1,0:T(8,128)(2,1)S(1)} %shard_map.74), channel_id=1, source_target_pairs={{16,0},{32,16},{48,32},{64,48},{80,64},{96,80},{112,96},{128,112},... | collective-permute-start | bytes 786440 | tf_op jit(solution)/shard_map/ppermute | solution.py:48
  49.2 13.6 %all-to-all-done.got_ref = bf16[16,16,3456]{2,1,0:T(8,128)(2,1)S(1)} async-done(((bf16[16,16,3456]{2,1,0:T(8,128)(2,1)}), bf16[16,16,3456]{2,1,0:T(8,128)(2,1)S(1)}, u32[]{:S(2)}, u32[]{:S(2)}) %all-to-all-start) | async-done | bytes 1769504 | tf_op jit(solution)/shard_map/all_to_all | solution.py:38
  62.8 0.5 shard_map.72
  63.3 9.1 %all_to_all.19.got_ref = bf16[8,2,3456]{2,1,0:T(2,128)(2,1)S(1)} all-to-all(bf16[8,2,3456]{2,1,0:T(2,128)(2,1)S(1)} %shard_map.72), channel_id=1, replica_groups={{4,5,6,7,0,1,2,3},{12,13,14,15,8,9,10,11},{20,21,22,23,16,17,18,19},{28..., dimensions={0} | all-to-all | bytes 221184 | tf_op jit(solution)/shard_map/all_to_all | solution.py:38
  72.4 0.7 shard_map.73
  73.1 0.0 collective-permute-done.7.later_ref
  73.1 6.2 %all-to-all-start.2 = ((f32[8,2,3456]{2,1,0:T(2,128)}), f32[8,2,3456]{2,1,0:T(2,128)S(1)}, u32[]{:S(2)}, u32[]{:S(2)}) async-start(f32[8,2,3456]{2,1,0:T(2,128)} %shard_map.73), calls=%async_computation.2 | async-start | bytes 442368 | tf_op jit(solution)/shard_map/all_to_all | solution.py:38
  79.3 3.5 %shard_map.75 = bf16[2,2,128,256]{3,2,1,0:T(8,128)(2,1)} custom-call(bf16[2,4,128,256]{3,2,1,0:T(8,128)(2,1)S(1)} %pad_maximum_fusion.1.tall_ref, bf16[2,2,128,256]{3,2,1,0:T(8,128)(2,1)S(1)} %collective-permute-done.7.later_ref, bf16[3,3,3,256,256]{4,3,2,1,0:T(8,128)(2,1)} %w_from.3, bf16[2,2,128,256]{3,2,1,0:T(8,128)(2,1)S(1)} %copy-done.1), custom_call_target="tpu_custom_call" | custom-call | flops 905969664 | bytes 5000000 | tf_op jit(solution)/shard_map/pallas_call | solution.py:345
  82.8 3.9 %all-to-all-done.2.mine_ref = f32[8,2,3456]{2,1,0:T(2,128)S(1)} async-done(((f32[8,2,3456]{2,1,0:T(2,128)}), f32[8,2,3456]{2,1,0:T(2,128)S(1)}, u32[]{:S(2)}, u32[]{:S(2)}) %all-to-all-start.2) | async-done | bytes 221216 | tf_op jit(solution)/shard_map/all_to_all | solution.py:38
  86.7 4.1 %collective-permute-start.8 = (f32[8,2,3456]{2,1,0:T(2,128)S(1)}, f32[8,2,3456]{2,1,0:T(2,128)S(1)}, u32[]{:S(2)}, u32[]{:S(2)}) collective-permute-start(f32[8,2,3456]{2,1,0:T(2,128)S(1)} %all-to-all-done.2.mine_ref), channel_id=1, source_target_pairs={{0,16},{16,0},{32,48},{48,32},{64,80},{80,64},{96,112},{112,96},{1... | collective-permute-start | bytes 663560 | tf_op jit(solution)/shard_map/ppermute | solution.py:42
  90.8 1.1 %collective-permute-done.8.other_ref = f32[8,2,3456]{2,1,0:T(2,128)S(1)} collective-permute-done((f32[8,2,3456]{2,1,0:T(2,128)S(1)}, f32[8,2,3456]{2,1,0:T(2,128)S(1)}, u32[]{:S(2)}, u32[]{:S(2)}) %collective-permute-start.8) | collective-permute-done | bytes 221216 | tf_op jit(solution)/shard_map/ppermute | solution.py:42
  91.9 0.9 shard_map.76
  (5 shorter events, 0.1 us)
Async XLA Ops:
  0.6 8.2 %collective-permute-start = (bf16[2,2,128,256]{3,2,1,0:T(8,128)(2,1)}, bf16[2,2,128,256]{3,2,1,0:T(8,128)(2,1)S(1)}, u32[]{:S(2)}, u32[]{:S(2)}) collective-permute-start(bf16[2,2,128,256]{3,2,1,0:T(8,128)(2,1)} %frames_ref.1), channel_id=1, source_target_pairs={{0,16},{16,32},{32,48},{48,64},{64,80},{80,96},{96,112},{112,128},... | collective-permute-start | bytes 786440 | tf_op jit(solution)/shard_map/ppermute | solution.py:48
  5.2 1.0 %copy-start.3 = (bf16[2,2,128,256]{3,2,1,0:T(8,128)(2,1)S(1)}, bf16[2,2,128,256]{3,2,1,0:T(8,128)(2,1)}, u32[]{:S(2)}) copy-start(bf16[2,2,128,256]{3,2,1,0:T(8,128)(2,1)} %frames_ref.1) | copy-start | bytes 786436
  8.9 6.3 %collective-permute-start.1 = (bf16[4,1,128,256]{3,2,1,0:T(8,128)(2,1)S(1)}, bf16[4,1,128,256]{3,2,1,0:T(8,128)(2,1)S(1)}, u32[]{:S(2)}, u32[]{:S(2)}) collective-permute-start(bf16[4,1,128,256]{3,2,1,0:T(8,128)(2,1)S(1)} %get-tuple-element.44), channel_id=1, source_target_pairs={{0,1},{2,3},{4,5},{6,7},{8,9},{10,11},{12,13},{14,15},{1,0},{3,2},... | collective-permute-start | bytes 786440 | tf_op jit(solution)/shard_map/ppermute | solution.py:53
  10.6 4.5 %collective-permute-start.2 = (bf16[4,1,128,256]{3,2,1,0:T(8,128)(2,1)S(1)}, bf16[4,1,128,256]{3,2,1,0:T(8,128)(2,1)S(1)}, u32[]{:S(2)}, u32[]{:S(2)}) collective-permute-start(bf16[4,1,128,256]{3,2,1,0:T(8,128)(2,1)S(1)} %get-tuple-element.43), channel_id=1, source_target_pairs={{1,2},{3,4},{5,6},{7,8},{9,10},{11,12},{13,14},{2,1},{4,3},{6,5},{... | collective-permute-start | bytes 786440 | tf_op jit(solution)/shard_map/ppermute | solution.py:53
  11.3 2.0 %copy-start = (bf16[3,3,3,256,256]{4,3,2,1,0:T(8,128)(2,1)S(1)}, bf16[3,3,3,256,256]{4,3,2,1,0:T(8,128)(2,1)}, u32[]{:S(2)}) copy-start(bf16[3,3,3,256,256]{4,3,2,1,0:T(8,128)(2,1)} %w_from.3) | copy-start | bytes 10616836
  13.3 1.8 %copy-start.1 = (bf16[2,2,128,256]{3,2,1,0:T(8,128)(2,1)S(1)}, bf16[2,2,128,256]{3,2,1,0:T(8,128)(2,1)}, u32[]{:S(2)}) copy-start(bf16[2,2,128,256]{3,2,1,0:T(8,128)(2,1)} %cot_ref.3) | copy-start | bytes 786436
  17.0 0.9 copy-start.2
  17.2 2.4 %collective-permute-start.3 = (bf16[4,4,128,128]{3,2,1,0:T(8,128)(2,1)S(1)}, bf16[4,4,128,128]{3,2,1,0:T(8,128)(2,1)S(1)}, u32[]{:S(2)}, u32[]{:S(2)}) collective-permute-start(bf16[4,4,128,128]{3,2,1,0:T(8,128)(2,1)S(1)} %get-tuple-element.40), channel_id=1, source_target_pairs={{0,16},{16,0},{32,48},{48,32},{64,80},{80,64},{96,112},{112,96},{1... | collective-permute-start | bytes 1572872 | tf_op jit(solution)/shard_map/ppermute | solution.py:42
  17.3 2.3 %collective-permute-start.4 = (bf16[2,2,128,256]{3,2,1,0:T(8,128)(2,1)S(1)}, bf16[2,2,128,256]{3,2,1,0:T(8,128)(2,1)S(1)}, u32[]{:S(2)}, u32[]{:S(2)}) collective-permute-start(bf16[2,2,128,256]{3,2,1,0:T(8,128)(2,1)S(1)} %get-tuple-element.33.grad_ref), channel_id=1, source_target_pairs={{0,16},{16,0},{32,48},{48,32},{64,80},{80,64},{96,112},{112,96},{1... | collective-permute-start | bytes 786440 | tf_op jit(solution)/shard_map/ppermute | solution.py:42
  22.0 40.8 %all-to-all-start = ((bf16[16,16,3456]{2,1,0:T(8,128)(2,1)}), bf16[16,16,3456]{2,1,0:T(8,128)(2,1)S(1)}, u32[]{:S(2)}, u32[]{:S(2)}) async-start(bf16[16,16,3456]{2,1,0:T(8,128)(2,1)} %bitcast), calls=%async_computation | async-start | bytes 3538944 | tf_op jit(solution)/shard_map/all_to_all | solution.py:38
  37.6 2.3 %collective-permute-start.5 = (bf16[2,1,128,256]{3,2,1,0:T(8,128)(2,1)S(1)}, bf16[2,1,128,256]{3,2,1,0:T(8,128)(2,1)S(1)}, u32[]{:S(2)}, u32[]{:S(2)}) collective-permute-start(bf16[2,1,128,256]{3,2,1,0:T(8,128)(2,1)S(1)} %get-tuple-element.47), channel_id=1, source_target_pairs={{1,2},{3,4},{5,6},{7,8},{9,10},{11,12},{13,14},{2,1},{4,3},{6,5},{... | collective-permute-start | bytes 393224 | tf_op jit(solution)/shard_map/ppermute | solution.py:53
  38.3 4.6 %collective-permute-start.6 = (bf16[2,1,128,256]{3,2,1,0:T(8,128)(2,1)S(1)}, bf16[2,1,128,256]{3,2,1,0:T(8,128)(2,1)S(1)}, u32[]{:S(2)}, u32[]{:S(2)}) collective-permute-start(bf16[2,1,128,256]{3,2,1,0:T(8,128)(2,1)S(1)} %get-tuple-element.48), channel_id=1, source_target_pairs={{0,1},{2,3},{4,5},{6,7},{8,9},{10,11},{12,13},{14,15},{1,0},{3,2},... | collective-permute-start | bytes 393224 | tf_op jit(solution)/shard_map/ppermute | solution.py:53
  45.8 27.4 %collective-permute-start.7 = (bf16[2,2,128,256]{3,2,1,0:T(8,128)(2,1)S(1)}, bf16[2,2,128,256]{3,2,1,0:T(8,128)(2,1)S(1)}, u32[]{:S(2)}, u32[]{:S(2)}) collective-permute-start(bf16[2,2,128,256]{3,2,1,0:T(8,128)(2,1)S(1)} %shard_map.74), channel_id=1, source_target_pairs={{16,0},{32,16},{48,32},{64,48},{80,64},{96,80},{112,96},{128,112},... | collective-permute-start | bytes 786440 | tf_op jit(solution)/shard_map/ppermute | solution.py:48
  73.1 13.6 %all-to-all-start.2 = ((f32[8,2,3456]{2,1,0:T(2,128)}), f32[8,2,3456]{2,1,0:T(2,128)S(1)}, u32[]{:S(2)}, u32[]{:S(2)}) async-start(f32[8,2,3456]{2,1,0:T(2,128)} %shard_map.73), calls=%async_computation.2 | async-start | bytes 442368 | tf_op jit(solution)/shard_map/all_to_all | solution.py:38
  86.7 5.2 %collective-permute-start.8 = (f32[8,2,3456]{2,1,0:T(2,128)S(1)}, f32[8,2,3456]{2,1,0:T(2,128)S(1)}, u32[]{:S(2)}, u32[]{:S(2)}) collective-permute-start(f32[8,2,3456]{2,1,0:T(2,128)S(1)} %all-to-all-done.2.mine_ref), channel_id=1, source_target_pairs={{0,16},{16,0},{32,48},{48,32},{64,80},{80,64},{96,112},{112,96},{1... | collective-permute-start | bytes 663560 | tf_op jit(solution)/shard_map/ppermute | solution.py:42

commit v10 on v9

--- a/solution.py
+++ b/solution.py
@@ -29,6 +29,7 @@
 
 
 Z_ORDER = (4, 5, 6, 7, 0, 1, 2, 3)
+SHARE_ORDER = (7, 6, 5, 4, 3, 2, 1, 0)
 
 
 def exchange(value, names, order=None):
@@ -255,8 +256,8 @@
     core = lax.axis_index("tm") % 2
     for tap in range(27):
         lanes = slice(tap * 128, (tap + 1) * 128)
-        mine = jnp.concatenate([mine_ref[q, :, lanes] for q in range(8)], axis=0)
-        other = jnp.concatenate([other_ref[q, :, lanes] for q in range(8)], axis=0)
+        mine = jnp.concatenate([mine_ref[SHARE_ORDER.index(q), :, lanes] for q in range(8)], axis=0)
+        other = jnp.concatenate([other_ref[SHARE_ORDER.index(q), :, lanes] for q in range(8)], axis=0)
         out_ref[tap] = jnp.where(
             core == 0,
             jnp.concatenate([mine, other], axis=1),
@@ -341,7 +342,7 @@
     got = exchange(plane, ("z",), Z_ORDER).reshape(8, 2, 3456)
     copies = call(line_kernel, jax.ShapeDtypeStruct((8, 2, 3456), jnp.float32), 100000)(got)
     copies, tall, follow = lax.optimization_barrier((copies, tall, follow))
-    share = exchange(copies, ("x_hi", "y")).reshape(8, 2, 3456)
+    share = exchange(copies, ("x_hi", "y"), SHARE_ORDER).reshape(8, 2, 3456)
     grad_input = call_back(backward_kernel, 2, 1, flops // 2)(
         tall, follow, weight, cotangent
     )

time: 93.3 us -> 92.1 us (0.987)
  waiting for transfers between devices: 24.7 us -> 20.9 us
  starting transfers between devices: 39.1 us -> 41.8 us
    all_to_all x2, waiting for transfers between devices: 17.5 us -> 13.7 us  [exchange(): lax.all_to_all(value, BOTH, 0, 0, tiled=True, axis_index_groups=groups)]
    all_to_all x2, starting transfers between devices: 21.7 us -> 23.3 us  [exchange(): lax.all_to_all(value, BOTH, 0, 0, tiled=True, axis_index_groups=groups)]
    ppermute x3, starting transfers between devices: 4.69 us -> 5.72 us  [flip_core(): return lax.ppermute(value, 'tm', [(i, i ^ 1) for i in range(16)])]
  transfers between devices with their start and end apart: 11 -> 11, of which waited for: 7 -> 6; matrix products, arithmetic and copies ran while one was open for 0% -> 0% of each run, Pallas kernels for 11% -> 11%
where the time goes in v10:
time: 92.1 us; the launch traced here: 91.6 us
  starting transfers between devices  41.8 us (45%)
  waiting for transfers between devices  20.9 us (23%)
  Pallas kernels  15.6 us (17%)
  blocking collectives  9.07 us (10%)
  local copies, waits for them, and re-layouts  3.05 us (3%)
    all_to_all x2, starting transfers between devices, exchange(): lax.all_to_all(value, BOTH, 0, 0, tiled=True, axis_index_groups=groups)  23.3 us
    all_to_all x2, waiting for transfers between devices, exchange(): lax.all_to_all(value, BOTH, 0, 0, tiled=True, axis_index_groups=groups)  13.7 us
    all_to_all x1, blocking collectives, exchange(): lax.all_to_all(value, BOTH, 0, 0, tiled=True, axis_index_groups=groups)  9.07 us
    ppermute x2, starting transfers between devices, shifted(): lax.ppermute(value, axis, [(source, source + steps) for source in range(l...  8.02 us
    ppermute x3, starting transfers between devices, flip_core(): return lax.ppermute(value, 'tm', [(i, i ^ 1) for i in range(16)])  5.72 us
    ppermute x4, starting transfers between devices, pairs(): return lax.ppermute(value, 'space', links + [(j, i) for i, j in links])  4.72 us
    pallas_call x1, Pallas kernels, local(): call_back(backward_kernel, 2, 1, flops // 2)  3.53 us
    ppermute x4, waiting for transfers between devices, pairs(): return lax.ppermute(value, 'space', links + [(j, i) for i, j in links])  3.23 us
  transfers between devices with their start and end apart: 11, of which 6 were waited for; matrix products, arithmetic and copies ran while one was open for 0% of the time, Pallas kernels for 11%

profile of v10, /device:TPU:1, one launch (start us, length us, event | category | flops | bytes accessed | tf_op | source)
XLA Modules:
  0.0 91.6 jit_solution(2915129606114736222)
XLA Ops:
  0.6 4.6 %collective-permute-start = (bf16[2,2,128,256]{3,2,1,0:T(8,128)(2,1)}, bf16[2,2,128,256]{3,2,1,0:T(8,128)(2,1)S(1)}, u32[]{:S(2)}, u32[]{:S(2)}) collective-permute-start(bf16[2,2,128,256]{3,2,1,0:T(8,128)(2,1)} %frames_ref.1), channel_id=1, source_target_pairs={{0,16},{16,32},{32,48},{48,64},{64,80},{80,96},{96,112},{112,128},... | collective-permute-start | bytes 786440 | tf_op jit(solution)/shard_map/ppermute | solution.py:49
  5.2 0.0 copy-start.3
  5.2 1.0 %copy-done.3 = bf16[2,2,128,256]{3,2,1,0:T(8,128)(2,1)S(1)} copy-done((bf16[2,2,128,256]{3,2,1,0:T(8,128)(2,1)S(1)}, bf16[2,2,128,256]{3,2,1,0:T(8,128)(2,1)}, u32[]{:S(2)}) %copy-start.3) | copy-done | bytes 262168
  6.2 2.6 %collective-permute-done.carried_ref = bf16[2,2,128,256]{3,2,1,0:T(8,128)(2,1)S(1)} collective-permute-done((bf16[2,2,128,256]{3,2,1,0:T(8,128)(2,1)}, bf16[2,2,128,256]{3,2,1,0:T(8,128)(2,1)S(1)}, u32[]{:S(2)}, u32[]{:S(2)}) %collective-permute-start) | collective-permute-done | bytes 262176 | tf_op jit(solution)/shard_map/ppermute | solution.py:49
  8.9 0.1 broadcast_select_fusion.4
  8.9 1.7 %collective-permute-start.1 = (bf16[4,1,128,256]{3,2,1,0:T(8,128)(2,1)S(1)}, bf16[4,1,128,256]{3,2,1,0:T(8,128)(2,1)S(1)}, u32[]{:S(2)}, u32[]{:S(2)}) collective-permute-start(bf16[4,1,128,256]{3,2,1,0:T(8,128)(2,1)S(1)} %get-tuple-element.44), channel_id=1, source_target_pairs={{0,1},{2,3},{4,5},{6,7},{8,9},{10,11},{12,13},{14,15},{1,0},{3,2},... | collective-permute-start | bytes 786440 | tf_op jit(solution)/shard_map/ppermute | solution.py:54
  10.6 0.7 collective-permute-start.2
  11.3 0.0 copy-start
  11.3 2.0 %copy-done = bf16[3,3,3,256,256]{4,3,2,1,0:T(8,128)(2,1)S(1)} copy-done((bf16[3,3,3,256,256]{4,3,2,1,0:T(8,128)(2,1)S(1)}, bf16[3,3,3,256,256]{4,3,2,1,0:T(8,128)(2,1)}, u32[]{:S(2)}) %copy-start) | copy-done | bytes 3538968
  13.3 0.0 copy-start.1
  13.3 1.5 %shard_map.68 = (f32[4,128,256]{2,1,0:T(8,128)S(1)}, bf16[3,2,3,256,256]{4,3,2,1,0:T(8,128)(2,1)S(1)}) custom-call(bf16[2,2,128,256]{3,2,1,0:T(8,128)(2,1)S(1)} %collective-permute-done.carried_ref, bf16[2,2,128,256]{3,2,1,0:T(8,128)(2,1)S(1)} %get-tuple-element.23.own_ref, bf16[3,3,3,256,256]{4,3,2,1,0:T(8,128)(2,1)S(1)} %copy-done), custom_call_target="tpu_custom_call" | custom-call | flops 1811939328 | bytes 5000000 | tf_op jit(solution)/shard_map/pallas_call | solution.py:295
  14.9 0.3 collective-permute-done.1.near_ref
  15.2 0.0 collective-permute-done.2.far_ref
  15.2 0.0 copy-done.1
  15.2 1.8 %shard_map.69 = (bf16[2,2,128,256]{3,2,1,0:T(8,128)(2,1)}, bf16[2,2,128,256]{3,2,1,0:T(8,128)(2,1)S(1)}) custom-call(bf16[4,1,128,256]{3,2,1,0:T(8,128)(2,1)S(1)} %collective-permute-done.1.near_ref, bf16[4,1,128,256]{3,2,1,0:T(8,128)(2,1)S(1)} %collective-permute-done.2.far_ref, bf16[2,2,128,256]{3,2,1,0:T(8,128)(2,1)S(1)} %get-tuple-element.23.own_ref, ...), custom_call_target="tpu_custom_call" | custom-call | flops 603979776 | bytes 5000000 | tf_op jit(solution)/shard_map/pallas_call | solution.py:304
  17.0 0.0 copy-start.2
  17.0 0.1 pad_maximum_fusion
  17.1 0.1 broadcast_select_fusion
  17.2 0.1 collective-permute-start.3
  17.3 0.5 collective-permute-start.4
  17.8 0.1 copy-done.2
  17.9 1.4 %shard_map.70.part_ref = f32[768,1152]{1,0:T(8,128)S(1)} custom-call(bf16[4,4,128,128]{3,2,1,0:T(8,128)(2,1)S(1)} %get-tuple-element.39.cells_ref, bf16[2,2,128,256]{3,2,1,0:T(8,128)(2,1)S(1)} %get-tuple-element.33.grad_ref, bf16[256,256]{1,0:T(8,128)(2,1)S(1)} %copy-done.2), custom_call_target="tpu_custom_call" | custom-call | flops 905969664 | bytes 5000000 | tf_op jit(solution)/shard_map/pallas_call | solution.py:317
  19.3 0.3 collective-permute-done.4.grad_ref
  19.6 0.0 collective-permute-done.3.cells_ref
  19.6 2.4 %shard_map.71 = bf16[256,3456]{1,0:T(8,128)(2,1)} custom-call(bf16[4,4,128,128]{3,2,1,0:T(8,128)(2,1)S(1)} %collective-permute-done.3.cells_ref, bf16[2,2,128,256]{3,2,1,0:T(8,128)(2,1)S(1)} %collective-permute-done.4.grad_ref, bf16[256,256]{1,0:T(8,128)(2,1)S(1)} %copy-done.2, f32[768,1152]{1,0:T(8,128)S(1)} %shard_map.70.part_ref), custom_call_target="tpu_custom_call" | custom-call | flops 905969664 | bytes 5000000 | tf_op jit(solution)/shard_map/pallas_call | solution.py:320
  22.0 15.5 %all-to-all-start = ((bf16[16,16,3456]{2,1,0:T(8,128)(2,1)}), bf16[16,16,3456]{2,1,0:T(8,128)(2,1)S(1)}, u32[]{:S(2)}, u32[]{:S(2)}) async-start(bf16[16,16,3456]{2,1,0:T(8,128)(2,1)} %bitcast), calls=%async_computation | async-start | bytes 3538944 | tf_op jit(solution)/shard_map/all_to_all | solution.py:39
  37.6 0.7 collective-permute-start.5
  38.3 1.7 %collective-permute-start.6 = (bf16[2,1,128,256]{3,2,1,0:T(8,128)(2,1)S(1)}, bf16[2,1,128,256]{3,2,1,0:T(8,128)(2,1)S(1)}, u32[]{:S(2)}, u32[]{:S(2)}) collective-permute-start(bf16[2,1,128,256]{3,2,1,0:T(8,128)(2,1)S(1)} %get-tuple-element.48), channel_id=1, source_target_pairs={{0,1},{2,3},{4,5},{6,7},{8,9},{10,11},{12,13},{14,15},{1,0},{3,2},... | collective-permute-start | bytes 393224 | tf_op jit(solution)/shard_map/ppermute | solution.py:54
  39.9 0.0 collective-permute-done.5
  39.9 2.9 %collective-permute-done.6 = bf16[2,1,128,256]{3,2,1,0:T(8,128)(2,1)S(1)} collective-permute-done((bf16[2,1,128,256]{3,2,1,0:T(8,128)(2,1)S(1)}, bf16[2,1,128,256]{3,2,1,0:T(8,128)(2,1)S(1)}, u32[]{:S(2)}, u32[]{:S(2)}) %collective-permute-start.6) | collective-permute-done | bytes 131104 | tf_op jit(solution)/shard_map/ppermute | solution.py:54
  42.9 0.1 pad_maximum_fusion.1.tall_ref
  43.0 2.8 %shard_map.74 = bf16[2,2,128,256]{3,2,1,0:T(8,128)(2,1)S(1)} custom-call(bf16[2,4,128,256]{3,2,1,0:T(8,128)(2,1)S(1)} %pad_maximum_fusion.1.tall_ref, bf16[3,3,3,256,256]{4,3,2,1,0:T(8,128)(2,1)} %w_from.3), custom_call_target="tpu_custom_call" | custom-call | flops 905969664 | bytes 5000000 | tf_op jit(solution)/shard_map/pallas_call | solution.py:331
  45.8 3.4 %collective-permute-start.7 = (bf16[2,2,128,256]{3,2,1,0:T(8,128)(2,1)S(1)}, bf16[2,2,128,256]{3,2,1,0:T(8,128)(2,1)S(1)}, u32[]{:S(2)}, u32[]{:S(2)}) collective-permute-start(bf16[2,2,128,256]{3,2,1,0:T(8,128)(2,1)S(1)} %shard_map.74), channel_id=1, source_target_pairs={{16,0},{32,16},{48,32},{64,48},{80,64},{96,80},{112,96},{128,112},... | collective-permute-start | bytes 786440 | tf_op jit(solution)/shard_map/ppermute | solution.py:49
  49.2 13.6 %all-to-all-done.got_ref = bf16[16,16,3456]{2,1,0:T(8,128)(2,1)S(1)} async-done(((bf16[16,16,3456]{2,1,0:T(8,128)(2,1)}), bf16[16,16,3456]{2,1,0:T(8,128)(2,1)S(1)}, u32[]{:S(2)}, u32[]{:S(2)}) %all-to-all-start) | async-done | bytes 1769504 | tf_op jit(solution)/shard_map/all_to_all | solution.py:39
  62.8 0.5 shard_map.72
  63.3 9.1 %all_to_all.19.got_ref = bf16[8,2,3456]{2,1,0:T(2,128)(2,1)S(1)} all-to-all(bf16[8,2,3456]{2,1,0:T(2,128)(2,1)S(1)} %shard_map.72), channel_id=1, replica_groups={{4,5,6,7,0,1,2,3},{12,13,14,15,8,9,10,11},{20,21,22,23,16,17,18,19},{28..., dimensions={0} | all-to-all | bytes 221184 | tf_op jit(solution)/shard_map/all_to_all | solution.py:39
  72.4 0.7 shard_map.73
  73.1 0.0 collective-permute-done.7.later_ref
  73.1 7.8 %all-to-all-start.2 = ((f32[8,2,3456]{2,1,0:T(2,128)}), f32[8,2,3456]{2,1,0:T(2,128)S(1)}, u32[]{:S(2)}, u32[]{:S(2)}) async-start(f32[8,2,3456]{2,1,0:T(2,128)} %shard_map.73), calls=%async_computation.2 | async-start | bytes 442368 | tf_op jit(solution)/shard_map/all_to_all | solution.py:39
  80.9 3.5 %shard_map.75 = bf16[2,2,128,256]{3,2,1,0:T(8,128)(2,1)} custom-call(bf16[2,4,128,256]{3,2,1,0:T(8,128)(2,1)S(1)} %pad_maximum_fusion.1.tall_ref, bf16[2,2,128,256]{3,2,1,0:T(8,128)(2,1)S(1)} %collective-permute-done.7.later_ref, bf16[3,3,3,256,256]{4,3,2,1,0:T(8,128)(2,1)} %w_from.3, bf16[2,2,128,256]{3,2,1,0:T(8,128)(2,1)S(1)} %copy-done.1), custom_call_target="tpu_custom_call" | custom-call | flops 905969664 | bytes 5000000 | tf_op jit(solution)/shard_map/pallas_call | solution.py:346
  84.5 0.0 all-to-all-done.2.mine_ref
  84.5 5.1 %collective-permute-start.8 = (f32[8,2,3456]{2,1,0:T(2,128)S(1)}, f32[8,2,3456]{2,1,0:T(2,128)S(1)}, u32[]{:S(2)}, u32[]{:S(2)}) collective-permute-start(f32[8,2,3456]{2,1,0:T(2,128)S(1)} %all-to-all-done.2.mine_ref), channel_id=1, source_target_pairs={{0,16},{16,0},{32,48},{48,32},{64,80},{80,64},{96,112},{112,96},{1... | collective-permute-start | bytes 663560 | tf_op jit(solution)/shard_map/ppermute | solution.py:43
  89.6 1.1 %collective-permute-done.8.other_ref = f32[8,2,3456]{2,1,0:T(2,128)S(1)} collective-permute-done((f32[8,2,3456]{2,1,0:T(2,128)S(1)}, f32[8,2,3456]{2,1,0:T(2,128)S(1)}, u32[]{:S(2)}, u32[]{:S(2)}) %collective-permute-start.8) | collective-permute-done | bytes 221216 | tf_op jit(solution)/shard_map/ppermute | solution.py:43
  90.7 0.9 shard_map.76
  (5 shorter events, 0.1 us)
Async XLA Ops:
  0.6 8.2 %collective-permute-start = (bf16[2,2,128,256]{3,2,1,0:T(8,128)(2,1)}, bf16[2,2,128,256]{3,2,1,0:T(8,128)(2,1)S(1)}, u32[]{:S(2)}, u32[]{:S(2)}) collective-permute-start(bf16[2,2,128,256]{3,2,1,0:T(8,128)(2,1)} %frames_ref.1), channel_id=1, source_target_pairs={{0,16},{16,32},{32,48},{48,64},{64,80},{80,96},{96,112},{112,128},... | collective-permute-start | bytes 786440 | tf_op jit(solution)/shard_map/ppermute | solution.py:49
  5.2 1.0 %copy-start.3 = (bf16[2,2,128,256]{3,2,1,0:T(8,128)(2,1)S(1)}, bf16[2,2,128,256]{3,2,1,0:T(8,128)(2,1)}, u32[]{:S(2)}) copy-start(bf16[2,2,128,256]{3,2,1,0:T(8,128)(2,1)} %frames_ref.1) | copy-start | bytes 786436
  8.9 6.3 %collective-permute-start.1 = (bf16[4,1,128,256]{3,2,1,0:T(8,128)(2,1)S(1)}, bf16[4,1,128,256]{3,2,1,0:T(8,128)(2,1)S(1)}, u32[]{:S(2)}, u32[]{:S(2)}) collective-permute-start(bf16[4,1,128,256]{3,2,1,0:T(8,128)(2,1)S(1)} %get-tuple-element.44), channel_id=1, source_target_pairs={{0,1},{2,3},{4,5},{6,7},{8,9},{10,11},{12,13},{14,15},{1,0},{3,2},... | collective-permute-start | bytes 786440 | tf_op jit(solution)/shard_map/ppermute | solution.py:54
  10.6 4.5 %collective-permute-start.2 = (bf16[4,1,128,256]{3,2,1,0:T(8,128)(2,1)S(1)}, bf16[4,1,128,256]{3,2,1,0:T(8,128)(2,1)S(1)}, u32[]{:S(2)}, u32[]{:S(2)}) collective-permute-start(bf16[4,1,128,256]{3,2,1,0:T(8,128)(2,1)S(1)} %get-tuple-element.43), channel_id=1, source_target_pairs={{1,2},{3,4},{5,6},{7,8},{9,10},{11,12},{13,14},{2,1},{4,3},{6,5},{... | collective-permute-start | bytes 786440 | tf_op jit(solution)/shard_map/ppermute | solution.py:54
  11.3 2.0 %copy-start = (bf16[3,3,3,256,256]{4,3,2,1,0:T(8,128)(2,1)S(1)}, bf16[3,3,3,256,256]{4,3,2,1,0:T(8,128)(2,1)}, u32[]{:S(2)}) copy-start(bf16[3,3,3,256,256]{4,3,2,1,0:T(8,128)(2,1)} %w_from.3) | copy-start | bytes 10616836
  13.3 1.8 %copy-start.1 = (bf16[2,2,128,256]{3,2,1,0:T(8,128)(2,1)S(1)}, bf16[2,2,128,256]{3,2,1,0:T(8,128)(2,1)}, u32[]{:S(2)}) copy-start(bf16[2,2,128,256]{3,2,1,0:T(8,128)(2,1)} %cot_ref.3) | copy-start | bytes 786436
  17.0 0.9 copy-start.2
  17.2 2.4 %collective-permute-start.3 = (bf16[4,4,128,128]{3,2,1,0:T(8,128)(2,1)S(1)}, bf16[4,4,128,128]{3,2,1,0:T(8,128)(2,1)S(1)}, u32[]{:S(2)}, u32[]{:S(2)}) collective-permute-start(bf16[4,4,128,128]{3,2,1,0:T(8,128)(2,1)S(1)} %get-tuple-element.40), channel_id=1, source_target_pairs={{0,16},{16,0},{32,48},{48,32},{64,80},{80,64},{96,112},{112,96},{1... | collective-permute-start | bytes 1572872 | tf_op jit(solution)/shard_map/ppermute | solution.py:43
  17.3 2.3 %collective-permute-start.4 = (bf16[2,2,128,256]{3,2,1,0:T(8,128)(2,1)S(1)}, bf16[2,2,128,256]{3,2,1,0:T(8,128)(2,1)S(1)}, u32[]{:S(2)}, u32[]{:S(2)}) collective-permute-start(bf16[2,2,128,256]{3,2,1,0:T(8,128)(2,1)S(1)} %get-tuple-element.33.grad_ref), channel_id=1, source_target_pairs={{0,16},{16,0},{32,48},{48,32},{64,80},{80,64},{96,112},{112,96},{1... | collective-permute-start | bytes 786440 | tf_op jit(solution)/shard_map/ppermute | solution.py:43
  22.0 40.8 %all-to-all-start = ((bf16[16,16,3456]{2,1,0:T(8,128)(2,1)}), bf16[16,16,3456]{2,1,0:T(8,128)(2,1)S(1)}, u32[]{:S(2)}, u32[]{:S(2)}) async-start(bf16[16,16,3456]{2,1,0:T(8,128)(2,1)} %bitcast), calls=%async_computation | async-start | bytes 3538944 | tf_op jit(solution)/shard_map/all_to_all | solution.py:39
  37.6 2.3 %collective-permute-start.5 = (bf16[2,1,128,256]{3,2,1,0:T(8,128)(2,1)S(1)}, bf16[2,1,128,256]{3,2,1,0:T(8,128)(2,1)S(1)}, u32[]{:S(2)}, u32[]{:S(2)}) collective-permute-start(bf16[2,1,128,256]{3,2,1,0:T(8,128)(2,1)S(1)} %get-tuple-element.47), channel_id=1, source_target_pairs={{1,2},{3,4},{5,6},{7,8},{9,10},{11,12},{13,14},{2,1},{4,3},{6,5},{... | collective-permute-start | bytes 393224 | tf_op jit(solution)/shard_map/ppermute | solution.py:54
  38.3 4.6 %collective-permute-start.6 = (bf16[2,1,128,256]{3,2,1,0:T(8,128)(2,1)S(1)}, bf16[2,1,128,256]{3,2,1,0:T(8,128)(2,1)S(1)}, u32[]{:S(2)}, u32[]{:S(2)}) collective-permute-start(bf16[2,1,128,256]{3,2,1,0:T(8,128)(2,1)S(1)} %get-tuple-element.48), channel_id=1, source_target_pairs={{0,1},{2,3},{4,5},{6,7},{8,9},{10,11},{12,13},{14,15},{1,0},{3,2},... | collective-permute-start | bytes 393224 | tf_op jit(solution)/shard_map/ppermute | solution.py:54
  45.8 27.4 %collective-permute-start.7 = (bf16[2,2,128,256]{3,2,1,0:T(8,128)(2,1)S(1)}, bf16[2,2,128,256]{3,2,1,0:T(8,128)(2,1)S(1)}, u32[]{:S(2)}, u32[]{:S(2)}) collective-permute-start(bf16[2,2,128,256]{3,2,1,0:T(8,128)(2,1)S(1)} %shard_map.74), channel_id=1, source_target_pairs={{16,0},{32,16},{48,32},{64,48},{80,64},{96,80},{112,96},{128,112},... | collective-permute-start | bytes 786440 | tf_op jit(solution)/shard_map/ppermute | solution.py:49
  73.1 11.3 %all-to-all-start.2 = ((f32[8,2,3456]{2,1,0:T(2,128)}), f32[8,2,3456]{2,1,0:T(2,128)S(1)}, u32[]{:S(2)}, u32[]{:S(2)}) async-start(f32[8,2,3456]{2,1,0:T(2,128)} %shard_map.73), calls=%async_computation.2 | async-start | bytes 442368 | tf_op jit(solution)/shard_map/all_to_all | solution.py:39
  84.5 6.2 %collective-permute-start.8 = (f32[8,2,3456]{2,1,0:T(2,128)S(1)}, f32[8,2,3456]{2,1,0:T(2,128)S(1)}, u32[]{:S(2)}, u32[]{:S(2)}) collective-permute-start(f32[8,2,3456]{2,1,0:T(2,128)S(1)} %all-to-all-done.2.mine_ref), channel_id=1, source_target_pairs={{0,16},{16,0},{32,48},{48,32},{64,80},{80,64},{96,112},{112,96},{1... | collective-permute-start | bytes 663560 | tf_op jit(solution)/shard_map/ppermute | solution.py:43
